TPU v7x, 512 devices: a whole 4x4x16 slice. The times are simulated.
512 devices in a mesh: dom: 32 (over z, y_lo), sp: 16 (over x, y_hi, core).
Axes of the slice: x: 4, y: 4 (y_hi: 2, y_lo: 2; y = y_hi * 2 + y_lo), z: 16, core: 2. Of those that a mesh axis runs over, the one named last changes fastest.
Arguments:
- descriptors: bfloat16 [4096, 2048], P('dom', 'sp'), may hold values from -6 to 6
- sparse_points: bfloat16 [32768, 2048], P('sp', 'dom'), may hold values from -6 to 6
- coefficients: float32 [32768], P('sp'), may hold values from -0.0078125 to 0.0078125
- derivatives: bfloat16 [4096, 3, 12, 2048], P('dom', None, None, 'sp'), may hold values from -4 to 4
- neighbours: int32 [4096, 12], P('dom'), may hold values from 0 to 383
- counts: int32 [4096], P('dom'), may hold values from 3 to 12, as said below
- ghost_index: int32 [8192], P('dom'), may hold values from 0 to 127
Outputs:
- forces: float32 [3, 4096], P(None, 'dom')
- energies: float32 [4096], P('dom')
Inputs may be any that keep to these rules, and one draw needn't show every extreme that they name: `counts`: each atom has between 3 and 12 live neighbour slots; the first atom of every domain has all 12.
All inputs are finite; a program needn't handle non-finite values.
Results may differ from a plain program's by a relative error of at most 0.0056.
Values may be sent and summed in bfloat16 or wider, within the bound.
No kernel may reach another device: no remote copies, remote signals or barrier semaphores. Data moves between devices by JAX's collectives and lax.ppermute only.
A program may use at most 64 MiB of HBM per device.

v0:
```python
import jax
import jax.numpy as jnp
from jax import lax
from jax.sharding import PartitionSpec as P


def extended_2(array, sides, width):
    for axis, dim in sides:
        size, length = (lax.axis_size(axis), array.shape[dim])
        up = [(i, (i + 1) % size) for i in range(size)]
        down = [(j, i) for i, j in up]
        last = lax.slice_in_dim(array, length - width, length, axis=dim)
        first = lax.slice_in_dim(array, 0, width, axis=dim)
        before = lax.ppermute(last, axis, up)
        after = lax.ppermute(first, axis, down)
        array = jnp.concatenate([before, array, after], axis=dim)
    return array


def body(descriptors, sparse_points, coefficients, derivatives, neighbours, counts, ghost_index):
    gathered = lax.all_gather(descriptors, "sp", axis=1, tiled=True)
    owned = gathered.shape[0]
    values = gathered.astype(jnp.float32)
    row_norm = jnp.sqrt(jnp.sum(values * values, axis=1, keepdims=True) + 1e-06)
    unit_rows = (values / row_norm).astype(jnp.bfloat16)
    contract_last = (((1,), (1,)), ((), ()))
    full_basis = lax.all_gather(sparse_points, "dom", axis=1, tiled=True)
    kernel = lax.dot_general(
        unit_rows, full_basis, contract_last, preferred_element_type=jnp.float32
    )
    energy_part = jnp.sum(coefficients[None, :] * kernel**4, axis=1)
    slopes = (4.0 * coefficients[None, :] * kernel**3).astype(jnp.bfloat16)
    gradient = jnp.dot(slopes, full_basis, preferred_element_type=jnp.float32)
    width = derivatives.shape[-1]
    offset = lax.axis_index("sp") * width
    unit_share = lax.dynamic_slice_in_dim(unit_rows, offset, width, 1).astype(jnp.float32)
    gradient = lax.psum(gradient, "sp")
    inner = jnp.sum(unit_rows.astype(jnp.float32) * gradient, axis=1, keepdims=True)
    gradient_share = lax.dynamic_slice_in_dim(gradient, offset, width, 1)
    descent = ((gradient_share - unit_share * inner) / row_norm).astype(jnp.bfloat16)
    partial_value = jnp.einsum(
        "ad,acnd->acn", descent, derivatives, preferred_element_type=jnp.float32
    )
    partial_value, energies = lax.psum((partial_value, energy_part), "sp")
    slots_count = neighbours.shape[1]
    live = jnp.arange(slots_count, dtype=jnp.int32)[None, :] < counts[:, None]
    partial_value = jnp.where(live[:, None, :], partial_value, jnp.float32(0.0))
    ghosts_side = ghost_index.shape[0] // 2
    slot_total = owned + 2 * ghosts_side
    onehot = (
        neighbours[:, :, None] == jnp.arange(slot_total, dtype=jnp.int32)[None, None, :]
    ).astype(jnp.float32)
    extended = -jnp.einsum("acn,ans->cs", partial_value, onehot, precision=lax.Precision.HIGHEST)
    own_forces = extended[:, :owned] + jnp.transpose(jnp.sum(partial_value, axis=2))
    atom_ids = jnp.arange(owned, dtype=jnp.int32)[None, :]
    left_table = (ghost_index[:ghosts_side, None] == atom_ids).astype(jnp.float32)
    right_table = (ghost_index[ghosts_side:, None] == atom_ids).astype(jnp.float32)
    to_left = jnp.dot(
        extended[:, owned : owned + ghosts_side], left_table, precision=lax.Precision.HIGHEST
    )
    to_right = jnp.dot(
        extended[:, owned + ghosts_side :], right_table, precision=lax.Precision.HIGHEST
    )
    outgoing = jnp.concatenate([to_left, to_right], axis=1)
    received = extended_2(outgoing, (("dom", 1),), owned)
    forces = own_forces + received[:, :owned] + received[:, 3 * owned :]
    return (forces, energies)


def solution(mesh):
    return jax.shard_map(
        body,
        mesh=mesh,
        in_specs=(
            P("dom", "sp"),
            P("sp", "dom"),
            P("sp"),
            P("dom", None, None, "sp"),
            P("dom", None),
            P("dom"),
            P("dom"),
        ),
        out_specs=(P(None, "dom"), P("dom")),
        check_vma=False,
    )
```

profile of v0, /device:TPU:1, one launch (start us, length us, event | category | flops | bytes accessed | tf_op | source)
XLA Modules:
  0.0 463.2 jit_solution(318694237568825469)
XLA Ops:
  7.2 0.0 copy-start
  7.2 0.0 all-gather.2.cloned.1.call-start
  7.2 0.7 all-gather.2.cloned.1.call-update
  7.9 0.0 all-reduce.3.cloned.1.call-start
  8.0 27.5 %all_gather.6 = bf16[128,2048]{1,0:T(8,128)(2,1)S(1)} all-gather(bf16[128,128]{1,0:T(8,128)(2,1)} %param.7), channel_id=1, replica_groups=mesh['dom'=32,'sp'=16] {'sp'}, dimensions={1}, use_global_device_ids=true | all-gather | bytes 557056 | tf_op jit(solution)/shard_map/all_gather | solution.py:21
  35.5 0.2 fusion.6
  35.7 0.7 broadcast_multiply_fusion
  36.4 0.2 fusion.7
  36.5 173.8 %all-gather.2.cloned.1.call-done = bf16[2048,2048]{0,1:T(8,128)(2,1)} async-done(((bf16[2048,64]{0,1:T(8,128)(2,1)}), bf16[2048,2048]{0,1:T(8,128)(2,1)}) %all-gather.2.cloned.1.call-update) | async-done | bytes 8388624 | tf_op jit(solution)/shard_map/all_gather | solution.py:27
  210.3 0.0 copy-start.1
  210.3 4.9 %fusion.11 = (f32[128]{0:T(128)S(1)}, f32[128,2048]{1,0:T(8,128)S(1)}) fusion(f32[2048]{0:T(1024)} %param.9, bf16[128,2048]{1,0:T(8,128)(2,1)S(1)} %fusion.7, bf16[2048,2048]{0,1:T(8,128)(2,1)} %all-gather.2.cloned.1.call-done), kind=kOutput, calls=%fused_computation.16 | convolution fusion | flops 1074790272 | bytes 9970176 | tf_op jit(solution)/shard_map/dot_general | solution.py:28
  215.3 0.0 copy-start.2
  215.3 0.0 copy-start.3
  215.3 0.0 copy-start.4
  215.3 0.8 copy-done.1
  216.1 3.9 fusion.12
  220.0 0.0 all-reduce.3.cloned.1.call-update
  220.1 0.0 copy-done.2
  220.1 0.0 copy-done.3
  220.1 155.7 %all-reduce.3.cloned.1.call-done = f32[128,2048]{1,0:T(8,128)} async-done(((f32[128,2048]{1,0:T(8,128)}), f32[128,2048]{1,0:T(8,128)}) %all-reduce.3.cloned.1.call-update) | async-done | bytes 1048592 | tf_op jit(solution)/shard_map/psum | solution.py:37
  375.8 1.5 multiply_reduce_fusion
  377.4 0.9 fusion.20
  378.3 0.0 copy-done
  378.3 2.8 fusion.1
  381.1 0.1 copy.11
  381.3 64.9 %all-reduce = (f32[128,3,12]{0,1,2:T(4,128)S(1)}, f32[128]{0:T(128)}) all-reduce(f32[128,3,12]{0,1,2:T(4,128)S(1)} %bitcast.12, f32[128]{0:T(128)S(1)} %get-tuple-element.6), channel_id=1, replica_groups=mesh['dom'=32,'sp'=16] {'sp'}, use_global_device_ids=true, to_apply=%region_3.0 | all-reduce | flops 4736 | bytes 37888 | tf_op jit(solution)/shard_map/psum | solution.py:44
  446.1 0.0 copy-done.4
  446.1 0.9 fusion.5
  447.0 0.2 fusion.16
  447.3 2.1 collective-permute-start
  449.4 0.2 fusion.17
  449.6 5.4 %collective-permute-start.1 = (f32[3,128]{1,0:T(4,128)S(1)}, f32[3,128]{1,0:T(4,128)S(1)}, u32[]{:S(2)}, u32[]{:S(2)}) collective-permute-start(f32[3,128]{1,0:T(4,128)S(1)} %fusion.17), channel_id=1, source_target_pairs={{16,0},{32,16},{48,32},{64,48},{80,64},{96,80},{112,96},{128,112},... | collective-permute-start | bytes 4616 | tf_op jit(solution)/shard_map/ppermute | solution.py:15
  455.1 0.0 collective-permute-done
  455.1 0.7 collective-permute-done.1
  455.7 0.6 fusion.27
  (4 shorter events, 0.0 us)
Async XLA Ops:
  7.2 371.1 %copy-start = (bf16[128,3,12,128]{3,0,2,1:T(8,128)(2,1)S(1)}, bf16[128,3,12,128]{3,0,2,1:T(8,128)(2,1)}, u32[]{:S(2)}) copy-start(bf16[128,3,12,128]{3,0,2,1:T(8,128)(2,1)} %param.10) | copy-start | bytes 3538948
  7.2 203.2 %all-gather.2.cloned.1.call-start = ((), (), s32[]{:S(2)}) async-start(), calls=%async_computation | async-start | bytes 8650752 | tf_op jit(solution)/shard_map/all_gather | solution.py:27
  7.9 367.9 %all-reduce.3.cloned.1.call-start = ((), (), s32[]{:S(2)}) async-start(), calls=%async_computation.1 | async-start | bytes 2097152 | tf_op jit(solution)/shard_map/psum | solution.py:37
  210.3 5.8 %copy-start.1 = (bf16[2048,2048]{0,1:T(8,128)(2,1)S(1)}, bf16[2048,2048]{0,1:T(8,128)(2,1)}, u32[]{:S(2)}) copy-start(bf16[2048,2048]{0,1:T(8,128)(2,1)} %all-gather.2.cloned.1.call-done) | copy-start | bytes 25165828
  215.3 4.8 %copy-start.2 = (s32[256]{0:T(256)S(1)}, s32[256]{0:T(256)}, u32[]{:S(2)}) copy-start(s32[256]{0:T(256)} %param.13) | copy-start | bytes 3076
  215.3 4.8 %copy-start.3 = (s32[128]{0:T(128)S(1)}, s32[128]{0:T(128)}, u32[]{:S(2)}) copy-start(s32[128]{0:T(128)} %param.12) | copy-start | bytes 1540
  215.3 230.8 %copy-start.4 = (s32[128,12]{0,1:T(8,128)S(1)}, s32[128,12]{0,1:T(8,128)}, u32[]{:S(2)}) copy-start(s32[128,12]{0,1:T(8,128)} %param.11) | copy-start | bytes 18436
  447.3 7.8 %collective-permute-start = (f32[3,128]{1,0:T(4,128)S(1)}, f32[3,128]{1,0:T(4,128)S(1)}, u32[]{:S(2)}, u32[]{:S(2)}) collective-permute-start(f32[3,128]{1,0:T(4,128)S(1)} %fusion.16), channel_id=1, source_target_pairs={{0,16},{16,32},{32,48},{48,64},{64,80},{80,96},{96,112},{112,128},... | collective-permute-start | bytes 4616 | tf_op jit(solution)/shard_map/ppermute | solution.py:14
  449.6 6.1 %collective-permute-start.1 = (f32[3,128]{1,0:T(4,128)S(1)}, f32[3,128]{1,0:T(4,128)S(1)}, u32[]{:S(2)}, u32[]{:S(2)}) collective-permute-start(f32[3,128]{1,0:T(4,128)S(1)} %fusion.17), channel_id=1, source_target_pairs={{16,0},{32,16},{48,32},{64,48},{80,64},{96,80},{112,96},{128,112},... | collective-permute-start | bytes 4616 | tf_op jit(solution)/shard_map/ppermute | solution.py:15
Sparse Core Ops, SparseCore 0:
  10.1 200.1 all-gather.1
  220.2 155.6 all-reduce.2
where the time goes:
time: 471 us; the launch traced here: 463 us
  waiting for transfers between devices  331 us (70%)
  blocking collectives  92.4 us (20%)
  between operations  14.2 us (3%)
  matrix products  13 us (3%)
  starting transfers between devices  7.63 us (2%)
    all_gather x1, waiting for transfers between devices, body(): full_basis = lax.all_gather(sparse_points, 'dom', axis=1, tiled=True)  174 us
    psum x1, waiting for transfers between devices, body(): gradient = lax.psum(gradient, 'sp')  156 us
    psum x1, blocking collectives, body(): partial_value, energies = lax.psum((partial_value, energy_part), 'sp')  64.9 us
    all_gather x1, blocking collectives, body(): gathered = lax.all_gather(descriptors, 'sp', axis=1, tiled=True)  27.5 us
  transfers between devices with their start and end apart: 4, of which 3 were waited for; matrix products, arithmetic and copies ran while one was open for 0% of the time, Pallas kernels for 0%

commit v1 on v0

v1 whole, which is shorter than its diff:
```python
import jax
import jax.numpy as jnp
from jax import lax
from jax.sharding import Mesh, PartitionSpec as P

DOM = ("z", "yl")
SP = ("x", "yh", "c")
PLANE = ("yl", "x", "yh", "c")


def pieces(value):
    high = lax.reduce_precision(value, 8, 7)
    rest = value - high
    mid = lax.reduce_precision(rest, 8, 7)
    return [p.astype(jnp.bfloat16) for p in (high, mid, rest - mid)]


def body(descriptors, sparse_points, coefficients, derivatives, neighbours, counts, ghost_index):
    f32, bf16 = jnp.float32, jnp.bfloat16
    yl = lax.axis_index("yl")
    owned, width = descriptors.shape
    points, part = sparse_points.shape
    n_sp, n_plane = lax.axis_size(SP), lax.axis_size(PLANE)
    half = points // 2
    slots_count = neighbours.shape[1]
    ghosts = ghost_index.shape[0] // 2

    with jax.named_scope("points_swap"):
        split = jnp.transpose(sparse_points.T.reshape(part, 2, half), (1, 0, 2))
        swapped = lax.all_to_all(split, "yl", 0, 0).reshape(2 * part, half)
    with jax.named_scope("points_gather"):
        basis = lax.all_gather(swapped, "z", axis=0, tiled=True)

    with jax.named_scope("descriptors_gather"):
        spread = jnp.broadcast_to(descriptors[None], (n_plane, owned, width))
        blocks = lax.all_to_all(spread, PLANE, 0, 0).reshape(2, n_sp, owned, width)
        rows = jnp.transpose(blocks, (0, 2, 1, 3)).reshape(2 * owned, n_sp * width)
    values = rows.astype(f32)
    row_norm = jnp.sqrt(jnp.sum(values * values, axis=1, keepdims=True) + 1e-06)
    unit_rows = (values / row_norm).astype(bf16)
    own_norm = lax.dynamic_slice_in_dim(row_norm, yl * owned, owned, 0)
    own_unit = (descriptors.astype(f32) / own_norm).astype(bf16).astype(f32)

    with jax.named_scope("scatter_table"):
        slot_total = owned + 2 * ghosts
        flat = neighbours.reshape(owned * slots_count)
        slot_ids = jnp.arange(slot_total, dtype=jnp.int32)
        hot = (flat[:, None] == slot_ids[None, :]).astype(bf16)
        target = jnp.concatenate(
            [
                jnp.arange(owned, dtype=jnp.int32),
                ghost_index[:ghosts] + owned,
                ghost_index[ghosts:] + 2 * owned,
            ]
        )
        column_ids = jnp.arange(3 * owned, dtype=jnp.int32)
        moves = (target[:, None] == column_ids[None, :]).astype(bf16)
        landed = jnp.dot(hot, moves, preferred_element_type=f32)
        atom_of = jnp.arange(owned * slots_count, dtype=jnp.int32) // slots_count
        slot_of = jnp.arange(owned * slots_count, dtype=jnp.int32) % slots_count
        self_hot = (atom_of[:, None] == column_ids[None, :]).astype(f32)
        live = slot_of < jnp.repeat(counts, slots_count)
        table = jnp.where(live[:, None], self_hot - landed, 0.0).astype(bf16)

    with jax.named_scope("kernel"):
        kernel = jnp.dot(unit_rows, basis, preferred_element_type=f32)
        mine = lax.dynamic_slice_in_dim(coefficients, yl * half, half, 0)[None, :]
        cube = mine * kernel**3
        energy_part = jnp.sum(cube * kernel, axis=1)
        slopes = (4.0 * cube).astype(bf16)
        inner_part = jnp.sum(slopes.astype(f32) * kernel, axis=1)
    with jax.named_scope("gradient"):
        gradient = lax.dot_general(
            slopes, basis, (((1,), (1,)), ((), ())), preferred_element_type=f32
        ).astype(bf16)
        shares = jnp.transpose(gradient.reshape(2, owned, n_sp, width), (0, 2, 1, 3))
        extra = jnp.stack(pieces(energy_part) + pieces(inner_part)).reshape(6, 2, owned)
        extra = jnp.pad(jnp.transpose(extra, (1, 0, 2)), ((0, 0), (0, 10), (0, 0)))
        extra = jnp.broadcast_to(extra[:, None], (2, n_sp, 16, owned))
        outgoing = jnp.concatenate([shares, extra], axis=2).reshape(n_plane, owned + 16, width)
    with jax.named_scope("gradient_exchange"):
        total = jnp.sum(lax.all_to_all(outgoing, PLANE, 0, 0).astype(f32), axis=0)
    share = total[:owned]
    energies = total[owned] + total[owned + 1] + total[owned + 2]
    inner = (total[owned + 3] + total[owned + 4] + total[owned + 5])[:, None]
    descent = ((share - own_unit * inner) / own_norm).astype(bf16)
    with jax.named_scope("contract"):
        partial = jnp.einsum("ad,acnd->can", descent, derivatives, preferred_element_type=f32)
    with jax.named_scope("scatter"):
        partial = partial.reshape(3, owned * slots_count)
        moved = jnp.dot(jnp.concatenate(pieces(partial)), table, preferred_element_type=f32)
        moved = moved[0:3] + moved[3:6] + moved[6:9]
        own, to_left, to_right = jnp.split(moved, 3, axis=1)
    with jax.named_scope("ghosts"):
        first = yl == 0
        across = jnp.where(first, to_left, to_right)
        beside = jnp.where(first, to_right, to_left)
        size = lax.axis_size(DOM)
        pairs = [(i, (i - 1) % size if i % 2 == 0 else (i + 1) % size) for i in range(size)]
        own = own + lax.ppermute(across, DOM, pairs)
        both = jnp.stack([jnp.where(first, own, beside), jnp.where(first, beside, own)])
        both = jnp.broadcast_to(both[:, None], (2, n_sp, 3, owned)).reshape(n_plane, 3, owned)
        forces = jnp.sum(lax.all_to_all(both, PLANE, 0, 0), axis=0)
    return (forces, energies)


def solution(mesh):
    grid = Mesh(mesh.devices.reshape(16, 2, 4, 2, 2), ("z", "yl", "x", "yh", "c"))
    return jax.shard_map(
        body,
        mesh=grid,
        in_specs=(
            P(DOM, SP),
            P(SP, DOM),
            P(SP),
            P(DOM, None, None, SP),
            P(DOM, None),
            P(DOM),
            P(DOM),
        ),
        out_specs=(P(None, DOM), P(DOM)),
        check_vma=False,
    )
```

time: 471 us -> 167 us (0.35); the launches traced: 463 us -> 167 us
  waiting for transfers between devices: 331 us -> 80.6 us
  blocking collectives: 92.4 us -> 20 us
  starting transfers between devices: 7.63 us -> 31.1 us
  local copies, waits for them, and re-layouts: 0.95 us -> 7.03 us
    psum x1 -> x0, waiting for transfers between devices: 156 us -> none  [body(): gradient = lax.psum(gradient, 'sp')]
    all_gather x1, waiting for transfers between devices: 174 us -> 43 us  [body(): basis = lax.all_gather(swapped, 'z', axis=0, tiled=True)]
    psum x1 -> x0, blocking collectives: 64.9 us -> none  [body(): partial_value, energies = lax.psum((partial_value, energy_part), 'sp')]
    all_to_all x0 -> x2, waiting for transfers between devices: none -> 35.2 us  [the longest x1 18 us: body(): total = jnp.sum(lax.all_to_all(outgoing, PLANE, 0, 0).astype(f32), axis=0)]
    all_gather x1 -> x0, blocking collectives: 27.5 us -> none  [body(): gathered = lax.all_gather(descriptors, 'sp', axis=1, tiled=True)]
    all_to_all x0 -> x2, starting transfers between devices: none -> 27 us  [the longest x1 16 us: body(): total = jnp.sum(lax.all_to_all(outgoing, PLANE, 0, 0).astype(f32), axis=0)]
    all_to_all x0 -> x2, blocking collectives: none -> 20 us  [the longest x1 12.2 us: body(): forces = jnp.sum(lax.all_to_all(both, PLANE, 0, 0), axis=0)]
    dot_general x6 -> x4, matrix products: 13 us -> 10.3 us  [the longest x1 4.81 us: body(): kernel = jnp.dot(unit_rows, basis, preferred_element_type=f32)]
  transfers between devices with their start and end apart: 4 -> 4, of which waited for: 3 -> 4; matrix products, arithmetic and copies ran while one was open for 0% -> 4% of each run, Pallas kernels for 0% -> 0%
where the time goes in v1:
time: 167 us
  waiting for transfers between devices  80.6 us (48%)
  starting transfers between devices  31.1 us (19%)
  blocking collectives  20 us (12%)
  between operations  14.3 us (9%)
  matrix products  10.3 us (6%)
  local copies, waits for them, and re-layouts  7.03 us (4%)
  other arithmetic  3.49 us (2%)
    all_gather x1, waiting for transfers between devices, body(): basis = lax.all_gather(swapped, 'z', axis=0, tiled=True)  43 us
    all_to_all x1, waiting for transfers between devices, body(): total = jnp.sum(lax.all_to_all(outgoing, PLANE, 0, 0).astype(f32), axis=0)  18 us
    all_to_all x1, waiting for transfers between devices, body(): blocks = lax.all_to_all(spread, PLANE, 0, 0).reshape(2, n_sp, owned, width)  17.2 us
    all_to_all x1, starting transfers between devices, body(): total = jnp.sum(lax.all_to_all(outgoing, PLANE, 0, 0).astype(f32), axis=0)  16 us
    all_to_all x1, blocking collectives, body(): forces = jnp.sum(lax.all_to_all(both, PLANE, 0, 0), axis=0)  12.2 us
    all_to_all x1, starting transfers between devices, body(): blocks = lax.all_to_all(spread, PLANE, 0, 0).reshape(2, n_sp, owned, width)  10.9 us
    all_to_all x1, blocking collectives, body(): swapped = lax.all_to_all(split, 'yl', 0, 0).reshape(2 * part, half)  7.77 us
    dot_general x1, matrix products, body(): kernel = jnp.dot(unit_rows, basis, preferred_element_type=f32)  4.81 us
  transfers between devices with their start and end apart: 4, of which 4 were waited for; matrix products, arithmetic and copies ran while one was open for 4% of the time, Pallas kernels for 0%

profile of v1, /device:TPU:1, one launch (start us, length us, event | category | flops | bytes accessed | tf_op | source)
XLA Modules:
  0.0 166.8 jit_solution(472005079832102221)
XLA Ops:
  7.2 0.0 copy-start
  7.2 0.0 all-gather.2.cloned.1.call-start
  7.2 1.2 reshape.211
  8.5 0.0 copy-start.3
  8.5 7.8 %all_to_all.20 = bf16[2,64,1024]{2,1,0:T(8,128)(2,1)} all-to-all(bf16[2,64,1024]{2,1,0:T(8,128)(2,1)S(1)} %copy.25), channel_id=1, replica_groups=mesh['z'=16,'yl'=2,'x'=4,'yh'=2,'c'=2] {'yl'}, dimensions={0} | all-to-all | bytes 524288 | tf_op jit(solution)/shard_map/points_swap/all_to_all | solution.py:30
  16.3 0.0 all-gather.2.cloned.1.call-update
  16.3 2.0 %broadcast_in_dim.20 = bf16[32,128,128]{2,1,0:T(8,128)(2,1)} broadcast(bf16[128,128]{1,0:T(8,128)(2,1)} %param.7), dimensions={1,2} | broadcast | bytes 1081344 | tf_op jit(solution)/shard_map/descriptors_gather/broadcast_in_dim | solution.py:35
  18.3 10.9 %all-to-all-start = ((bf16[32,128,128]{2,1,0:T(8,128)(2,1)}), bf16[32,128,128]{2,1,0:T(8,128)(2,1)S(1)}, u32[]{:S(2)}, u32[]{:S(2)}) async-start(bf16[32,128,128]{2,1,0:T(8,128)(2,1)} %broadcast_in_dim.20), calls=%async_computation | async-start | bytes 2097152 | tf_op jit(solution)/shard_map/descriptors_gather/all_to_all | solution.py:36
  29.3 0.0 copy-done.3
  29.3 17.2 %all-to-all-done = bf16[32,128,128]{2,1,0:T(8,128)(2,1)S(1)} async-done(((bf16[32,128,128]{2,1,0:T(8,128)(2,1)}), bf16[32,128,128]{2,1,0:T(8,128)(2,1)S(1)}, u32[]{:S(2)}, u32[]{:S(2)}) %all-to-all-start) | async-done | bytes 1048608 | tf_op jit(solution)/shard_map/descriptors_gather/all_to_all | solution.py:36
  46.5 0.2 convert_element_type.156
  46.7 2.5 %copy.24 = f32[2,128,16,128]{3,2,1,0:T(8,128)} copy(f32[2,128,16,128]{3,1,2,0:T(8,128)S(1)} %bitcast.51) | data formatting | bytes 4194304 | tf_op jit(solution)/shard_map/convert_element_type | solution.py:38
  49.3 0.6 multiply_reduce_fusion
  49.9 43.0 %all-gather.2.cloned.1.call-done = bf16[2048,1024]{1,0:T(8,128)(2,1)} async-done(((bf16[128,1024]{1,0:T(8,128)(2,1)}), bf16[2048,1024]{1,0:T(8,128)(2,1)}) %all-gather.2.cloned.1.call-update) | async-done | bytes 4194320 | tf_op jit(solution)/shard_map/points_gather/all_gather | solution.py:32
  93.0 0.0 copy-start.6
  93.0 4.8 %multiply_reduce_fusion.1 = (f32[256]{0:T(256)S(1)}, f32[256]{0:T(256)S(1)}, f32[256,1024]{1,0:T(8,128)S(1)}) fusion(f32[1024]{0:T(1024)S(1)} %dynamic_slice.6, bf16[2048,1024]{1,0:T(8,128)(2,1)} %all-gather.2.cloned.1.call-done, f32[32,8,16,128]{3,2,1,0:T(8,128)} %bitcast.54, f32[256]{0:T(256)S(1)} %get-tuple-element.12), kind=kOutput, calls=%fused_computation.27 | convolution fusion | flops 1077411328 | bytes 7347200 | tf_op jit(solution)/shard_map/kernel/dot_general | solution.py:66
  97.8 0.0 copy-done.6
  97.8 1.3 fusion.5
  99.1 0.2 copy.34
  99.3 0.3 copy.45
  99.7 0.0 copy-start.5
  99.7 0.0 copy-start.2
  99.7 0.0 copy-start.4
  99.7 1.1 pad_maximum_fusion
  100.9 0.0 copy-start.1
  100.9 16.0 %all-to-all-start.2 = ((bf16[32,144,128]{2,1,0:T(8,128)(2,1)}), bf16[32,144,128]{2,1,0:T(8,128)(2,1)S(1)}, u32[]{:S(2)}, u32[]{:S(2)}) async-start(bf16[32,144,128]{2,1,0:T(8,128)(2,1)} %bitcast.11), calls=%async_computation.2 | async-start | bytes 2359296 | tf_op jit(solution)/shard_map/gradient_exchange/all_to_all | solution.py:82
  116.9 0.0 copy-done.5
  116.9 0.1 broadcast_in_dim.22
  117.0 0.1 reshape.216
  117.1 0.0 copy-done.2
  117.1 0.1 copy.27
  117.2 0.1 eq.50
  117.3 0.0 copy-done.4
  117.4 18.0 %all-to-all-done.2 = bf16[32,144,128]{2,1,0:T(8,128)(2,1)S(1)} async-done(((bf16[32,144,128]{2,1,0:T(8,128)(2,1)}), bf16[32,144,128]{2,1,0:T(8,128)(2,1)S(1)}, u32[]{:S(2)}, u32[]{:S(2)}) %all-to-all-start.2) | async-done | bytes 1179680 | tf_op jit(solution)/shard_map/gradient_exchange/all_to_all | solution.py:82
  135.4 0.2 convert_reduce_fusion
  135.6 0.5 fusion.42
  136.1 0.0 copy-done.1
  136.1 0.1 fusion.32
  136.2 0.0 copy-done
  136.3 2.8 %fusion.3 = f32[128,1,3,12]{3,1,2,0:T(1,128)S(1)} fusion(bf16[128,3,12,128]{3,0,2,1:T(8,128)(2,1)S(1)} %copy-done, bf16[128,128,1,1]{1,0,2,3:T(8,128)(2,1)S(1)} %fusion.32), kind=kOutput, calls=%fused_computation.10 | convolution fusion | flops 1179648 | bytes 1230848 | tf_op jit(solution)/shard_map/contract/ad,acnd->can/dot_general | solution.py:88
  139.1 0.2 reshape.215
  139.3 1.3 fusion.6
  140.7 4.1 %collective-permute-start = (f32[3,128]{1,0:T(4,128)S(1)}, f32[3,128]{1,0:T(4,128)S(1)}, u32[]{:S(2)}, u32[]{:S(2)}) collective-permute-start(f32[3,128]{1,0:T(4,128)S(1)} %slice_select_fusion.1), channel_id=1, source_target_pairs={{0,496},{16,32},{32,16},{48,64},{64,48},{80,96},{96,80},{112,128},... | collective-permute-start | bytes 4616 | tf_op jit(solution)/shard_map/ghosts/ppermute | solution.py:100
  144.8 2.3 %collective-permute-done = f32[3,128]{1,0:T(4,128)S(1)} collective-permute-done((f32[3,128]{1,0:T(4,128)S(1)}, f32[3,128]{1,0:T(4,128)S(1)}, u32[]{:S(2)}, u32[]{:S(2)}) %collective-permute-start) | collective-permute-done | bytes 1568 | tf_op jit(solution)/shard_map/ghosts/ppermute | solution.py:100
  147.1 12.2 %all_to_all.21 = f32[32,3,128]{2,1,0:T(4,128)S(1)} all-to-all(f32[32,3,128]{2,1,0:T(4,128)S(1)} %bitcast.59), channel_id=1, replica_groups=mesh['z'=16,'yl'=2,'x'=4,'yh'=2,'c'=2] {'yl','x','yh','c'}, dimensions={0} | all-to-all | bytes 98304 | tf_op jit(solution)/shard_map/ghosts/all_to_all | solution.py:103
  159.3 0.6 reduce_sum.64
  (21 shorter events, 0.3 us)
Async XLA Ops:
  7.2 129.1 %copy-start = (bf16[128,3,12,128]{3,0,2,1:T(8,128)(2,1)S(1)}, bf16[128,3,12,128]{3,0,2,1:T(8,128)(2,1)}, u32[]{:S(2)}) copy-start(bf16[128,3,12,128]{3,0,2,1:T(8,128)(2,1)} %param.10) | copy-start | bytes 3538948
  7.2 85.8 %all-gather.2.cloned.1.call-start = ((), (), s32[]{:S(2)}) async-start(), calls=%async_computation.4 | async-start | bytes 4456448 | tf_op jit(solution)/shard_map/points_gather/all_gather | solution.py:32
  8.5 20.7 %copy-start.3 = (f32[2048]{0:T(1024)S(1)}, f32[2048]{0:T(1024)}, u32[]{:S(2)}) copy-start(f32[2048]{0:T(1024)} %param.9) | copy-start | bytes 24580
  18.3 28.2 %all-to-all-start = ((bf16[32,128,128]{2,1,0:T(8,128)(2,1)}), bf16[32,128,128]{2,1,0:T(8,128)(2,1)S(1)}, u32[]{:S(2)}, u32[]{:S(2)}) async-start(bf16[32,128,128]{2,1,0:T(8,128)(2,1)} %broadcast_in_dim.20), calls=%async_computation | async-start | bytes 2097152 | tf_op jit(solution)/shard_map/descriptors_gather/all_to_all | solution.py:36
  93.0 4.8 %copy-start.6 = (bf16[2048,1024]{1,0:T(8,128)(2,1)S(1)}, bf16[2048,1024]{1,0:T(8,128)(2,1)}, u32[]{:S(2)}) copy-start(bf16[2048,1024]{1,0:T(8,128)(2,1)} %all-gather.2.cloned.1.call-done) | copy-start | bytes 12582916
  99.7 17.2 %copy-start.5 = (s32[128]{0:T(128)S(1)}, s32[128]{0:T(128)}, u32[]{:S(2)}) copy-start(s32[128]{0:T(128)} %param.12) | copy-start | bytes 1540
  99.7 17.4 %copy-start.2 = (s32[128,12]{0,1:T(8,128)S(1)}, s32[128,12]{0,1:T(8,128)}, u32[]{:S(2)}) copy-start(s32[128,12]{0,1:T(8,128)} %param.11) | copy-start | bytes 18436
  99.7 17.6 %copy-start.4 = (s32[256]{0:T(256)S(1)}, s32[256]{0:T(256)}, u32[]{:S(2)}) copy-start(s32[256]{0:T(256)} %param.13) | copy-start | bytes 3076
  100.9 35.3 %copy-start.1 = (bf16[128,128]{1,0:T(8,128)(2,1)S(1)}, bf16[128,128]{1,0:T(8,128)(2,1)}, u32[]{:S(2)}) copy-start(bf16[128,128]{1,0:T(8,128)(2,1)} %param.7) | copy-start | bytes 98308
  100.9 34.6 %all-to-all-start.2 = ((bf16[32,144,128]{2,1,0:T(8,128)(2,1)}), bf16[32,144,128]{2,1,0:T(8,128)(2,1)S(1)}, u32[]{:S(2)}, u32[]{:S(2)}) async-start(bf16[32,144,128]{2,1,0:T(8,128)(2,1)} %bitcast.11), calls=%async_computation.2 | async-start | bytes 2359296 | tf_op jit(solution)/shard_map/gradient_exchange/all_to_all | solution.py:82
  140.7 6.4 %collective-permute-start = (f32[3,128]{1,0:T(4,128)S(1)}, f32[3,128]{1,0:T(4,128)S(1)}, u32[]{:S(2)}, u32[]{:S(2)}) collective-permute-start(f32[3,128]{1,0:T(4,128)S(1)} %slice_select_fusion.1), channel_id=1, source_target_pairs={{0,496},{16,32},{32,16},{48,64},{64,48},{80,96},{96,80},{112,128},... | collective-permute-start | bytes 4616 | tf_op jit(solution)/shard_map/ghosts/ppermute | solution.py:100
Sparse Core Ops, SparseCore 0:
  16.4 76.4 all-gather.1

commit v2 on v1

v2 whole, which is shorter than its diff:
```python
import jax
import jax.numpy as jnp
from jax import lax
from jax.experimental import pallas as pl
from jax.experimental.pallas import tpu as pltpu
from jax.sharding import Mesh, PartitionSpec as P

DOM = ("z", "yl")
SP = ("x", "yh", "c")
CHIPS = ("yl", "x", "yh")
PLANE = ("yl", "x", "yh", "c")
CHUNKS = 4
F32, BF16 = jnp.float32, jnp.bfloat16
LAST = (((1,), (1,)), ((), ()))


def main_kernel(
    core_ref, unit_ref, scale_ref, coef_ref, basis_hbm, own_ref, other_ref, energy_ref,
    basis, kernel, slopes, inner, sems,
):
    columns = basis.shape[0]
    step = columns // CHUNKS
    atoms = unit_ref.shape[0]
    half = atoms // 2
    copies = [
        pltpu.make_async_copy(
            basis_hbm.at[pl.ds(i * step, step)], basis.at[pl.ds(i * step, step)], sems.at[i]
        )
        for i in range(CHUNKS)
    ]
    for copy in copies:
        copy.start()
    for i, copy in enumerate(copies):
        copy.wait()
        term = jnp.dot(
            unit_ref[:, i * step : (i + 1) * step],
            basis[i * step : (i + 1) * step, :],
            preferred_element_type=F32,
        )
        if i == 0:
            kernel[...] = term
        else:
            kernel[...] += term
    four = 4.0 * coef_ref[...]
    block = 32
    for r in range(0, atoms, block):
        k = kernel[r : r + block, :]
        s = four * (k * k * k)
        low = s.astype(BF16)
        slopes[r : r + block, :] = low
        inner[r : r + block, :] = jnp.broadcast_to(
            jnp.sum(low.astype(F32) * k, axis=1, keepdims=True), (block, 128)
        )
        kernel[r : r + block, 0:128] = jnp.broadcast_to(
            0.25 * jnp.sum(s * k, axis=1, keepdims=True), (block, 128)
        )
    for y in range(2):
        energy_ref[y] = kernel[y * half : (y + 1) * half, 0:128].T[0:8, :]
    even_first = core_ref[0] == 0
    for j in range(columns // 256):
        g = lax.dot_general(
            slopes[...], basis[j * 256 : (j + 1) * 256, :], LAST, preferred_element_type=F32
        )
        for p in range(2):
            at = slice(j * 256 + p * 128, j * 256 + (p + 1) * 128)
            u = unit_ref[:, at].astype(F32)
            part = (g[:, p * 128 : (p + 1) * 128] - u * inner[...]) * scale_ref[...]

            @pl.when(even_first if p == 0 else jnp.logical_not(even_first))
            def _():
                own_ref[0, j] = part[:half]
                own_ref[1, j] = part[half:]

            @pl.when(jnp.logical_not(even_first) if p == 0 else even_first)
            def _():
                other_ref[0, j] = part[:half]
                other_ref[1, j] = part[half:]


def tail_kernel(parts_ref, deriv_ref, table_ref, out_ref):
    total = parts_ref[0].astype(F32)
    for i in range(1, parts_ref.shape[0]):
        total += parts_ref[i].astype(F32)
    atoms = total.shape[0]
    pairs = deriv_ref.shape[2]
    high = total.astype(BF16)
    low = (total - high.astype(F32)).astype(BF16)
    both = jnp.concatenate([high, low], axis=0)
    slots = pairs // atoms
    row = lax.broadcasted_iota(jnp.int32, (atoms, pairs), 0) * slots
    lane = lax.broadcasted_iota(jnp.int32, (atoms, pairs), 1)
    diagonal = jnp.logical_and(lane >= row, lane < row + slots)
    rows = []
    for c in range(3):
        f = jnp.dot(both, deriv_ref[c], preferred_element_type=F32)
        f = jnp.where(diagonal, f[:atoms] + f[atoms:], 0.0)
        rows.append(jnp.sum(f, axis=0, keepdims=True))
    partial = jnp.concatenate(rows + [jnp.zeros((5, pairs), F32)], axis=0)
    first = partial.astype(BF16)
    rest = partial - first.astype(F32)
    second = rest.astype(BF16)
    third = (rest - second.astype(F32)).astype(BF16)
    pieces = jnp.concatenate([first.astype(F32), second.astype(F32), third.astype(F32)], axis=0)
    moved = jnp.dot(pieces.astype(BF16), table_ref[...], preferred_element_type=F32)
    out_ref[...] = moved[0:8] + moved[8:16] + moved[16:24]


def body(descriptors, sparse_points, coefficients, derivatives, neighbours, counts, ghost_index):
    yl, core = lax.axis_index("yl"), lax.axis_index("c")
    first = yl == 0
    owned, width = descriptors.shape
    points, part = sparse_points.shape
    n_sp, n_plane = lax.axis_size(SP), lax.axis_size(PLANE)
    n_chips = lax.axis_size(CHIPS)
    columns = n_sp * width
    half = points // 2
    slots_count = neighbours.shape[1]
    pairs_count = owned * slots_count
    ghosts = ghost_index.shape[0] // 2

    with jax.named_scope("points_swap"):
        turned = sparse_points.T
        one, two = turned[:, :half], turned[:, half:]
        got = lax.ppermute(jnp.where(first, two, one), "yl", [(0, 1), (1, 0)])
        swapped = jnp.concatenate(
            [jnp.where(first, one, got), jnp.where(first, got, two)], axis=0
        )
    with jax.named_scope("points_gather"):
        basis = lax.all_gather(swapped, "z", axis=0, tiled=True)

    with jax.named_scope("descriptors_gather"):
        spread = jnp.broadcast_to(descriptors[None], (n_plane, owned, width))
        blocks = lax.all_to_all(spread, PLANE, 0, 0).reshape(2, n_sp, owned, width)
        rows = jnp.transpose(blocks, (0, 2, 1, 3)).reshape(2 * owned, columns)
        values = rows.astype(F32)
        row_norm = jnp.sqrt(jnp.sum(values * values, axis=1, keepdims=True) + 1e-06)
        unit_rows = (values / row_norm).astype(BF16)
        scale = 1.0 / row_norm

    with jax.named_scope("scatter_table"):
        slot_total = owned + 2 * ghosts
        flat = neighbours.reshape(pairs_count)
        slot_ids = jnp.arange(slot_total, dtype=jnp.int32)
        hot = (flat[:, None] == slot_ids[None, :]).astype(BF16)
        target = jnp.concatenate(
            [
                jnp.arange(owned, dtype=jnp.int32),
                ghost_index[:ghosts] + owned,
                ghost_index[ghosts:] + 2 * owned,
            ]
        )
        column_ids = jnp.arange(3 * owned, dtype=jnp.int32)
        moves = (target[:, None] == column_ids[None, :]).astype(BF16)
        landed = jnp.dot(hot, moves, preferred_element_type=F32)
        atom_of = jnp.arange(pairs_count, dtype=jnp.int32) // slots_count
        slot_of = jnp.arange(pairs_count, dtype=jnp.int32) % slots_count
        self_hot = (atom_of[:, None] == column_ids[None, :]).astype(F32)
        live = slot_of < jnp.repeat(counts, slots_count)
        table = jnp.where(live[:, None], self_hot - landed, 0.0).astype(BF16)
        lined = jnp.transpose(derivatives, (1, 3, 0, 2)).reshape(3, width, pairs_count)

    with jax.named_scope("main"):
        mine = lax.dynamic_slice_in_dim(coefficients, yl * half, half, 0)[None, :]
        vmem = pl.BlockSpec(memory_space=pltpu.VMEM)
        share = jax.ShapeDtypeStruct((2, n_chips // 2, owned, width), F32)
        own, other, energy_part = pl.pallas_call(
            main_kernel,
            out_shape=(share, share, jax.ShapeDtypeStruct((2, 8, owned), F32)),
            in_specs=[
                pl.BlockSpec(memory_space=pltpu.SMEM),
                vmem,
                vmem,
                vmem,
                pl.BlockSpec(memory_space=pltpu.HBM),
            ],
            out_specs=(vmem, vmem, vmem),
            scratch_shapes=[
                pltpu.VMEM((columns, half), BF16),
                pltpu.VMEM((2 * owned, half), F32),
                pltpu.VMEM((2 * owned, half), BF16),
                pltpu.VMEM((2 * owned, 128), F32),
                pltpu.SemaphoreType.DMA((CHUNKS,)),
            ],
            compiler_params=pltpu.CompilerParams(vmem_limit_bytes=32 << 20),
            cost_estimate=pl.CostEstimate(
                flops=8 * owned * half * columns, bytes_accessed=8 << 20, transcendentals=0
            ),
        )(core.reshape(1).astype(jnp.int32), unit_rows, scale, mine, basis)
    with jax.named_scope("core_pair"):
        theirs = lax.ppermute(other, "c", [(0, 1), (1, 0)])
        outgoing = (own + theirs).astype(BF16).reshape(n_chips, owned, width)
    with jax.named_scope("gradient_exchange"):
        parts = lax.all_to_all(outgoing, CHIPS, 0, 0)
    with jax.named_scope("tail"):
        moved = pl.pallas_call(
            tail_kernel,
            out_shape=jax.ShapeDtypeStruct((8, 3 * owned), F32),
            in_specs=[vmem, vmem, vmem],
            out_specs=vmem,
            compiler_params=pltpu.CompilerParams(vmem_limit_bytes=24 << 20),
            cost_estimate=pl.CostEstimate(
                flops=12 * owned * width * pairs_count, bytes_accessed=4 << 20, transcendentals=0
            ),
        )(parts, lined, table)
        keep, to_left, to_right = jnp.split(moved[:3], 3, axis=1)
    with jax.named_scope("ghosts"):
        across = jnp.where(first, to_left, to_right)
        beside = jnp.where(first, to_right, to_left)
        size = lax.axis_size(DOM)
        pairs = [(i, (i - 1) % size if i % 2 == 0 else (i + 1) % size) for i in range(size)]
        keep = keep + lax.ppermute(across, DOM, pairs)
        both = jnp.stack([jnp.where(first, keep, beside), jnp.where(first, beside, keep)])
        both = jnp.concatenate([both, energy_part[:, :1]], axis=1)
        both = jnp.broadcast_to(both[:, None], (2, n_sp, 4, owned)).reshape(n_plane, 4, owned)
        received = jnp.sum(lax.all_to_all(both, PLANE, 0, 0), axis=0)
    return (received[:3], received[3])


def solution(mesh):
    grid = Mesh(mesh.devices.reshape(16, 2, 4, 2, 2), ("z", "yl", "x", "yh", "c"))
    return jax.shard_map(
        body,
        mesh=grid,
        in_specs=(
            P(DOM, SP),
            P(SP, DOM),
            P(SP),
            P(DOM, None, None, SP),
            P(DOM, None),
            P(DOM),
            P(DOM),
        ),
        out_specs=(P(None, DOM), P(DOM)),
        check_vma=False,
    )
```

time: 167 us -> 162 us (0.970)
  waiting for transfers between devices: 80.6 us -> 71 us
  matrix products: 10.3 us -> 1.18 us
  Pallas kernels: 0 us -> 7.18 us
  blocking collectives: 20 us -> 14 us
  starting transfers between devices: 31.1 us -> 37 us
  local copies, waits for them, and re-layouts: 7.03 us -> 11.4 us
  other arithmetic: 3.49 us -> 5.35 us
    ppermute x1 -> x3, starting transfers between devices: 4.11 us -> 19.4 us  [the longest x1 11.1 us: body(): theirs = lax.ppermute(other, 'c', [(0, 1), (1, 0)])]
    all_to_all x1, waiting for transfers between devices: 18 us -> 3.73 us  [body(): parts = lax.all_to_all(outgoing, CHIPS, 0, 0)]
    all_to_all x1, starting transfers between devices: 16 us -> 6.61 us  [body(): parts = lax.all_to_all(outgoing, CHIPS, 0, 0)]
    dot_general x4 -> x1, matrix products: 10.3 us -> 1.18 us  [body(): landed = jnp.dot(hot, moves, preferred_element_type=F32)]
    pallas_call x0 -> x2, Pallas kernels: none -> 7.18 us  [the longest x1 6.18 us: body(): pl.pallas_call(main_kernel, out_shape=(share, share, jax.ShapeDtypeStruct...]
    all_to_all x2 -> x1, blocking collectives: 20 us -> 14 us  [body(): received = jnp.sum(lax.all_to_all(both, PLANE, 0, 0), axis=0)]
    ppermute x1 -> x3, waiting for transfers between devices: 2.32 us -> 6.66 us  [the longest x1 2.34 us: body(): got = lax.ppermute(jnp.where(first, two, one), 'yl', [(0, 1), (1, 0)])]
    unnamed x16 -> x15, local copies, waits for them, and re-layouts: 0.39 us -> 2.38 us
  transfers between devices with their start and end apart: 4 -> 6, of which waited for: 4 -> 6; matrix products, arithmetic and copies ran while one was open for 4% -> 7% of each run, Pallas kernels for 0% -> 0%
where the time goes in v2:
time: 162 us; the launch traced here: 161 us
  waiting for transfers between devices  71 us (44%)
  starting transfers between devices  37 us (23%)
  between operations  14.3 us (9%)
  blocking collectives  14 us (9%)
  local copies, waits for them, and re-layouts  11.4 us (7%)
  Pallas kernels  7.18 us (4%)
  other arithmetic  5.35 us (3%)
    all_gather x1, waiting for transfers between devices, body(): basis = lax.all_gather(swapped, 'z', axis=0, tiled=True)  43.4 us
    all_to_all x1, waiting for transfers between devices, body(): blocks = lax.all_to_all(spread, PLANE, 0, 0).reshape(2, n_sp, owned, width)  17.2 us
    all_to_all x1, blocking collectives, body(): received = jnp.sum(lax.all_to_all(both, PLANE, 0, 0), axis=0)  14 us
    ppermute x1, starting transfers between devices, body(): theirs = lax.ppermute(other, 'c', [(0, 1), (1, 0)])  11.1 us
    all_to_all x1, starting transfers between devices, body(): blocks = lax.all_to_all(spread, PLANE, 0, 0).reshape(2, n_sp, owned, width)  10.9 us
    all_to_all x1, starting transfers between devices, body(): parts = lax.all_to_all(outgoing, CHIPS, 0, 0)  6.61 us
    pallas_call x1, Pallas kernels, body(): pl.pallas_call(main_kernel, out_shape=(share, share, jax.ShapeDtypeStruct...  6.18 us
    ppermute x1, starting transfers between devices, body(): keep = keep + lax.ppermute(across, DOM, pairs)  4.33 us
  transfers between devices with their start and end apart: 6, of which 6 were waited for; matrix products, arithmetic and copies ran while one was open for 7% of the time, Pallas kernels for 0%

profile of v2, /device:TPU:1, one launch (start us, length us, event | category | flops | bytes accessed | tf_op | source)
XLA Modules:
  0.0 161.5 jit_solution(3141927001655917485)
XLA Ops:
  7.2 0.0 all-gather.2.cloned.1.call-start
  7.2 1.0 broadcast_select_fusion.2
  8.2 4.0 %collective-permute-start = (bf16[64,1024]{1,0:T(8,128)(2,1)S(1)}, bf16[64,1024]{1,0:T(8,128)(2,1)S(1)}, u32[]{:S(2)}, u32[]{:S(2)}) collective-permute-start(bf16[64,1024]{1,0:T(8,128)(2,1)S(1)} %broadcast_select_fusion.2), channel_id=1, source_target_pairs={{0,16},{16,0},{1,17},{17,1},{2,18},{18,2},{3,19},{19,3},{4,20},{20... | collective-permute-start | bytes 393224 | tf_op jit(solution)/shard_map/points_swap/ppermute | solution.py:124
  12.2 2.3 %collective-permute-done = bf16[64,1024]{1,0:T(8,128)(2,1)S(1)} collective-permute-done((bf16[64,1024]{1,0:T(8,128)(2,1)S(1)}, bf16[64,1024]{1,0:T(8,128)(2,1)S(1)}, u32[]{:S(2)}, u32[]{:S(2)}) %collective-permute-start) | collective-permute-done | bytes 131104 | tf_op jit(solution)/shard_map/points_swap/ppermute | solution.py:124
  14.6 1.0 broadcast_select_fusion.1
  15.6 0.0 copy-start.4
  15.6 0.7 pad_maximum_fusion
  16.3 0.0 all-gather.2.cloned.1.call-update
  16.4 2.0 %broadcast_in_dim.20 = bf16[32,128,128]{2,1,0:T(8,128)(2,1)} broadcast(bf16[128,128]{1,0:T(8,128)(2,1)} %param.7), dimensions={1,2} | broadcast | bytes 1081344 | tf_op jit(solution)/shard_map/descriptors_gather/broadcast_in_dim | solution.py:132
  18.3 10.9 %all-to-all-start = ((bf16[32,128,128]{2,1,0:T(8,128)(2,1)}), bf16[32,128,128]{2,1,0:T(8,128)(2,1)S(1)}, u32[]{:S(2)}, u32[]{:S(2)}) async-start(bf16[32,128,128]{2,1,0:T(8,128)(2,1)} %broadcast_in_dim.20), calls=%async_computation | async-start | bytes 2097152 | tf_op jit(solution)/shard_map/descriptors_gather/all_to_all | solution.py:133
  29.3 0.0 copy-done.4
  29.3 17.2 %all-to-all-done = bf16[32,128,128]{2,1,0:T(8,128)(2,1)S(1)} async-done(((bf16[32,128,128]{2,1,0:T(8,128)(2,1)}), bf16[32,128,128]{2,1,0:T(8,128)(2,1)S(1)}, u32[]{:S(2)}, u32[]{:S(2)}) %all-to-all-start) | async-done | bytes 1048608 | tf_op jit(solution)/shard_map/descriptors_gather/all_to_all | solution.py:133
  46.5 0.2 convert_element_type.42
  46.7 1.2 copy.21
  48.0 0.6 multiply_reduce_fusion
  48.6 0.1 copy.22.scale_ref
  48.8 0.7 fusion.2.unit_ref
  49.5 43.4 %all-gather.2.cloned.1.call-done.basis_hbm = bf16[2048,1024]{1,0:T(8,128)(2,1)} async-done(((bf16[128,1024]{1,0:T(8,128)(2,1)}), bf16[2048,1024]{1,0:T(8,128)(2,1)}) %all-gather.2.cloned.1.call-update) | async-done | bytes 4194320 | tf_op jit(solution)/shard_map/points_gather/all_gather | solution.py:129
  92.9 0.0 copy-start
  92.9 2.2 %copy-done = bf16[2048,1024]{1,0:T(8,128)(2,1)S(1)} copy-done((bf16[2048,1024]{1,0:T(8,128)(2,1)S(1)}, bf16[2048,1024]{1,0:T(8,128)(2,1)}, u32[]{:S(2)}) %copy-start) | copy-done | bytes 4194328
  95.1 0.0 copy-start.5
  95.1 6.2 %main.1 = (f32[2,8,128,128]{3,2,1,0:T(8,128)S(1)}, f32[2,8,128,128]{3,2,1,0:T(8,128)S(1)}, f32[2,8,128]{2,1,0:T(8,128)S(1)}) custom-call(s32[1]{0:T(128)} %bitcast.core_ref, bf16[256,2048]{1,0:T(8,128)(2,1)S(1)} %fusion.2.unit_ref, f32[256,1]{1,0:T(8,128)S(1)} %copy.22.scale_ref, f32[1,1024]{1,0:T(1,128)S(1)} %bitcast.29, bf16[2048,1024]{1,0:T(8,128)(2,1)S(1)} %copy-done), custom_call_target="tpu_custom_call" | custom-call | flops 2147483648 | bytes 8388608 | tf_op jit(solution)/shard_map/main/pallas_call | solution.py:166
  101.3 0.0 copy-start.1
  101.3 11.1 %collective-permute-start.1 = (f32[2,8,128,128]{3,2,1,0:T(8,128)S(1)}, f32[2,8,128,128]{3,2,1,0:T(8,128)S(1)}, u32[]{:S(2)}, u32[]{:S(2)}) collective-permute-start(f32[2,8,128,128]{3,2,1,0:T(8,128)S(1)} %get-tuple-element.6), channel_id=1, source_target_pairs={{0,1},{1,0},{2,3},{3,2},{4,5},{5,4},{6,7},{7,6},{8,9},{9,8},{10,11... | collective-permute-start | bytes 3145736 | tf_op jit(solution)/shard_map/core_pair/ppermute | solution.py:190
  112.4 0.0 copy-done.5
  112.4 2.2 %collective-permute-done.1 = f32[2,8,128,128]{3,2,1,0:T(8,128)S(1)} collective-permute-done((f32[2,8,128,128]{3,2,1,0:T(8,128)S(1)}, f32[2,8,128,128]{3,2,1,0:T(8,128)S(1)}, u32[]{:S(2)}, u32[]{:S(2)}) %collective-permute-start.1) | collective-permute-done | bytes 1048608 | tf_op jit(solution)/shard_map/core_pair/ppermute | solution.py:190
  114.6 0.9 add_convert_fusion
  115.6 6.6 %all-to-all-start.1 = ((bf16[16,128,128]{2,1,0:T(8,128)(2,1)}), bf16[16,128,128]{2,1,0:T(8,128)(2,1)S(1)}, u32[]{:S(2)}, u32[]{:S(2)}) async-start(bf16[16,128,128]{2,1,0:T(8,128)(2,1)} %bitcast.8), calls=%async_computation.1 | async-start | bytes 1048576 | tf_op jit(solution)/shard_map/gradient_exchange/all_to_all | solution.py:193
  122.2 0.0 copy-done.1
  122.2 2.0 %copy.23 = bf16[3,128,128,12]{1,3,2,0:T(8,128)(2,1)} copy(bf16[3,128,128,12]{1,2,3,0:T(8,128)(2,1)S(1)} %bitcast.32) | data formatting | bytes 2359296 | tf_op jit(solution)/shard_map/scatter_table/transpose | solution.py:160
  124.2 0.0 copy-start.2
  124.2 0.0 copy-start.6
  124.2 2.3 %reshape.89 = bf16[3,128,1536]{1,2,0:T(8,128)(2,1)S(1)} reshape(bf16[3,128,128,12]{1,3,2,0:T(8,128)(2,1)} %copy.23) | data formatting | bytes 2359296 | tf_op jit(solution)/shard_map/scatter_table/reshape | solution.py:160
  126.5 0.6 copy.25.deriv_ref
  127.1 0.0 copy-done.2
  127.2 0.1 copy.24
  127.3 0.1 eq.50
  127.4 0.0 copy-done.6
  127.4 0.1 broadcast_in_dim.22
  127.5 0.1 reshape.90
  127.6 1.2 fusion.1.table_ref
  128.8 3.7 %all-to-all-done.1.parts_ref = bf16[16,128,128]{2,1,0:T(8,128)(2,1)S(1)} async-done(((bf16[16,128,128]{2,1,0:T(8,128)(2,1)}), bf16[16,128,128]{2,1,0:T(8,128)(2,1)S(1)}, u32[]{:S(2)}, u32[]{:S(2)}) %all-to-all-start.1) | async-done | bytes 524320 | tf_op jit(solution)/shard_map/gradient_exchange/all_to_all | solution.py:193
  132.5 1.0 tail.1
  133.5 4.3 %collective-permute-start.2 = (f32[3,128]{1,0:T(4,128)S(1)}, f32[3,128]{1,0:T(4,128)S(1)}, u32[]{:S(2)}, u32[]{:S(2)}) collective-permute-start(f32[3,128]{1,0:T(4,128)S(1)} %slice_select_fusion.1), channel_id=1, source_target_pairs={{0,496},{16,32},{32,16},{48,64},{64,48},{80,96},{96,80},{112,128},... | collective-permute-start | bytes 4616 | tf_op jit(solution)/shard_map/ghosts/ppermute | solution.py:211
  137.9 2.1 %collective-permute-done.2 = f32[3,128]{1,0:T(4,128)S(1)} collective-permute-done((f32[3,128]{1,0:T(4,128)S(1)}, f32[3,128]{1,0:T(4,128)S(1)}, u32[]{:S(2)}, u32[]{:S(2)}) %collective-permute-start.2) | collective-permute-done | bytes 1568 | tf_op jit(solution)/shard_map/ghosts/ppermute | solution.py:211
  140.0 14.0 %all_to_all.15 = f32[32,4,128]{2,1,0:T(4,128)S(1)} all-to-all(f32[32,4,128]{2,1,0:T(4,128)S(1)} %bitcast.35), channel_id=1, replica_groups=mesh['z'=16,'yl'=2,'x'=4,'yh'=2,'c'=2] {'yl','x','yh','c'}, dimensions={0} | all-to-all | bytes 131072 | tf_op jit(solution)/shard_map/ghosts/all_to_all | solution.py:215
  154.0 0.0 copy-start.3
  154.0 0.5 slice_bitcast_fusion
  154.5 0.1 copy-done.3
  (14 shorter events, 0.2 us)
Async XLA Ops:
  7.2 85.7 %all-gather.2.cloned.1.call-start = ((), (), s32[]{:S(2)}) async-start(), calls=%async_computation.3 | async-start | bytes 4456448 | tf_op jit(solution)/shard_map/points_gather/all_gather | solution.py:129
  8.2 6.4 %collective-permute-start = (bf16[64,1024]{1,0:T(8,128)(2,1)S(1)}, bf16[64,1024]{1,0:T(8,128)(2,1)S(1)}, u32[]{:S(2)}, u32[]{:S(2)}) collective-permute-start(bf16[64,1024]{1,0:T(8,128)(2,1)S(1)} %broadcast_select_fusion.2), channel_id=1, source_target_pairs={{0,16},{16,0},{1,17},{17,1},{2,18},{18,2},{3,19},{19,3},{4,20},{20... | collective-permute-start | bytes 393224 | tf_op jit(solution)/shard_map/points_swap/ppermute | solution.py:124
  15.6 13.7 %copy-start.4 = (f32[2048]{0:T(1024)S(1)}, f32[2048]{0:T(1024)}, u32[]{:S(2)}) copy-start(f32[2048]{0:T(1024)} %param.9) | copy-start | bytes 24580
  18.3 28.2 %all-to-all-start = ((bf16[32,128,128]{2,1,0:T(8,128)(2,1)}), bf16[32,128,128]{2,1,0:T(8,128)(2,1)S(1)}, u32[]{:S(2)}, u32[]{:S(2)}) async-start(bf16[32,128,128]{2,1,0:T(8,128)(2,1)} %broadcast_in_dim.20), calls=%async_computation | async-start | bytes 2097152 | tf_op jit(solution)/shard_map/descriptors_gather/all_to_all | solution.py:133
  92.9 2.2 %copy-start = (bf16[2048,1024]{1,0:T(8,128)(2,1)S(1)}, bf16[2048,1024]{1,0:T(8,128)(2,1)}, u32[]{:S(2)}) copy-start(bf16[2048,1024]{1,0:T(8,128)(2,1)} %all-gather.2.cloned.1.call-done.basis_hbm) | copy-start | bytes 12582916
  95.1 17.3 %copy-start.5 = (s32[256]{0:T(256)S(1)}, s32[256]{0:T(256)}, u32[]{:S(2)}) copy-start(s32[256]{0:T(256)} %param.13) | copy-start | bytes 3076
  101.3 21.0 %copy-start.1 = (bf16[128,3,12,128]{3,0,2,1:T(8,128)(2,1)S(1)}, bf16[128,3,12,128]{3,0,2,1:T(8,128)(2,1)}, u32[]{:S(2)}) copy-start(bf16[128,3,12,128]{3,0,2,1:T(8,128)(2,1)} %param.10) | copy-start | bytes 3538948
  101.3 13.3 %collective-permute-start.1 = (f32[2,8,128,128]{3,2,1,0:T(8,128)S(1)}, f32[2,8,128,128]{3,2,1,0:T(8,128)S(1)}, u32[]{:S(2)}, u32[]{:S(2)}) collective-permute-start(f32[2,8,128,128]{3,2,1,0:T(8,128)S(1)} %get-tuple-element.6), channel_id=1, source_target_pairs={{0,1},{1,0},{2,3},{3,2},{4,5},{5,4},{6,7},{7,6},{8,9},{9,8},{10,11... | collective-permute-start | bytes 3145736 | tf_op jit(solution)/shard_map/core_pair/ppermute | solution.py:190
  115.6 16.9 %all-to-all-start.1 = ((bf16[16,128,128]{2,1,0:T(8,128)(2,1)}), bf16[16,128,128]{2,1,0:T(8,128)(2,1)S(1)}, u32[]{:S(2)}, u32[]{:S(2)}) async-start(bf16[16,128,128]{2,1,0:T(8,128)(2,1)} %bitcast.8), calls=%async_computation.1 | async-start | bytes 1048576 | tf_op jit(solution)/shard_map/gradient_exchange/all_to_all | solution.py:193
  124.2 2.9 %copy-start.2 = (s32[128,12]{0,1:T(8,128)S(1)}, s32[128,12]{0,1:T(8,128)}, u32[]{:S(2)}) copy-start(s32[128,12]{0,1:T(8,128)} %param.11) | copy-start | bytes 18436
  124.2 3.1 %copy-start.6 = (s32[128]{0:T(128)S(1)}, s32[128]{0:T(128)}, u32[]{:S(2)}) copy-start(s32[128]{0:T(128)} %param.12) | copy-start | bytes 1540
  133.5 6.4 %collective-permute-start.2 = (f32[3,128]{1,0:T(4,128)S(1)}, f32[3,128]{1,0:T(4,128)S(1)}, u32[]{:S(2)}, u32[]{:S(2)}) collective-permute-start(f32[3,128]{1,0:T(4,128)S(1)} %slice_select_fusion.1), channel_id=1, source_target_pairs={{0,496},{16,32},{32,16},{48,64},{64,48},{80,96},{96,80},{112,128},... | collective-permute-start | bytes 4616 | tf_op jit(solution)/shard_map/ghosts/ppermute | solution.py:211
  154.0 0.6 copy-start.3
Sparse Core Ops, SparseCore 0:
  16.5 76.3 all-gather.1

commit v3 on v2

v3 whole, which is shorter than its diff:
```python
import jax
import jax.numpy as jnp
from jax import lax
from jax.experimental import pallas as pl
from jax.experimental.pallas import tpu as pltpu
from jax.sharding import Mesh, PartitionSpec as P

DOM = ("zh", "zl", "yl")
SP = ("x", "yh", "c")
QUARTER = ("zl", "yl")
CHIPS = ("zl", "yl", "x", "yh")
SLAB = ("zl", "yl", "x", "yh", "c")
F32, BF16 = jnp.float32, jnp.bfloat16
LAST = (((1,), (1,)), ((), ()))


def main_kernel(place_ref, unit_ref, scale_ref, coef_ref, *rest):
    (*blocks, own_ref, other_ref, energy_ref, basis, kernel, slopes, inner, scale) = rest
    depth = blocks[0].shape[0]
    atoms = unit_ref.shape[0]
    domains = energy_ref.shape[0]
    owned = atoms // domains
    for i, block in enumerate(blocks):
        at = pl.multiple_of(place_ref[1 + i] * depth, depth)
        basis[pl.ds(at, depth), :] = block[...]
    kernel[...] = jnp.dot(unit_ref[...], basis[...], preferred_element_type=F32)
    four = 4.0 * coef_ref[...]
    rows = 32
    for r in range(0, atoms, rows):
        k = kernel[r : r + rows, :]
        s = four * (k * k * k)
        low = s.astype(BF16)
        slopes[r : r + rows, :] = low
        wide = jnp.broadcast_to(scale_ref[r : r + rows, :], (rows, 128))
        scale[r : r + rows, :] = wide
        inner[r : r + rows, :] = wide * jnp.sum(low.astype(F32) * k, axis=1, keepdims=True)
        kernel[r : r + rows, 0:128] = jnp.broadcast_to(
            0.25 * jnp.sum(s * k, axis=1, keepdims=True), (rows, 128)
        )
    for y in range(domains):
        energy_ref[y] = kernel[y * owned : (y + 1) * owned, 0:128].T[0:8, :]
    even_first = place_ref[0] == 0
    for j in range(len(blocks)):
        g = lax.dot_general(
            slopes[...],
            basis[j * depth : (j + 1) * depth, :],
            LAST,
            preferred_element_type=F32,
        )
        for p in range(2):
            lanes = slice(j * depth + p * 128, j * depth + (p + 1) * 128)
            u = unit_ref[:, lanes].astype(F32)
            part = g[:, p * 128 : (p + 1) * 128] * scale[...] - u * inner[...]

            @pl.when(even_first if p == 0 else jnp.logical_not(even_first))
            def _():
                for y in range(domains):
                    own_ref[y, j] = part[y * owned : (y + 1) * owned]

            @pl.when(jnp.logical_not(even_first) if p == 0 else even_first)
            def _():
                for y in range(domains):
                    other_ref[y, j] = part[y * owned : (y + 1) * owned]


def tail_kernel(parts_ref, deriv_ref, table_ref, out_ref):
    total = parts_ref[0].astype(F32)
    for i in range(1, parts_ref.shape[0]):
        total += parts_ref[i].astype(F32)
    atoms = total.shape[0]
    pairs = deriv_ref.shape[2]
    high = total.astype(BF16)
    low = (total - high.astype(F32)).astype(BF16)
    both = jnp.concatenate([high, low], axis=0)
    slots = pairs // atoms
    row = lax.broadcasted_iota(jnp.int32, (atoms, pairs), 0) * slots
    lane = lax.broadcasted_iota(jnp.int32, (atoms, pairs), 1)
    diagonal = jnp.logical_and(lane >= row, lane < row + slots)
    rows = []
    for c in range(3):
        f = jnp.dot(both, deriv_ref[c], preferred_element_type=F32)
        f = jnp.where(diagonal, f[:atoms] + f[atoms:], 0.0)
        rows.append(jnp.sum(f, axis=0, keepdims=True))
    partial = jnp.concatenate(rows + [jnp.zeros((5, pairs), F32)], axis=0)
    first = partial.astype(BF16)
    rest = partial - first.astype(F32)
    second = rest.astype(BF16)
    third = (rest - second.astype(F32)).astype(BF16)
    pieces = jnp.concatenate([first.astype(F32), second.astype(F32), third.astype(F32)], axis=0)
    moved = jnp.dot(pieces.astype(BF16), table_ref[...], preferred_element_type=F32)
    out_ref[...] = moved[0:8] + moved[8:16] + moved[16:24]


def body(descriptors, sparse_points, coefficients, derivatives, neighbours, counts, ghost_index):
    core = lax.axis_index("c")
    quarter = lax.axis_index(QUARTER)
    slab = lax.axis_index("zh")
    owned, width = descriptors.shape
    points, part = sparse_points.shape
    n_sp, n_chips, n_slab = (lax.axis_size(SP), lax.axis_size(CHIPS), lax.axis_size(SLAB))
    n_quarter, n_ring = lax.axis_size(QUARTER), lax.axis_size("zh")
    columns = n_sp * width
    share = points // n_quarter
    atoms = n_quarter * owned
    slots_count = neighbours.shape[1]
    pairs_count = owned * slots_count
    ghosts = ghost_index.shape[0] // 2
    swap = [(0, 1), (1, 0)]

    with jax.named_scope("points_swap"):
        split = jnp.transpose(sparse_points.T.reshape(part, n_quarter, share), (1, 0, 2))
        block = lax.all_to_all(split, QUARTER, 0, 0).reshape(n_quarter * part, share)
    with jax.named_scope("points_ring"):
        up = [(i, (i + 1) % n_ring) for i in range(n_ring)]
        down = [(i, (i - 1) % n_ring) for i in range(n_ring)]
        blocks, places = [block], [slab]
        above = below = block
        for step in range(1, n_ring // 2 + 1):
            above = lax.ppermute(above, "zh", up)
            blocks.append(above)
            places.append((slab - step) % n_ring)
            if step < n_ring // 2:
                below = lax.ppermute(below, "zh", down)
                blocks.append(below)
                places.append((slab + step) % n_ring)
            if step == 2:
                middle = above

    with jax.named_scope("descriptors_gather"):
        spread = jnp.broadcast_to(descriptors[None], (n_chips, owned, width))
        spread, _ = lax.optimization_barrier((spread, block))
        mine = lax.all_to_all(spread, CHIPS, 0, 0)
        mine, _ = lax.optimization_barrier((mine, middle))
        theirs = lax.ppermute(mine, "c", swap)
        even, odd = jnp.where(core == 0, mine, theirs), jnp.where(core == 0, theirs, mine)
        halves = jnp.stack([even, odd]).reshape(2, n_quarter, n_sp // 2, owned, width)
        rows = jnp.transpose(halves, (1, 3, 2, 0, 4)).reshape(atoms, columns)
        values = rows.astype(F32)
        row_norm = jnp.sqrt(jnp.sum(values * values, axis=1, keepdims=True) + 1e-06)
        unit_rows = (values / row_norm).astype(BF16)
        scale = 1.0 / row_norm

    with jax.named_scope("scatter_table"):
        slot_total = owned + 2 * ghosts
        flat = neighbours.reshape(pairs_count)
        slot_ids = jnp.arange(slot_total, dtype=jnp.int32)
        hot = (flat[:, None] == slot_ids[None, :]).astype(BF16)
        target = jnp.concatenate(
            [
                jnp.arange(owned, dtype=jnp.int32),
                ghost_index[:ghosts] + owned,
                ghost_index[ghosts:] + 2 * owned,
            ]
        )
        column_ids = jnp.arange(3 * owned, dtype=jnp.int32)
        moves = (target[:, None] == column_ids[None, :]).astype(BF16)
        landed = jnp.dot(hot, moves, preferred_element_type=F32)
        atom_of = jnp.arange(pairs_count, dtype=jnp.int32) // slots_count
        slot_of = jnp.arange(pairs_count, dtype=jnp.int32) % slots_count
        self_hot = (atom_of[:, None] == column_ids[None, :]).astype(F32)
        live = slot_of < jnp.repeat(counts, slots_count)
        table = jnp.where(live[:, None], self_hot - landed, 0.0).astype(BF16)
        lined = jnp.transpose(derivatives, (1, 3, 0, 2)).reshape(3, width, pairs_count)

    unit_rows, scale, table, lined = lax.optimization_barrier((unit_rows, scale, table, lined))
    with jax.named_scope("main"):
        coefs = lax.dynamic_slice_in_dim(coefficients, quarter * share, share, 0)[None, :]
        vmem = pl.BlockSpec(memory_space=pltpu.VMEM)
        piece = jax.ShapeDtypeStruct((n_quarter, n_sp // 2, owned, width), F32)
        own, other, energy_part = pl.pallas_call(
            main_kernel,
            out_shape=(piece, piece, jax.ShapeDtypeStruct((n_quarter, 8, owned), F32)),
            in_specs=[pl.BlockSpec(memory_space=pltpu.SMEM)] + [vmem] * (3 + len(blocks)),
            out_specs=(vmem, vmem, vmem),
            scratch_shapes=[
                pltpu.VMEM((columns, share), BF16),
                pltpu.VMEM((atoms, share), F32),
                pltpu.VMEM((atoms, share), BF16),
                pltpu.VMEM((atoms, 128), F32),
                pltpu.VMEM((atoms, 128), F32),
            ],
            compiler_params=pltpu.CompilerParams(vmem_limit_bytes=32 << 20),
            cost_estimate=pl.CostEstimate(
                flops=4 * atoms * share * columns, bytes_accessed=8 << 20, transcendentals=0
            ),
        )(jnp.stack([core] + places).astype(jnp.int32), unit_rows, scale, coefs, *blocks)
    with jax.named_scope("core_pair"):
        outgoing = (own + lax.ppermute(other, "c", swap)).astype(BF16)
        outgoing = outgoing.reshape(n_chips, owned, width)
    with jax.named_scope("gradient_exchange"):
        parts = lax.all_to_all(outgoing, CHIPS, 0, 0)
    with jax.named_scope("tail"):
        moved = pl.pallas_call(
            tail_kernel,
            out_shape=jax.ShapeDtypeStruct((8, 3 * owned), F32),
            in_specs=[vmem, vmem, vmem],
            out_specs=vmem,
            compiler_params=pltpu.CompilerParams(vmem_limit_bytes=24 << 20),
            cost_estimate=pl.CostEstimate(
                flops=12 * owned * width * pairs_count, bytes_accessed=4 << 20, transcendentals=0
            ),
        )(parts, lined, table)
        keep, to_left, to_right = jnp.split(moved[:3], 3, axis=1)
    with jax.named_scope("ghosts"):
        lowest = quarter == 0
        size = lax.axis_size(DOM)
        pairs = [(i, (i - 1) % size) for i in range(0, size, n_quarter)]
        pairs += [(i, (i + 1) % size) for i in range(n_quarter - 1, size, n_quarter)]
        keep = keep + lax.ppermute(jnp.where(lowest, to_left, to_right), DOM, pairs)
        to = jnp.arange(n_quarter, dtype=jnp.int32)[:, None, None]
        sent = jnp.where(to == quarter, keep, 0.0)
        sent = jnp.where(to == quarter - 1, to_left, sent)
        sent = jnp.where(to == quarter + 1, to_right, sent)
        sent = jnp.concatenate([sent, energy_part[:, :1]], axis=1)
        sent = jnp.broadcast_to(sent[:, None], (n_quarter, n_sp, 4, owned))
        received = lax.all_to_all(sent.reshape(n_slab, 4, owned), SLAB, 0, 0)
        received = jnp.sum(received, axis=0)
    return (received[:3], received[3])


def solution(mesh):
    grid = Mesh(
        mesh.devices.reshape(8, 2, 2, 4, 2, 2), ("zh", "zl", "yl", "x", "yh", "c")
    )
    return jax.shard_map(
        body,
        mesh=grid,
        in_specs=(
            P(DOM, SP),
            P(SP, DOM),
            P(SP),
            P(DOM, None, None, SP),
            P(DOM, None),
            P(DOM),
            P(DOM),
        ),
        out_specs=(P(None, DOM), P(DOM)),
        check_vma=False,
    )
```

time: 162 us -> 194 us (1.20)
  local copies, waits for them, and re-layouts: 11.4 us -> 26.5 us
  between operations: 14.3 us -> 1.02 us
  blocking collectives: 14 us -> 25.1 us
  starting transfers between devices: 37 us -> 47.6 us
  waiting for transfers between devices: 71 us -> 74.1 us
  other arithmetic: 5.35 us -> 7.96 us
    ppermute x3 -> x10, waiting for transfers between devices: 6.66 us -> 59.3 us  [the longest x4 37.3 us: body(): above = lax.ppermute(above, 'zh', up)]
    all_gather x1 -> x0, waiting for transfers between devices: 43.4 us -> none  [body(): basis = lax.all_gather(swapped, 'z', axis=0, tiled=True)]
    all_to_all x1, waiting for transfers between devices: 17.2 us -> 0.01 us  [body(): mine = lax.all_to_all(spread, CHIPS, 0, 0)]
    ppermute x3 -> x10, starting transfers between devices: 19.4 us -> 35.7 us  [the longest x4 15.3 us: body(): above = lax.ppermute(above, 'zh', up)]
    all_to_all x1 -> x2, blocking collectives: 14 us -> 25.1 us  [the longest x1 15.9 us: body(): received = lax.all_to_all(sent.reshape(n_slab, 4, owned), SLAB, 0, 0)]
    all_to_all x1, waiting for transfers between devices: 3.73 us -> 14.8 us  [body(): parts = lax.all_to_all(outgoing, CHIPS, 0, 0)]
    convert_element_type x1 -> x2, local copies, waits for them, and re-layouts: 1.22 us -> 11.7 us  [body(): values = rows.astype(F32)]
    all_to_all x1, starting transfers between devices: 10.9 us -> 7.52 us  [body(): mine = lax.all_to_all(spread, CHIPS, 0, 0)]
  transfers between devices with their start and end apart: 6 -> 12, of which waited for: 6 -> 7; matrix products, arithmetic and copies ran while one was open for 7% -> 13% of each run, Pallas kernels for 0% -> 0%
where the time goes in v3:
time: 194 us; the launch traced here: 192 us
  waiting for transfers between devices  74.1 us (38%)
  starting transfers between devices  47.6 us (25%)
  local copies, waits for them, and re-layouts  26.5 us (14%)
  blocking collectives  25.1 us (13%)
  Pallas kernels  8.39 us (4%)
  other arithmetic  7.96 us (4%)
    ppermute x4, waiting for transfers between devices, body(): above = lax.ppermute(above, 'zh', up)  37.3 us
    ppermute x3, waiting for transfers between devices, body(): below = lax.ppermute(below, 'zh', down)  17.3 us
    all_to_all x1, blocking collectives, body(): received = lax.all_to_all(sent.reshape(n_slab, 4, owned), SLAB, 0, 0)  15.9 us
    ppermute x4, starting transfers between devices, body(): above = lax.ppermute(above, 'zh', up)  15.3 us
    all_to_all x1, waiting for transfers between devices, body(): parts = lax.all_to_all(outgoing, CHIPS, 0, 0)  14.8 us
    convert_element_type x2, local copies, waits for them, and re-layouts, body(): values = rows.astype(F32)  11.7 us
    all_to_all x1, blocking collectives, body(): lax.all_to_all(split, QUARTER, 0, 0).reshape(n_quarter * part, share)  9.26 us
    all_to_all x1, starting transfers between devices, body(): mine = lax.all_to_all(spread, CHIPS, 0, 0)  7.52 us
  transfers between devices with their start and end apart: 12, of which 7 were waited for; matrix products, arithmetic and copies ran while one was open for 13% of the time, Pallas kernels for 0%

profile of v3, /device:TPU:1, one launch (start us, length us, event | category | flops | bytes accessed | tf_op | source)
XLA Modules:
  0.0 191.8 jit_solution(1034386334697848542)
XLA Ops:
  0.7 1.0 copy.36
  1.6 0.0 copy-start.10
  1.6 0.0 copy-start.9
  1.7 9.3 %all_to_all.20 = bf16[4,64,512]{2,1,0:T(8,128)(2,1)S(1)} all-to-all(bf16[4,64,512]{2,1,0:T(8,128)(2,1)S(1)} %bitcast.43), channel_id=1, replica_groups=mesh['zh'=8,'zl'=2,'yl'=2,'x'=4,'yh'=2,'c'=2] {'zl','yl'}, dimensions={0} | all-to-all | bytes 524288 | tf_op jit(solution)/shard_map/points_swap/all_to_all | solution.py:112
  10.9 2.0 %broadcast_in_dim.75 = bf16[32,128,128]{2,1,0:T(8,128)(2,1)} broadcast(bf16[128,128]{1,0:T(8,128)(2,1)} %param.7), dimensions={1,2} | broadcast | bytes 1081344 | tf_op jit(solution)/shard_map/descriptors_gather/broadcast_in_dim | solution.py:130
  12.9 7.5 %all-to-all-start.1 = ((bf16[32,128,128]{2,1,0:T(8,128)(2,1)}), bf16[32,128,128]{2,1,0:T(8,128)(2,1)}, u32[]{:S(2)}, u32[]{:S(2)}) async-start(bf16[32,128,128]{2,1,0:T(8,128)(2,1)} %broadcast_in_dim.75), calls=%async_computation.1 | async-start | bytes 2097152 | tf_op jit(solution)/shard_map/descriptors_gather/all_to_all | solution.py:132
  20.4 4.9 %collective-permute-start = (bf16[256,512]{1,0:T(8,128)(2,1)S(1)}, bf16[256,512]{1,0:T(8,128)(2,1)S(1)}, u32[]{:S(2)}, u32[]{:S(2)}) collective-permute-start(bf16[256,512]{1,0:T(8,128)(2,1)S(1)} %bitcast.34), channel_id=1, source_target_pairs={{0,64},{64,128},{128,192},{192,256},{256,320},{320,384},{384,448},... | collective-permute-start | bytes 786440 | tf_op jit(solution)/shard_map/points_ring/ppermute | solution.py:119
  25.3 30.7 %collective-permute-done.rest_1_ = bf16[256,512]{1,0:T(8,128)(2,1)S(1)} collective-permute-done((bf16[256,512]{1,0:T(8,128)(2,1)S(1)}, bf16[256,512]{1,0:T(8,128)(2,1)S(1)}, u32[]{:S(2)}, u32[]{:S(2)}) %collective-permute-start) | collective-permute-done | bytes 262176 | tf_op jit(solution)/shard_map/points_ring/ppermute | solution.py:119
  56.0 1.9 collective-permute-start.1
  57.9 0.7 copy-done.3
  58.6 6.6 %collective-permute-done.1.rest_3_ = bf16[256,512]{1,0:T(8,128)(2,1)S(1)} collective-permute-done((bf16[256,512]{1,0:T(8,128)(2,1)S(1)}, bf16[256,512]{1,0:T(8,128)(2,1)S(1)}, u32[]{:S(2)}, u32[]{:S(2)}) %collective-permute-start.1) | collective-permute-done | bytes 262176 | tf_op jit(solution)/shard_map/points_ring/ppermute | solution.py:119
  65.2 0.0 all-to-all-done.1
  65.2 5.8 %collective-permute-start.2 = (bf16[32,128,128]{2,1,0:T(8,128)(2,1)}, bf16[32,128,128]{2,1,0:T(8,128)(2,1)}, u32[]{:S(2)}, u32[]{:S(2)}) collective-permute-start(bf16[32,128,128]{2,1,0:T(8,128)(2,1)} %all-to-all-done.1), channel_id=1, source_target_pairs={{0,1},{1,0},{2,3},{3,2},{4,5},{5,4},{6,7},{7,6},{8,9},{9,8},{10,11... | collective-permute-start | bytes 3145736 | tf_op jit(solution)/shard_map/descriptors_gather/ppermute | solution.py:134
  71.0 1.9 %collective-permute-start.3 = (bf16[256,512]{1,0:T(8,128)(2,1)S(1)}, bf16[256,512]{1,0:T(8,128)(2,1)S(1)}, u32[]{:S(2)}, u32[]{:S(2)}) collective-permute-start(bf16[256,512]{1,0:T(8,128)(2,1)S(1)} %bitcast.35), channel_id=1, source_target_pairs={{0,448},{64,0},{128,64},{192,128},{256,192},{320,256},{384,320},{4... | collective-permute-start | bytes 786440 | tf_op jit(solution)/shard_map/points_ring/ppermute | solution.py:123
  73.0 0.1 broadcast_in_dim.76
  73.1 0.1 reshape.106
  73.2 0.6 fusion.5
  73.8 13.6 %collective-permute-done.3.rest_2_ = bf16[256,512]{1,0:T(8,128)(2,1)S(1)} collective-permute-done((bf16[256,512]{1,0:T(8,128)(2,1)S(1)}, bf16[256,512]{1,0:T(8,128)(2,1)S(1)}, u32[]{:S(2)}, u32[]{:S(2)}) %collective-permute-start.3) | collective-permute-done | bytes 262176 | tf_op jit(solution)/shard_map/points_ring/ppermute | solution.py:123
  87.4 1.9 collective-permute-start.4
  89.3 4.3 %collective-permute-start.5 = (bf16[256,512]{1,0:T(8,128)(2,1)S(1)}, bf16[256,512]{1,0:T(8,128)(2,1)}, u32[]{:S(2)}, u32[]{:S(2)}) collective-permute-start(bf16[256,512]{1,0:T(8,128)(2,1)S(1)} %collective-permute-done.1.rest_3_), channel_id=1, source_target_pairs={{0,64},{64,128},{128,192},{192,256},{256,320},{320,384},{384,448},... | collective-permute-start | bytes 786440 | tf_op jit(solution)/shard_map/points_ring/ppermute | solution.py:119
  93.6 0.6 pad_add_fusion
  94.2 0.1 copy.26
  94.3 0.1 eq.97
  94.4 0.8 copy.27
  95.3 0.0 copy-done
  95.3 0.0 copy-start.12
  95.3 1.2 reshape.107
  96.5 0.8 dynamic_slice.3
  97.3 0.1 stack.48.place_ref
  97.4 1.2 fusion.2.table_ref
  98.6 3.6 %collective-permute-done.4.rest_4_ = bf16[256,512]{1,0:T(8,128)(2,1)} collective-permute-done((bf16[256,512]{1,0:T(8,128)(2,1)S(1)}, bf16[256,512]{1,0:T(8,128)(2,1)}, u32[]{:S(2)}, u32[]{:S(2)}) %collective-permute-start.4) | collective-permute-done | bytes 262176 | tf_op jit(solution)/shard_map/points_ring/ppermute | solution.py:123
  102.2 1.9 collective-permute-start.6
  104.1 0.0 collective-permute-done.5.rest_5_
  104.1 4.3 %collective-permute-start.7 = (bf16[256,512]{1,0:T(8,128)(2,1)}, bf16[256,512]{1,0:T(8,128)(2,1)}, u32[]{:S(2)}, u32[]{:S(2)}) collective-permute-start(bf16[256,512]{1,0:T(8,128)(2,1)} %collective-permute-done.5.rest_5_), channel_id=1, source_target_pairs={{0,64},{64,128},{128,192},{192,256},{256,320},{320,384},{384,448},... | collective-permute-start | bytes 786440 | tf_op jit(solution)/shard_map/points_ring/ppermute | solution.py:119
  108.4 0.0 collective-permute-done.2
  108.4 1.7 broadcast_select_fusion.1
  110.1 0.5 fusion
  110.6 0.3 convert_bitcast_fusion
  110.9 5.2 %copy.25 = f32[4,128,8,2,128]{4,3,2,1,0:T(2,128)} copy(f32[4,128,8,2,128]{4,1,2,0,3:T(8,128)S(1)} %convert_bitcast_fusion) | data formatting | bytes 8388608 | tf_op jit(solution)/shard_map/descriptors_gather/convert_element_type | solution.py:138
  116.1 6.5 %reshape.110 = f32[512,2048]{1,0:T(8,128)} reshape(f32[4,128,8,2,128]{4,3,2,1,0:T(2,128)} %copy.25) | data formatting | bytes 8388608 | tf_op jit(solution)/shard_map/descriptors_gather/convert_element_type | solution.py:138
  122.6 2.8 %divide_convert_fusion.unit_ref = bf16[512,2048]{1,0:T(8,128)(2,1)S(1)} fusion(f32[512,2048]{1,0:T(8,128)} %reshape.110, f32[512]{0:T(512)S(1)} %get-tuple-element.26), kind=kLoop, calls=%fused_computation.3 | loop fusion | flops 2097152 | bytes 6293504 | tf_op jit(solution)/shard_map/descriptors_gather/convert_element_type | solution.py:140
  125.4 0.9 copy.28.scale_ref
  126.2 0.0 collective-permute-done.6.rest_6_
  126.2 0.0 collective-permute-done.7.rest_7_
  126.2 0.9 copy-done.1
  127.2 0.9 copy-done.2
  128.2 0.9 copy-done.4
  129.1 0.9 copy-done.6
  130.1 0.9 copy-done.8
  131.0 7.3 %main.1 = (f32[4,8,128,128]{3,2,1,0:T(8,128)S(1)}, f32[4,8,128,128]{3,2,1,0:T(8,128)S(1)}, f32[4,8,128]{2,1,0:T(8,128)S(1)}) custom-call(s32[9]{0:T(128)S(1)} %stack.48.place_ref, bf16[512,2048]{1,0:T(8,128)(2,1)S(1)} %divide_convert_fusion.unit_ref, f32[512,1]{1,0:T(8,128)S(1)} %copy-done.2, f32[1,512]{1,0:T(1,128)S(1)} %bitcast.37, ...), custom_call_target="tpu_custom_call" | custom-call | flops 2147483648 | bytes 8388608 | tf_op jit(solution)/shard_map/main/pallas_call | solution.py:170
  138.3 3.4 %collective-permute-start.8 = (f32[4,8,128,128]{3,2,1,0:T(8,128)S(1)}, f32[4,8,128,128]{3,2,1,0:T(8,128)S(1)}, u32[]{:S(2)}, u32[]{:S(2)}) collective-permute-start(f32[4,8,128,128]{3,2,1,0:T(8,128)S(1)} %get-tuple-element.16), channel_id=1, source_target_pairs={{0,1},{1,0},{2,3},{3,2},{4,5},{5,4},{6,7},{7,6},{8,9},{9,8},{10,11... | collective-permute-start | bytes 6291464 | tf_op jit(solution)/shard_map/core_pair/ppermute | solution.py:188
  141.7 3.8 %collective-permute-done.8 = f32[4,8,128,128]{3,2,1,0:T(8,128)S(1)} collective-permute-done((f32[4,8,128,128]{3,2,1,0:T(8,128)S(1)}, f32[4,8,128,128]{3,2,1,0:T(8,128)S(1)}, u32[]{:S(2)}, u32[]{:S(2)}) %collective-permute-start.8) | collective-permute-done | bytes 2097184 | tf_op jit(solution)/shard_map/core_pair/ppermute | solution.py:188
  145.5 1.3 add_convert_fusion
  146.8 4.4 %all-to-all-start.2 = ((bf16[32,128,128]{2,1,0:T(8,128)(2,1)}), bf16[32,128,128]{2,1,0:T(8,128)(2,1)S(1)}, u32[]{:S(2)}, u32[]{:S(2)}) async-start(bf16[32,128,128]{2,1,0:T(8,128)(2,1)} %bitcast.19), calls=%async_computation.2 | async-start | bytes 2097152 | tf_op jit(solution)/shard_map/gradient_exchange/all_to_all | solution.py:191
  151.2 1.6 copy.29.deriv_ref
  152.8 14.8 %all-to-all-done.2.parts_ref = bf16[32,128,128]{2,1,0:T(8,128)(2,1)S(1)} async-done(((bf16[32,128,128]{2,1,0:T(8,128)(2,1)}), bf16[32,128,128]{2,1,0:T(8,128)(2,1)S(1)}, u32[]{:S(2)}, u32[]{:S(2)}) %all-to-all-start.2) | async-done | bytes 1048608 | tf_op jit(solution)/shard_map/gradient_exchange/all_to_all | solution.py:191
  167.6 1.1 tail.1
  168.7 5.4 %collective-permute-start.9 = (f32[3,128]{1,0:T(4,128)S(1)}, f32[3,128]{1,0:T(4,128)S(1)}, u32[]{:S(2)}, u32[]{:S(2)}) collective-permute-start(f32[3,128]{1,0:T(4,128)S(1)} %get-tuple-element.23), channel_id=1, source_target_pairs={{0,496},{64,48},{128,112},{192,176},{256,240},{320,304},{384,368},... | collective-permute-start | bytes 4616 | tf_op jit(solution)/shard_map/ghosts/ppermute | solution.py:209
  174.1 1.0 collective-permute-done.9
  175.1 0.1 select_select_fusion
  175.3 15.9 %all_to_all.21 = f32[64,4,128]{2,1,0:T(4,128)S(1)} all-to-all(f32[64,4,128]{2,1,0:T(4,128)S(1)} %bitcast.44), channel_id=1, replica_groups=mesh['zh'=8,'zl'=2,'yl'=2,'x'=4,'yh'=2,'c'=2] {'zl','yl','x','yh','c'}, dimensions={0} | all-to-all | bytes 262144 | tf_op jit(solution)/shard_map/ghosts/all_to_all | solution.py:216
  191.2 0.1 reduce_sum.19
  191.2 0.5 slice_bitcast_fusion
  191.8 0.1 copy-done.11
  (32 shorter events, 0.1 us)
Async XLA Ops:
  0.6 70.4 %copy-start.14 = (s32[256]{0:T(256)S(1)}, s32[256]{0:T(256)}, u32[]{:S(2)}) copy-start(s32[256]{0:T(256)} %param.13) | copy-start | bytes 3076
  0.6 72.3 %copy-start.15 = (s32[128]{0:T(128)S(1)}, s32[128]{0:T(128)}, u32[]{:S(2)}) copy-start(s32[128]{0:T(128)} %param.12) | copy-start | bytes 1540
  1.6 92.6 %copy-start.10 = (s32[128,12]{0,1:T(8,128)S(1)}, s32[128,12]{0,1:T(8,128)}, u32[]{:S(2)}) copy-start(s32[128,12]{0,1:T(8,128)} %param.11) | copy-start | bytes 18436
  1.6 92.8 %copy-start.9 = (bf16[128,3,12,128]{3,0,2,1:T(8,128)(2,1)S(1)}, bf16[128,3,12,128]{3,0,2,1:T(8,128)(2,1)}, u32[]{:S(2)}) copy-start(bf16[128,3,12,128]{3,0,2,1:T(8,128)(2,1)} %param.10) | copy-start | bytes 3538948
  10.9 84.4 %copy-start = (bf16[4,64,512]{2,1,0:T(8,128)(2,1)}, bf16[4,64,512]{2,1,0:T(8,128)(2,1)S(1)}, u32[]{:S(2)}) copy-start(bf16[4,64,512]{2,1,0:T(8,128)(2,1)S(1)} %all_to_all.20) | copy-start | bytes 786436
  12.9 52.3 %all-to-all-start.1 = ((bf16[32,128,128]{2,1,0:T(8,128)(2,1)}), bf16[32,128,128]{2,1,0:T(8,128)(2,1)}, u32[]{:S(2)}, u32[]{:S(2)}) async-start(bf16[32,128,128]{2,1,0:T(8,128)(2,1)} %broadcast_in_dim.75), calls=%async_computation.1 | async-start | bytes 2097152 | tf_op jit(solution)/shard_map/descriptors_gather/all_to_all | solution.py:132
  20.4 35.6 %collective-permute-start = (bf16[256,512]{1,0:T(8,128)(2,1)S(1)}, bf16[256,512]{1,0:T(8,128)(2,1)S(1)}, u32[]{:S(2)}, u32[]{:S(2)}) collective-permute-start(bf16[256,512]{1,0:T(8,128)(2,1)S(1)} %bitcast.34), channel_id=1, source_target_pairs={{0,64},{64,128},{128,192},{192,256},{256,320},{320,384},{384,448},... | collective-permute-start | bytes 786440 | tf_op jit(solution)/shard_map/points_ring/ppermute | solution.py:119
  56.0 9.2 %collective-permute-start.1 = (bf16[256,512]{1,0:T(8,128)(2,1)S(1)}, bf16[256,512]{1,0:T(8,128)(2,1)S(1)}, u32[]{:S(2)}, u32[]{:S(2)}) collective-permute-start(bf16[256,512]{1,0:T(8,128)(2,1)S(1)} %collective-permute-done.rest_1_), channel_id=1, source_target_pairs={{0,64},{64,128},{128,192},{192,256},{256,320},{320,384},{384,448},... | collective-permute-start | bytes 786440 | tf_op jit(solution)/shard_map/points_ring/ppermute | solution.py:119
  57.9 0.7 copy-start.3
  65.2 31.3 %copy-start.5 = (bf16[256,512]{1,0:T(8,128)(2,1)}, bf16[256,512]{1,0:T(8,128)(2,1)S(1)}, u32[]{:S(2)}) copy-start(bf16[256,512]{1,0:T(8,128)(2,1)S(1)} %collective-permute-done.1.rest_3_) | copy-start | bytes 786436
  65.2 43.2 %collective-permute-start.2 = (bf16[32,128,128]{2,1,0:T(8,128)(2,1)}, bf16[32,128,128]{2,1,0:T(8,128)(2,1)}, u32[]{:S(2)}, u32[]{:S(2)}) collective-permute-start(bf16[32,128,128]{2,1,0:T(8,128)(2,1)} %all-to-all-done.1), channel_id=1, source_target_pairs={{0,1},{1,0},{2,3},{3,2},{4,5},{5,4},{6,7},{7,6},{8,9},{9,8},{10,11... | collective-permute-start | bytes 3145736 | tf_op jit(solution)/shard_map/descriptors_gather/ppermute | solution.py:134
  71.0 16.4 %collective-permute-start.3 = (bf16[256,512]{1,0:T(8,128)(2,1)S(1)}, bf16[256,512]{1,0:T(8,128)(2,1)S(1)}, u32[]{:S(2)}, u32[]{:S(2)}) collective-permute-start(bf16[256,512]{1,0:T(8,128)(2,1)S(1)} %bitcast.35), channel_id=1, source_target_pairs={{0,448},{64,0},{128,64},{192,128},{256,192},{320,256},{384,320},{4... | collective-permute-start | bytes 786440 | tf_op jit(solution)/shard_map/points_ring/ppermute | solution.py:123
  87.4 9.1 %copy-start.7 = (bf16[256,512]{1,0:T(8,128)(2,1)}, bf16[256,512]{1,0:T(8,128)(2,1)S(1)}, u32[]{:S(2)}) copy-start(bf16[256,512]{1,0:T(8,128)(2,1)S(1)} %collective-permute-done.3.rest_2_) | copy-start | bytes 786436
  87.4 14.8 %collective-permute-start.4 = (bf16[256,512]{1,0:T(8,128)(2,1)S(1)}, bf16[256,512]{1,0:T(8,128)(2,1)}, u32[]{:S(2)}, u32[]{:S(2)}) collective-permute-start(bf16[256,512]{1,0:T(8,128)(2,1)S(1)} %collective-permute-done.3.rest_2_), channel_id=1, source_target_pairs={{0,448},{64,0},{128,64},{192,128},{256,192},{320,256},{384,320},{4... | collective-permute-start | bytes 786440 | tf_op jit(solution)/shard_map/points_ring/ppermute | solution.py:123
  89.3 14.8 %collective-permute-start.5 = (bf16[256,512]{1,0:T(8,128)(2,1)S(1)}, bf16[256,512]{1,0:T(8,128)(2,1)}, u32[]{:S(2)}, u32[]{:S(2)}) collective-permute-start(bf16[256,512]{1,0:T(8,128)(2,1)S(1)} %collective-permute-done.1.rest_3_), channel_id=1, source_target_pairs={{0,64},{64,128},{128,192},{192,256},{256,320},{320,384},{384,448},... | collective-permute-start | bytes 786440 | tf_op jit(solution)/shard_map/points_ring/ppermute | solution.py:119
  95.3 2.1 %copy-start.12 = (pred[1536]{0:T(1024)(128)(4,1)S(1)}, pred[1536]{0:T(1024)(128)(4,1)}, u32[]{:S(2)}) copy-start(pred[1536]{0:T(1024)(128)(4,1)} %fusion.5) | copy-start | bytes 4612
  95.3 2.1 %copy-start.13 = (s32[384]{0:T(512)S(1)}, s32[384]{0:T(512)}, u32[]{:S(2)}) copy-start(s32[384]{0:T(512)} %pad_add_fusion) | copy-start | bytes 4612
  102.2 24.0 %collective-permute-start.6 = (bf16[256,512]{1,0:T(8,128)(2,1)}, bf16[256,512]{1,0:T(8,128)(2,1)}, u32[]{:S(2)}, u32[]{:S(2)}) collective-permute-start(bf16[256,512]{1,0:T(8,128)(2,1)} %collective-permute-done.4.rest_4_), channel_id=1, source_target_pairs={{0,448},{64,0},{128,64},{192,128},{256,192},{320,256},{384,320},{4... | collective-permute-start | bytes 786440 | tf_op jit(solution)/shard_map/points_ring/ppermute | solution.py:123
  104.1 22.1 %collective-permute-start.7 = (bf16[256,512]{1,0:T(8,128)(2,1)}, bf16[256,512]{1,0:T(8,128)(2,1)}, u32[]{:S(2)}, u32[]{:S(2)}) collective-permute-start(bf16[256,512]{1,0:T(8,128)(2,1)} %collective-permute-done.5.rest_5_), channel_id=1, source_target_pairs={{0,64},{64,128},{128,192},{192,256},{256,320},{320,384},{384,448},... | collective-permute-start | bytes 786440 | tf_op jit(solution)/shard_map/points_ring/ppermute | solution.py:119
  126.2 1.0 copy-start.1
  127.2 0.9 copy-start.2
  128.1 0.9 copy-start.4
  129.1 0.9 copy-start.6
  130.0 0.9 copy-start.8
  138.3 7.2 %collective-permute-start.8 = (f32[4,8,128,128]{3,2,1,0:T(8,128)S(1)}, f32[4,8,128,128]{3,2,1,0:T(8,128)S(1)}, u32[]{:S(2)}, u32[]{:S(2)}) collective-permute-start(f32[4,8,128,128]{3,2,1,0:T(8,128)S(1)} %get-tuple-element.16), channel_id=1, source_target_pairs={{0,1},{1,0},{2,3},{3,2},{4,5},{5,4},{6,7},{7,6},{8,9},{9,8},{10,11... | collective-permute-start | bytes 6291464 | tf_op jit(solution)/shard_map/core_pair/ppermute | solution.py:188
  146.8 20.8 %all-to-all-start.2 = ((bf16[32,128,128]{2,1,0:T(8,128)(2,1)}), bf16[32,128,128]{2,1,0:T(8,128)(2,1)S(1)}, u32[]{:S(2)}, u32[]{:S(2)}) async-start(bf16[32,128,128]{2,1,0:T(8,128)(2,1)} %bitcast.19), calls=%async_computation.2 | async-start | bytes 2097152 | tf_op jit(solution)/shard_map/gradient_exchange/all_to_all | solution.py:191
  168.7 6.4 %collective-permute-start.9 = (f32[3,128]{1,0:T(4,128)S(1)}, f32[3,128]{1,0:T(4,128)S(1)}, u32[]{:S(2)}, u32[]{:S(2)}) collective-permute-start(f32[3,128]{1,0:T(4,128)S(1)} %get-tuple-element.23), channel_id=1, source_target_pairs={{0,496},{64,48},{128,112},{192,176},{256,240},{320,304},{384,368},... | collective-permute-start | bytes 4616 | tf_op jit(solution)/shard_map/ghosts/ppermute | solution.py:209
  191.2 0.6 copy-start.11

commit v4 on v2

v4 whole, which is shorter than its diff:
```python
import jax
import jax.numpy as jnp
from jax import lax
from jax.experimental import pallas as pl
from jax.experimental.pallas import tpu as pltpu
from jax.sharding import Mesh, PartitionSpec as P

DOM = ("z", "yl")
SP = ("x", "yh", "c")
PLANE = ("yl", "x", "yh", "c")
LIFT = 4096.0
F32, BF16, F16 = jnp.float32, jnp.bfloat16, jnp.float16
LAST = (((1,), (1,)), ((), ()))


def spread_kernel(rows_ref, out_hbm, sems):
    copies = [
        pltpu.make_async_copy(rows_ref, out_hbm.at[i], sems.at[i]) for i in range(out_hbm.shape[0])
    ]
    for copy in copies:
        copy.start()
    for copy in copies:
        copy.wait()


def prepare_kernel(side_ref, rows_ref, unit_ref, scale_ref):
    domains = 2
    blocks = rows_ref.shape[0] // domains
    owned, width = rows_ref.shape[1:]
    shift = side_ref[0] * (width // 2)
    for y in range(domains):
        total = jnp.zeros((owned, width), F32)
        for s in range(blocks):
            value = rows_ref[y * blocks + s].astype(F32)
            total += value * value
        norm = jnp.sqrt(jnp.sum(total, axis=1, keepdims=True) + 1e-06)
        scale = jnp.broadcast_to(1.0 / norm, (owned, width))
        scale_ref[y * owned : (y + 1) * owned, :] = scale
        for s in range(blocks):
            value = rows_ref[y * blocks + s].astype(F32) * scale
            unit_ref[y * owned : (y + 1) * owned, s * width : (s + 1) * width] = pltpu.roll(
                value, shift, 1
            ).astype(BF16)


def main_kernel(unit, scale_ref, coef_ref, basis, share_ref, energy_ref, kernel, slopes, inner):
    columns = basis.shape[0]
    width = scale_ref.shape[1]
    atoms = unit.shape[0]
    domains = energy_ref.shape[0]
    owned = atoms // domains
    blocks = columns // width
    kernel[...] = jnp.dot(unit[...], basis[...], preferred_element_type=F32)
    four = 4.0 * coef_ref[...]
    rows = 32
    for r in range(0, atoms, rows):
        k = kernel[r : r + rows, :]
        s = four * (k * k * k)
        low = s.astype(BF16)
        slopes[r : r + rows, :] = low
        inner[r : r + rows, :] = scale_ref[r : r + rows, :] * jnp.sum(
            low.astype(F32) * k, axis=1, keepdims=True
        )
        kernel[r : r + rows, 0:128] = jnp.broadcast_to(
            0.25 * jnp.sum(s * k, axis=1, keepdims=True), (rows, 128)
        )
    for y in range(domains):
        energy_ref[y] = kernel[y * owned : (y + 1) * owned, 0:128].T[0:8, :]
    for i in range(0, blocks, 2):
        g = lax.dot_general(
            slopes[...],
            basis[i * width : (i + 2) * width, :],
            LAST,
            preferred_element_type=F32,
        )
        for p in range(2):
            lanes = slice((i + p) * width, (i + p + 1) * width)
            part = (
                g[:, p * width : (p + 1) * width] * scale_ref[...]
                - unit[:, lanes].astype(F32) * inner[...]
            ).astype(BF16)
            for y in range(domains):
                share_ref[y * blocks + i + p] = part[y * owned : (y + 1) * owned]


def tail_kernel(parts_ref, deriv_ref, table_ref, out_ref):
    count, atoms, width = parts_ref.shape
    sides = []
    for y in range(2):
        total = parts_ref[y * (count // 2)].astype(F32)
        for i in range(1, count // 2):
            total += parts_ref[y * (count // 2) + i].astype(F32)
        sides.append(total)
    total = sides[0] + pltpu.roll(sides[1], width // 2, 1)
    pairs = deriv_ref.shape[1]
    high = total.astype(BF16)
    low = (total - high.astype(F32)).astype(BF16)
    both = jnp.concatenate([high, low], axis=0)
    row = lax.broadcasted_iota(jnp.int32, (atoms, pairs), 0)
    lane = lax.broadcasted_iota(jnp.int32, (atoms, pairs), 1)
    diagonal = row == lane % atoms
    rows = []
    for c in range(3):
        f = lax.dot_general(both, deriv_ref[c], LAST, preferred_element_type=F32)
        f = jnp.where(diagonal, f[:atoms] + f[atoms:], 0.0)
        rows.append(jnp.sum(f, axis=0, keepdims=True))
    partial = jnp.concatenate(rows + [jnp.zeros((5, pairs), F32)], axis=0)
    first = partial.astype(BF16)
    rest = partial - first.astype(F32)
    second = rest.astype(BF16)
    third = (rest - second.astype(F32)).astype(BF16)
    pieces = jnp.concatenate([first.astype(F32), second.astype(F32), third.astype(F32)], axis=0)
    moved = jnp.dot(pieces.astype(BF16), table_ref[...], preferred_element_type=F32)
    out_ref[...] = moved[0:8] + moved[8:16] + moved[16:24]


def body(descriptors, sparse_points, coefficients, derivatives, neighbours, counts, ghost_index):
    yl = lax.axis_index("yl")
    first = yl == 0
    owned, width = descriptors.shape
    points, part = sparse_points.shape
    n_sp, n_plane = lax.axis_size(SP), lax.axis_size(PLANE)
    columns = n_sp * width
    half = points // 2
    atoms = 2 * owned
    slots_count = neighbours.shape[1]
    pairs_count = owned * slots_count
    ghosts = ghost_index.shape[0] // 2
    swap = [(0, 1), (1, 0)]
    vmem = pl.BlockSpec(memory_space=pltpu.VMEM)
    smem = pl.BlockSpec(memory_space=pltpu.SMEM)
    anywhere = pl.BlockSpec(memory_space=pl.ANY)

    with jax.named_scope("points_swap"):
        turned = sparse_points.T
        kept = lax.dynamic_slice_in_dim(turned, yl * half, half, 1).astype(F32) * LIFT
        sent = lax.dynamic_slice_in_dim(turned, (1 - yl) * half, half, 1).astype(F32) * LIFT
        got = lax.ppermute(sent.astype(F16), "yl", swap)
        block = jnp.concatenate([kept.astype(F16), got], axis=0)
    with jax.named_scope("points_gather"):
        lifted = lax.all_gather(block, "z", axis=0, tiled=True)
        basis = (lifted.astype(F32) * (1.0 / LIFT)).astype(BF16)

    with jax.named_scope("descriptors_gather"):
        spread = pl.pallas_call(
            spread_kernel,
            out_shape=jax.ShapeDtypeStruct((n_plane, owned, width), BF16),
            in_specs=[vmem],
            out_specs=anywhere,
            scratch_shapes=[pltpu.SemaphoreType.DMA((n_plane,))],
            compiler_params=pltpu.CompilerParams(vmem_limit_bytes=4 << 20),
        )(descriptors)
        spread, block = lax.optimization_barrier((spread, block))
        rows = lax.all_to_all(spread, PLANE, 0, 0)
        unit_rows, scale = pl.pallas_call(
            prepare_kernel,
            out_shape=(
                jax.ShapeDtypeStruct((atoms, columns), BF16),
                jax.ShapeDtypeStruct((atoms, width), F32),
            ),
            in_specs=[smem, vmem],
            out_specs=(vmem, vmem),
            compiler_params=pltpu.CompilerParams(vmem_limit_bytes=16 << 20),
            cost_estimate=pl.CostEstimate(
                flops=8 * atoms * columns, bytes_accessed=4 << 20, transcendentals=0
            ),
        )(yl.reshape(1).astype(jnp.int32), rows)

    with jax.named_scope("scatter_table"):
        slot_total = owned + 2 * ghosts
        flat = neighbours.T.reshape(pairs_count)
        slot_ids = jnp.arange(slot_total, dtype=jnp.int32)
        hot = (flat[:, None] == slot_ids[None, :]).astype(BF16)
        target = jnp.concatenate(
            [
                jnp.arange(owned, dtype=jnp.int32),
                ghost_index[:ghosts] + owned,
                ghost_index[ghosts:] + 2 * owned,
            ]
        )
        column_ids = jnp.arange(3 * owned, dtype=jnp.int32)
        moves = (target[:, None] == column_ids[None, :]).astype(BF16)
        landed = jnp.dot(hot, moves, preferred_element_type=F32)
        atom_of = jnp.arange(pairs_count, dtype=jnp.int32) % owned
        slot_of = jnp.arange(pairs_count, dtype=jnp.int32) // owned
        self_hot = (atom_of[:, None] == column_ids[None, :]).astype(F32)
        live = slot_of < jnp.tile(counts, slots_count)
        table = jnp.where(live[:, None], self_hot - landed, 0.0).astype(BF16)
        lined = jnp.transpose(derivatives, (1, 2, 0, 3)).reshape(3, pairs_count, width)

    unit_rows, scale, table = lax.optimization_barrier((unit_rows, scale, table))
    with jax.named_scope("main"):
        coefs = lax.dynamic_slice_in_dim(coefficients, yl * half, half, 0)[None, :]
        outgoing, energy_part = pl.pallas_call(
            main_kernel,
            out_shape=(
                jax.ShapeDtypeStruct((n_plane, owned, width), BF16),
                jax.ShapeDtypeStruct((2, 8, owned), F32),
            ),
            in_specs=[vmem] * 4,
            out_specs=(vmem, vmem),
            scratch_shapes=[
                pltpu.VMEM((atoms, half), F32),
                pltpu.VMEM((atoms, half), BF16),
                pltpu.VMEM((atoms, width), F32),
            ],
            compiler_params=pltpu.CompilerParams(vmem_limit_bytes=24 << 20),
            cost_estimate=pl.CostEstimate(
                flops=4 * atoms * half * columns, bytes_accessed=8 << 20, transcendentals=0
            ),
        )(unit_rows, scale, coefs, basis)
    with jax.named_scope("gradient_exchange"):
        parts = lax.all_to_all(outgoing, PLANE, 0, 0)
    with jax.named_scope("tail"):
        moved = pl.pallas_call(
            tail_kernel,
            out_shape=jax.ShapeDtypeStruct((8, 3 * owned), F32),
            in_specs=[vmem, vmem, vmem],
            out_specs=vmem,
            compiler_params=pltpu.CompilerParams(vmem_limit_bytes=24 << 20),
            cost_estimate=pl.CostEstimate(
                flops=12 * owned * width * pairs_count, bytes_accessed=4 << 20, transcendentals=0
            ),
        )(parts, lined, table)
        keep, to_left, to_right = jnp.split(moved[:3], 3, axis=1)
    with jax.named_scope("ghosts"):
        across = jnp.where(first, to_left, to_right)
        beside = jnp.where(first, to_right, to_left)
        size = lax.axis_size(DOM)
        pairs = [(i, (i - 1) % size if i % 2 == 0 else (i + 1) % size) for i in range(size)]
        keep = keep + lax.ppermute(across, DOM, pairs)
        both = jnp.stack([jnp.where(first, keep, beside), jnp.where(first, beside, keep)])
        both = jnp.concatenate([both, energy_part[:, :1]], axis=1)
        both = jnp.broadcast_to(both[:, None], (2, n_sp, 4, owned)).reshape(n_plane, 4, owned)
        received = jnp.sum(lax.all_to_all(both, PLANE, 0, 0), axis=0)
    return (received[:3], received[3])


def solution(mesh):
    grid = Mesh(mesh.devices.reshape(16, 2, 4, 2, 2), ("z", "yl", "x", "yh", "c"))
    return jax.shard_map(
        body,
        mesh=grid,
        in_specs=(
            P(DOM, SP),
            P(SP, DOM),
            P(SP),
            P(DOM, None, None, SP),
            P(DOM, None),
            P(DOM),
            P(DOM),
        ),
        out_specs=(P(None, DOM), P(DOM)),
        check_vma=False,
    )
```

time: 162 us -> 141 us (0.87)
  blocking collectives: 14 us -> 72.2 us
  waiting for transfers between devices: 71 us -> 21.7 us
  between operations: 14.3 us -> 0.78 us
  starting transfers between devices: 37 us -> 27.9 us
  local copies, waits for them, and re-layouts: 11.4 us -> 5.18 us
  Pallas kernels: 7.18 us -> 5.4 us
    all_gather x0 -> x1, blocking collectives: none -> 60.1 us  [body(): lifted = lax.all_gather(block, 'z', axis=0, tiled=True)]
    all_gather x1 -> x0, waiting for transfers between devices: 43.4 us -> none  [body(): basis = lax.all_gather(swapped, 'z', axis=0, tiled=True)]
    ppermute x2 -> x1, starting transfers between devices: 15.1 us -> 4.03 us  [body(): got = lax.ppermute(sent.astype(F16), 'yl', swap)]
    ppermute x2 -> x1, waiting for transfers between devices: 4.57 us -> 0.01 us  [body(): got = lax.ppermute(sent.astype(F16), 'yl', swap)]
    all_to_all x2, starting transfers between devices: 17.6 us -> 21.9 us  [the longest x1 13.6 us: body(): parts = lax.all_to_all(outgoing, PLANE, 0, 0)]
    all_to_all x2, waiting for transfers between devices: 20.9 us -> 17.2 us  [the longest x1 17.1 us: body(): parts = lax.all_to_all(outgoing, PLANE, 0, 0)]
    reshape x3 -> x0, local copies, waits for them, and re-layouts: 3.01 us -> none  [the longest x2 2.9 us: body(): jnp.transpose(derivatives, (1, 3, 0, 2)).reshape(3, width, pairs_count)]
    ppermute x1, waiting for transfers between devices: 2.09 us -> 4.5 us  [body(): keep = keep + lax.ppermute(across, DOM, pairs)]
  transfers between devices with their start and end apart: 6 -> 4, of which waited for: 6 -> 2; matrix products, arithmetic and copies ran while one was open for 7% -> 5% of each run, Pallas kernels for 0% -> 1%
where the time goes in v4:
time: 141 us
  blocking collectives  72.2 us (51%)
  starting transfers between devices  27.9 us (20%)
  waiting for transfers between devices  21.7 us (15%)
  other arithmetic  5.83 us (4%)
  Pallas kernels  5.4 us (4%)
  local copies, waits for them, and re-layouts  5.18 us (4%)
  matrix products  1.88 us (1%)
    all_gather x1, blocking collectives, body(): lifted = lax.all_gather(block, 'z', axis=0, tiled=True)  60.1 us
    all_to_all x1, waiting for transfers between devices, body(): parts = lax.all_to_all(outgoing, PLANE, 0, 0)  17.1 us
    all_to_all x1, starting transfers between devices, body(): parts = lax.all_to_all(outgoing, PLANE, 0, 0)  13.6 us
    all_to_all x1, blocking collectives, body(): received = jnp.sum(lax.all_to_all(both, PLANE, 0, 0), axis=0)  12.1 us
    all_to_all x1, starting transfers between devices, body(): rows = lax.all_to_all(spread, PLANE, 0, 0)  8.36 us
    ppermute x1, waiting for transfers between devices, body(): keep = keep + lax.ppermute(across, DOM, pairs)  4.5 us
    ppermute x1, starting transfers between devices, body(): got = lax.ppermute(sent.astype(F16), 'yl', swap)  4.03 us
    unnamed x10, local copies, waits for them, and re-layouts  3.96 us
  transfers between devices with their start and end apart: 4, of which 2 were waited for; matrix products, arithmetic and copies ran while one was open for 5% of the time, Pallas kernels for 1%

profile of v4, /device:TPU:1, one launch (start us, length us, event | category | flops | bytes accessed | tf_op | source)
XLA Modules:
  0.0 140.8 jit_solution(630047364433862819)
XLA Ops:
  0.6 1.0 fusion.4
  1.7 4.0 %collective-permute-start = (f16[64,1024]{1,0:T(8,128)(2,1)S(1)}, f16[64,1024]{1,0:T(8,128)(2,1)S(1)}, u32[]{:S(2)}, u32[]{:S(2)}) collective-permute-start(f16[64,1024]{1,0:T(8,128)(2,1)S(1)} %get-tuple-element.19), channel_id=1, source_target_pairs={{0,16},{16,0},{1,17},{17,1},{2,18},{18,2},{3,19},{19,3},{4,20},{20... | collective-permute-start | bytes 393224 | tf_op jit(solution)/shard_map/points_swap/ppermute | solution.py:138
  5.7 0.0 copy-start.3
  5.7 0.7 copy-done.3
  6.5 1.2 descriptors_gather.2
  7.7 0.8 slice_add_fusion.2
  8.5 0.7 fusion.12
  9.2 0.7 dynamic_slice.11
  9.9 1.9 %fusion.1.table_ref = bf16[1536,384]{1,0:T(8,128)(2,1)S(1)} fusion(s32[1536]{0:T(1024)} %bitcast.26, s32[1536]{0:T(1024)S(1)} %fusion.6, pred[1536]{0:T(1024)(128)(4,1)S(1)} %fusion.12, s32[384]{0:T(512)S(1)} %pad_add_fusion), kind=kOutput, calls=%fused_computation.3 | convolution fusion | flops 456671232 | bytes 1195008 | tf_op jit(solution)/shard_map/scatter_table/dot_general | solution.py:183
  11.8 0.0 collective-permute-done
  11.8 0.1 pad_maximum_fusion
  11.8 8.4 %all-to-all-start = ((bf16[32,128,128]{2,1,0:T(8,128)(2,1)}), bf16[32,128,128]{2,1,0:T(8,128)(2,1)S(1)}, u32[]{:S(2)}, u32[]{:S(2)}) async-start(bf16[32,128,128]{2,1,0:T(8,128)(2,1)} %descriptors_gather.2), calls=%async_computation | async-start | bytes 2097152 | tf_op jit(solution)/shard_map/descriptors_gather/all_to_all | solution.py:154
  20.2 60.1 %all-gather.1 = f16[2048,1024]{1,0:T(8,128)(2,1)S(1)} all-gather(f16[128,1024]{1,0:T(8,128)(2,1)S(1)} %pad_maximum_fusion), channel_id=1, replica_groups=mesh['z'=16,'yl'=2,'x'=4,'yh'=2,'c'=2] {'z'}, dimensions={0}, use_global_device_ids=true | all-gather | bytes 4456448 | tf_op jit(solution)/shard_map/points_gather/all_gather | solution.py:141
  80.3 3.2 %multiply_convert_fusion.basis = bf16[2048,1024]{1,0:T(8,128)(2,1)} fusion(f16[2048,1024]{1,0:T(8,128)(2,1)S(1)} %all-gather.1), kind=kLoop, calls=%fused_computation | loop fusion | flops 6291456 | bytes 8388608 | tf_op jit(solution)/shard_map/points_gather/convert_element_type | solution.py:142
  83.5 0.0 all-to-all-done.rows_ref
  83.5 0.6 descriptors_gather.3
  84.2 0.0 copy-start
  84.2 2.2 %copy-done = bf16[2048,1024]{1,0:T(8,128)(2,1)S(1)} copy-done((bf16[2048,1024]{1,0:T(8,128)(2,1)S(1)}, bf16[2048,1024]{1,0:T(8,128)(2,1)}, u32[]{:S(2)}) %copy-start) | copy-done | bytes 4194328
  86.4 2.5 %main.1 = (bf16[32,128,128]{2,1,0:T(8,128)(2,1)S(1)}, f32[2,8,128]{2,1,0:T(8,128)S(1)}) custom-call(bf16[256,2048]{1,0:T(8,128)(2,1)S(1)} %get-tuple-element.13.unit, f32[256,128]{1,0:T(8,128)S(1)} %get-tuple-element.14.scale_ref, f32[1,1024]{1,0:T(1,128)S(1)} %bitcast.23, bf16[2048,1024]{1,0:T(8,128)(2,1)S(1)} %copy-done), custom_call_target="tpu_custom_call" | custom-call | flops 2147483648 | bytes 8388608 | tf_op jit(solution)/shard_map/main/pallas_call | solution.py:194
  88.9 0.0 copy-start.2
  88.9 1.0 copy-done.2
  89.8 0.0 copy-start.1
  89.9 13.6 %all-to-all-start.1 = ((bf16[32,128,128]{2,1,0:T(8,128)(2,1)}), bf16[32,128,128]{2,1,0:T(8,128)(2,1)S(1)}, u32[]{:S(2)}, u32[]{:S(2)}) async-start(bf16[32,128,128]{2,1,0:T(8,128)(2,1)} %copy-done.2), calls=%async_computation.1 | async-start | bytes 2097152 | tf_op jit(solution)/shard_map/gradient_exchange/all_to_all | solution.py:213
  103.4 17.1 %all-to-all-done.1.parts_ref = bf16[32,128,128]{2,1,0:T(8,128)(2,1)S(1)} async-done(((bf16[32,128,128]{2,1,0:T(8,128)(2,1)}), bf16[32,128,128]{2,1,0:T(8,128)(2,1)S(1)}, u32[]{:S(2)}, u32[]{:S(2)}) %all-to-all-start.1) | async-done | bytes 1048608 | tf_op jit(solution)/shard_map/gradient_exchange/all_to_all | solution.py:213
  120.6 0.0 copy-done.1
  120.6 1.0 tail.1
  121.6 1.9 %collective-permute-start.1 = (f32[3,128]{1,0:T(4,128)S(1)}, f32[3,128]{1,0:T(4,128)S(1)}, u32[]{:S(2)}, u32[]{:S(2)}) collective-permute-start(f32[3,128]{1,0:T(4,128)S(1)} %slice_select_fusion.1), channel_id=1, source_target_pairs={{0,496},{16,32},{32,16},{48,64},{64,48},{80,96},{96,80},{112,128},... | collective-permute-start | bytes 4616 | tf_op jit(solution)/shard_map/ghosts/ppermute | solution.py:231
  123.5 4.5 %collective-permute-done.1 = f32[3,128]{1,0:T(4,128)S(1)} collective-permute-done((f32[3,128]{1,0:T(4,128)S(1)}, f32[3,128]{1,0:T(4,128)S(1)}, u32[]{:S(2)}, u32[]{:S(2)}) %collective-permute-start.1) | collective-permute-done | bytes 1568 | tf_op jit(solution)/shard_map/ghosts/ppermute | solution.py:231
  128.1 12.1 %all_to_all.15 = f32[32,4,128]{2,1,0:T(4,128)S(1)} all-to-all(f32[32,4,128]{2,1,0:T(4,128)S(1)} %bitcast.24), channel_id=1, replica_groups=mesh['z'=16,'yl'=2,'x'=4,'yh'=2,'c'=2] {'yl','x','yh','c'}, dimensions={0} | all-to-all | bytes 131072 | tf_op jit(solution)/shard_map/ghosts/all_to_all | solution.py:235
  140.2 0.0 copy-start.4
  140.2 0.5 slice_bitcast_fusion
  140.7 0.1 copy-done.4
  (9 shorter events, 0.1 us)
Async XLA Ops:
  1.7 10.1 %collective-permute-start = (f16[64,1024]{1,0:T(8,128)(2,1)S(1)}, f16[64,1024]{1,0:T(8,128)(2,1)S(1)}, u32[]{:S(2)}, u32[]{:S(2)}) collective-permute-start(f16[64,1024]{1,0:T(8,128)(2,1)S(1)} %get-tuple-element.19), channel_id=1, source_target_pairs={{0,16},{16,0},{1,17},{17,1},{2,18},{18,2},{3,19},{19,3},{4,20},{20... | collective-permute-start | bytes 393224 | tf_op jit(solution)/shard_map/points_swap/ppermute | solution.py:138
  5.7 0.8 copy-start.3
  11.8 71.7 %all-to-all-start = ((bf16[32,128,128]{2,1,0:T(8,128)(2,1)}), bf16[32,128,128]{2,1,0:T(8,128)(2,1)S(1)}, u32[]{:S(2)}, u32[]{:S(2)}) async-start(bf16[32,128,128]{2,1,0:T(8,128)(2,1)} %descriptors_gather.2), calls=%async_computation | async-start | bytes 2097152 | tf_op jit(solution)/shard_map/descriptors_gather/all_to_all | solution.py:154
  84.2 2.2 %copy-start = (bf16[2048,1024]{1,0:T(8,128)(2,1)S(1)}, bf16[2048,1024]{1,0:T(8,128)(2,1)}, u32[]{:S(2)}) copy-start(bf16[2048,1024]{1,0:T(8,128)(2,1)} %multiply_convert_fusion.basis) | copy-start | bytes 12582916
  88.9 1.0 copy-start.2
  89.8 30.7 %copy-start.1 = (bf16[128,3,12,128]{3,0,2,1:T(8,128)(2,1)S(1)}, bf16[128,3,12,128]{3,0,2,1:T(8,128)(2,1)}, u32[]{:S(2)}) copy-start(bf16[128,3,12,128]{3,0,2,1:T(8,128)(2,1)} %param.10) | copy-start | bytes 3538948
  89.9 30.7 %all-to-all-start.1 = ((bf16[32,128,128]{2,1,0:T(8,128)(2,1)}), bf16[32,128,128]{2,1,0:T(8,128)(2,1)S(1)}, u32[]{:S(2)}, u32[]{:S(2)}) async-start(bf16[32,128,128]{2,1,0:T(8,128)(2,1)} %copy-done.2), calls=%async_computation.1 | async-start | bytes 2097152 | tf_op jit(solution)/shard_map/gradient_exchange/all_to_all | solution.py:213
  121.6 6.4 %collective-permute-start.1 = (f32[3,128]{1,0:T(4,128)S(1)}, f32[3,128]{1,0:T(4,128)S(1)}, u32[]{:S(2)}, u32[]{:S(2)}) collective-permute-start(f32[3,128]{1,0:T(4,128)S(1)} %slice_select_fusion.1), channel_id=1, source_target_pairs={{0,496},{16,32},{32,16},{48,64},{64,48},{80,96},{96,80},{112,128},... | collective-permute-start | bytes 4616 | tf_op jit(solution)/shard_map/ghosts/ppermute | solution.py:231
  140.2 0.6 copy-start.4

commit v5 on v4

--- a/solution.py
+++ b/solution.py
@@ -37,50 +37,53 @@
         scale = jnp.broadcast_to(1.0 / norm, (owned, width))
         scale_ref[y * owned : (y + 1) * owned, :] = scale
         for s in range(blocks):
-            value = rows_ref[y * blocks + s].astype(F32) * scale
+            value = rows_ref[y * blocks + s].astype(F32) * (scale * (1.0 / LIFT))
             unit_ref[y * owned : (y + 1) * owned, s * width : (s + 1) * width] = pltpu.roll(
                 value, shift, 1
             ).astype(BF16)
 
 
-def main_kernel(unit, scale_ref, coef_ref, basis, share_ref, energy_ref, kernel, slopes, inner):
-    columns = basis.shape[0]
-    width = scale_ref.shape[1]
-    atoms = unit.shape[0]
+def slope_kernel(side_ref, kernel_ref, scale_ref, coef_ref, slopes_ref, inner_ref, energy_ref, wide):
+    atoms = kernel_ref.shape[0]
     domains = energy_ref.shape[0]
     owned = atoms // domains
-    blocks = columns // width
-    kernel[...] = jnp.dot(unit[...], basis[...], preferred_element_type=F32)
-    four = 4.0 * coef_ref[...]
+    four = 4.0 * coef_ref[pl.ds(side_ref[0], 1), :]
     rows = 32
     for r in range(0, atoms, rows):
-        k = kernel[r : r + rows, :]
+        k = kernel_ref[r : r + rows, :]
         s = four * (k * k * k)
         low = s.astype(BF16)
-        slopes[r : r + rows, :] = low
-        inner[r : r + rows, :] = scale_ref[r : r + rows, :] * jnp.sum(
+        slopes_ref[r : r + rows, :] = low
+        inner_ref[r : r + rows, :] = (scale_ref[r : r + rows, :] * LIFT) * jnp.sum(
             low.astype(F32) * k, axis=1, keepdims=True
         )
-        kernel[r : r + rows, 0:128] = jnp.broadcast_to(
+        wide[r : r + rows, :] = jnp.broadcast_to(
             0.25 * jnp.sum(s * k, axis=1, keepdims=True), (rows, 128)
         )
     for y in range(domains):
-        energy_ref[y] = kernel[y * owned : (y + 1) * owned, 0:128].T[0:8, :]
-    for i in range(0, blocks, 2):
-        g = lax.dot_general(
-            slopes[...],
-            basis[i * width : (i + 2) * width, :],
-            LAST,
-            preferred_element_type=F32,
-        )
-        for p in range(2):
-            lanes = slice((i + p) * width, (i + p + 1) * width)
+        energy_ref[y] = wide[y * owned : (y + 1) * owned, :].T[0:8, :]
+
+
+def project_kernel(gradient_ref, unit_ref, scale_ref, inner_ref, share_hbm, share, sems):
+    count, owned, width = share.shape
+    domains = unit_ref.shape[0] // owned
+    blocks = count // domains
+    scale = scale_ref[...] * (1.0 / LIFT)
+    sends = []
+    for i in range(0, blocks, 4):
+        for p in range(i, i + 4):
+            lanes = slice(p * width, (p + 1) * width)
             part = (
-                g[:, p * width : (p + 1) * width] * scale_ref[...]
-                - unit[:, lanes].astype(F32) * inner[...]
+                gradient_ref[:, lanes] * scale - unit_ref[:, lanes].astype(F32) * inner_ref[...]
             ).astype(BF16)
             for y in range(domains):
-                share_ref[y * blocks + i + p] = part[y * owned : (y + 1) * owned]
+                share[y * blocks + p] = part[y * owned : (y + 1) * owned]
+        for y in range(domains):
+            at = pl.ds(y * blocks + i, 4)
+            sends.append(pltpu.make_async_copy(share.at[at], share_hbm.at[at], sems.at[len(sends)]))
+            sends[-1].start()
+    for send in sends:
+        send.wait()
 
 
 def tail_kernel(parts_ref, deriv_ref, table_ref, out_ref):
@@ -131,6 +134,8 @@
     smem = pl.BlockSpec(memory_space=pltpu.SMEM)
     anywhere = pl.BlockSpec(memory_space=pl.ANY)
 
+    side = yl.reshape(1).astype(jnp.int32)
+
     with jax.named_scope("points_swap"):
         turned = sparse_points.T
         kept = lax.dynamic_slice_in_dim(turned, yl * half, half, 1).astype(F32) * LIFT
@@ -139,18 +144,16 @@
         block = jnp.concatenate([kept.astype(F16), got], axis=0)
     with jax.named_scope("points_gather"):
         lifted = lax.all_gather(block, "z", axis=0, tiled=True)
-        basis = (lifted.astype(F32) * (1.0 / LIFT)).astype(BF16)
 
     with jax.named_scope("descriptors_gather"):
         spread = pl.pallas_call(
             spread_kernel,
             out_shape=jax.ShapeDtypeStruct((n_plane, owned, width), BF16),
-            in_specs=[vmem],
+            in_specs=[anywhere],
             out_specs=anywhere,
             scratch_shapes=[pltpu.SemaphoreType.DMA((n_plane,))],
             compiler_params=pltpu.CompilerParams(vmem_limit_bytes=4 << 20),
         )(descriptors)
-        spread, block = lax.optimization_barrier((spread, block))
         rows = lax.all_to_all(spread, PLANE, 0, 0)
         unit_rows, scale = pl.pallas_call(
             prepare_kernel,
@@ -164,9 +167,45 @@
             cost_estimate=pl.CostEstimate(
                 flops=8 * atoms * columns, bytes_accessed=4 << 20, transcendentals=0
             ),
-        )(yl.reshape(1).astype(jnp.int32), rows)
+        )(side, rows)
+
+    with jax.named_scope("kernel"):
+        kernel = jnp.dot(unit_rows, lifted.astype(BF16), preferred_element_type=F32)
+        slopes, inner, energy_part = pl.pallas_call(
+            slope_kernel,
+            out_shape=(
+                jax.ShapeDtypeStruct((atoms, half), BF16),
+                jax.ShapeDtypeStruct((atoms, width), F32),
+                jax.ShapeDtypeStruct((2, 8, owned), F32),
+            ),
+            in_specs=[smem] + [vmem] * 3,
+            out_specs=(vmem, vmem, vmem),
+            scratch_shapes=[pltpu.VMEM((atoms, width), F32)],
+            compiler_params=pltpu.CompilerParams(vmem_limit_bytes=8 << 20),
+        )(side, kernel, scale, coefficients.reshape(2, half))
+    with jax.named_scope("gradient"):
+        slopes, again = lax.optimization_barrier((slopes, lifted))
+        gradient = lax.dot_general(
+            slopes, again.astype(BF16), LAST, preferred_element_type=F32
+        )
+        outgoing = pl.pallas_call(
+            project_kernel,
+            out_shape=jax.ShapeDtypeStruct((n_plane, owned, width), BF16),
+            in_specs=[vmem] * 4,
+            out_specs=anywhere,
+            scratch_shapes=[
+                pltpu.VMEM((n_plane, owned, width), BF16),
+                pltpu.SemaphoreType.DMA((8,)),
+            ],
+            compiler_params=pltpu.CompilerParams(vmem_limit_bytes=8 << 20),
+        )(gradient, unit_rows, scale, inner)
+    with jax.named_scope("gradient_exchange"):
+        parts = lax.all_to_all(outgoing, PLANE, 0, 0)
 
     with jax.named_scope("scatter_table"):
+        neighbours, counts, ghost_index, energy_part = lax.optimization_barrier(
+            (neighbours, counts, ghost_index, energy_part)
+        )
         slot_total = owned + 2 * ghosts
         flat = neighbours.T.reshape(pairs_count)
         slot_ids = jnp.arange(slot_total, dtype=jnp.int32)
@@ -188,29 +227,6 @@
         table = jnp.where(live[:, None], self_hot - landed, 0.0).astype(BF16)
         lined = jnp.transpose(derivatives, (1, 2, 0, 3)).reshape(3, pairs_count, width)
 
-    unit_rows, scale, table = lax.optimization_barrier((unit_rows, scale, table))
-    with jax.named_scope("main"):
-        coefs = lax.dynamic_slice_in_dim(coefficients, yl * half, half, 0)[None, :]
-        outgoing, energy_part = pl.pallas_call(
-            main_kernel,
-            out_shape=(
-                jax.ShapeDtypeStruct((n_plane, owned, width), BF16),
-                jax.ShapeDtypeStruct((2, 8, owned), F32),
-            ),
-            in_specs=[vmem] * 4,
-            out_specs=(vmem, vmem),
-            scratch_shapes=[
-                pltpu.VMEM((atoms, half), F32),
-                pltpu.VMEM((atoms, half), BF16),
-                pltpu.VMEM((atoms, width), F32),
-            ],
-            compiler_params=pltpu.CompilerParams(vmem_limit_bytes=24 << 20),
-            cost_estimate=pl.CostEstimate(
-                flops=4 * atoms * half * columns, bytes_accessed=8 << 20, transcendentals=0
-            ),
-        )(unit_rows, scale, coefs, basis)
-    with jax.named_scope("gradient_exchange"):
-        parts = lax.all_to_all(outgoing, PLANE, 0, 0)
     with jax.named_scope("tail"):
         moved = pl.pallas_call(
             tail_kernel,

time: 141 us -> 137 us (0.972)
  other arithmetic: 5.83 us -> 1.2 us
  matrix products: 1.88 us -> 6.1 us
  local copies, waits for them, and re-layouts: 5.18 us -> 1.39 us
    dot_general x0 -> x2, matrix products: none -> 4.92 us  [the longest x1 3.62 us: body(): kernel = jnp.dot(unit_rows, lifted.astype(BF16), preferred_element_type=F32)]
    convert_element_type x1 -> x0, other arithmetic: 3.22 us -> none  [body(): basis = (lifted.astype(F32) * (1.0 / LIFT)).astype(BF16)]
    unnamed x10 -> x16, local copies, waits for them, and re-layouts: 3.96 us -> 0.85 us
  transfers between devices with their start and end apart: 4 -> 4, of which waited for: 2 -> 2; matrix products, arithmetic and copies ran while one was open for 5% -> 1% of each run, Pallas kernels for 1% -> 1%
where the time goes in v5:
time: 137 us; the launch traced here: 136 us
  blocking collectives  73.6 us (54%)
  starting transfers between devices  28 us (20%)
  waiting for transfers between devices  20.4 us (15%)
  matrix products  6.1 us (4%)
  Pallas kernels  4.68 us (3%)
  local copies, waits for them, and re-layouts  1.39 us (1%)
    all_gather x1, blocking collectives, body(): lifted = lax.all_gather(block, 'z', axis=0, tiled=True)  61.5 us
    all_to_all x1, waiting for transfers between devices, body(): parts = lax.all_to_all(outgoing, PLANE, 0, 0)  15.9 us
    all_to_all x1, starting transfers between devices, body(): parts = lax.all_to_all(outgoing, PLANE, 0, 0)  13.6 us
    all_to_all x1, blocking collectives, body(): received = jnp.sum(lax.all_to_all(both, PLANE, 0, 0), axis=0)  12.1 us
    all_to_all x1, starting transfers between devices, body(): rows = lax.all_to_all(spread, PLANE, 0, 0)  8.36 us
    ppermute x1, waiting for transfers between devices, body(): keep = keep + lax.ppermute(across, DOM, pairs)  4.5 us
    ppermute x1, starting transfers between devices, body(): got = lax.ppermute(sent.astype(F16), 'yl', swap)  4.03 us
    dot_general x1, matrix products, body(): kernel = jnp.dot(unit_rows, lifted.astype(BF16), preferred_element_type=F32)  3.62 us
  transfers between devices with their start and end apart: 4, of which 2 were waited for; matrix products, arithmetic and copies ran while one was open for 1% of the time, Pallas kernels for 1%

profile of v5, /device:TPU:1, one launch (start us, length us, event | category | flops | bytes accessed | tf_op | source)
XLA Modules:
  0.0 136.2 jit_solution(15856211378198570094)
XLA Ops:
  0.6 0.0 copy-start.3
  0.6 1.0 fusion.8
  1.7 4.0 %collective-permute-start = (f16[64,1024]{1,0:T(8,128)(2,1)S(1)}, f16[64,1024]{1,0:T(8,128)(2,1)S(1)}, u32[]{:S(2)}, u32[]{:S(2)}) collective-permute-start(f16[64,1024]{1,0:T(8,128)(2,1)S(1)} %get-tuple-element.25), channel_id=1, source_target_pairs={{0,16},{16,0},{1,17},{17,1},{2,18},{18,2},{3,19},{19,3},{4,20},{20... | collective-permute-start | bytes 393224 | tf_op jit(solution)/shard_map/points_swap/ppermute | solution.py:143
  5.7 0.0 copy-start.1
  5.7 0.7 copy-done.1
  6.5 1.3 descriptors_gather.2
  7.8 8.4 %all-to-all-start = ((bf16[32,128,128]{2,1,0:T(8,128)(2,1)}), bf16[32,128,128]{2,1,0:T(8,128)(2,1)S(1)}, u32[]{:S(2)}, u32[]{:S(2)}) async-start(bf16[32,128,128]{2,1,0:T(8,128)(2,1)} %descriptors_gather.2), calls=%async_computation | async-start | bytes 2097152 | tf_op jit(solution)/shard_map/descriptors_gather/all_to_all | solution.py:157
  16.1 0.0 copy-done.3
  16.2 0.0 collective-permute-done
  16.2 0.1 pad_maximum_fusion
  16.2 61.5 %all-gather.1 = f16[2048,1024]{1,0:T(8,128)(2,1)} all-gather(f16[128,1024]{1,0:T(8,128)(2,1)S(1)} %pad_maximum_fusion), channel_id=1, replica_groups=mesh['z'=16,'yl'=2,'x'=4,'yh'=2,'c'=2] {'z'}, dimensions={0}, use_global_device_ids=true | all-gather | bytes 4456448 | tf_op jit(solution)/shard_map/points_gather/all_gather | solution.py:146
  77.7 0.0 all-to-all-done.rows_ref
  77.7 0.7 descriptors_gather.3
  78.4 0.0 copy-start.2
  78.4 3.6 %fusion.2.kernel_ref = f32[256,1024]{1,0:T(8,128)S(1)} fusion(bf16[256,2048]{1,0:T(8,128)(2,1)S(1)} %get-tuple-element.13.unit_ref, f16[2048,1024]{1,0:T(8,128)(2,1)} %all-gather.1), kind=kOutput, calls=%fused_computation.2 | convolution fusion | flops 1075838976 | bytes 6291456 | tf_op jit(solution)/shard_map/kernel/dot_general | solution.py:173
  82.1 0.4 kernel.1
  82.5 0.0 copy-done.2
  82.5 1.3 fusion.gradient_ref
  83.8 0.0 copy-start.5
  83.8 0.0 copy-start.6
  83.8 0.0 copy-start.7
  83.8 1.3 gradient.1
  85.1 13.6 %all-to-all-start.1 = ((bf16[32,128,128]{2,1,0:T(8,128)(2,1)}), bf16[32,128,128]{2,1,0:T(8,128)(2,1)S(1)}, u32[]{:S(2)}, u32[]{:S(2)}) async-start(bf16[32,128,128]{2,1,0:T(8,128)(2,1)} %gradient.1), calls=%async_computation.1 | async-start | bytes 2097152 | tf_op jit(solution)/shard_map/gradient_exchange/all_to_all | solution.py:203
  98.8 0.0 copy-start
  98.8 0.0 copy-done.5
  98.8 0.0 copy-done.6
  98.9 0.0 copy-done.7
  98.9 1.2 fusion.5.table_ref
  100.1 15.9 %all-to-all-done.1.parts_ref = bf16[32,128,128]{2,1,0:T(8,128)(2,1)S(1)} async-done(((bf16[32,128,128]{2,1,0:T(8,128)(2,1)}), bf16[32,128,128]{2,1,0:T(8,128)(2,1)S(1)}, u32[]{:S(2)}, u32[]{:S(2)}) %all-to-all-start.1) | async-done | bytes 1048608 | tf_op jit(solution)/shard_map/gradient_exchange/all_to_all | solution.py:203
  115.9 0.0 copy-done
  115.9 1.0 tail.1
  117.0 1.9 %collective-permute-start.1 = (f32[3,128]{1,0:T(4,128)S(1)}, f32[3,128]{1,0:T(4,128)S(1)}, u32[]{:S(2)}, u32[]{:S(2)}) collective-permute-start(f32[3,128]{1,0:T(4,128)S(1)} %slice_select_fusion.1), channel_id=1, source_target_pairs={{0,496},{16,32},{32,16},{48,64},{64,48},{80,96},{96,80},{112,128},... | collective-permute-start | bytes 4616 | tf_op jit(solution)/shard_map/ghosts/ppermute | solution.py:247
  118.9 4.5 %collective-permute-done.1 = f32[3,128]{1,0:T(4,128)S(1)} collective-permute-done((f32[3,128]{1,0:T(4,128)S(1)}, f32[3,128]{1,0:T(4,128)S(1)}, u32[]{:S(2)}, u32[]{:S(2)}) %collective-permute-start.1) | collective-permute-done | bytes 1568 | tf_op jit(solution)/shard_map/ghosts/ppermute | solution.py:247
  123.5 12.1 %all_to_all.15 = f32[32,4,128]{2,1,0:T(4,128)S(1)} all-to-all(f32[32,4,128]{2,1,0:T(4,128)S(1)} %bitcast.24), channel_id=1, replica_groups=mesh['z'=16,'yl'=2,'x'=4,'yh'=2,'c'=2] {'yl','x','yh','c'}, dimensions={0} | all-to-all | bytes 131072 | tf_op jit(solution)/shard_map/ghosts/all_to_all | solution.py:251
  135.6 0.0 copy-start.4
  135.6 0.5 slice_bitcast_fusion
  136.1 0.1 copy-done.4
  (12 shorter events, 0.1 us)
Async XLA Ops:
  0.6 15.5 %copy-start.3 = (f32[2048]{0:T(1024)S(1)}, f32[2048]{0:T(1024)}, u32[]{:S(2)}) copy-start(f32[2048]{0:T(1024)} %param.9) | copy-start | bytes 24580
  1.7 14.5 %collective-permute-start = (f16[64,1024]{1,0:T(8,128)(2,1)S(1)}, f16[64,1024]{1,0:T(8,128)(2,1)S(1)}, u32[]{:S(2)}, u32[]{:S(2)}) collective-permute-start(f16[64,1024]{1,0:T(8,128)(2,1)S(1)} %get-tuple-element.25), channel_id=1, source_target_pairs={{0,16},{16,0},{1,17},{17,1},{2,18},{18,2},{3,19},{19,3},{4,20},{20... | collective-permute-start | bytes 393224 | tf_op jit(solution)/shard_map/points_swap/ppermute | solution.py:143
  5.7 0.8 copy-start.1
  7.8 70.0 %all-to-all-start = ((bf16[32,128,128]{2,1,0:T(8,128)(2,1)}), bf16[32,128,128]{2,1,0:T(8,128)(2,1)S(1)}, u32[]{:S(2)}, u32[]{:S(2)}) async-start(bf16[32,128,128]{2,1,0:T(8,128)(2,1)} %descriptors_gather.2), calls=%async_computation | async-start | bytes 2097152 | tf_op jit(solution)/shard_map/descriptors_gather/all_to_all | solution.py:157
  78.4 4.1 %copy-start.2 = (f16[2048,1024]{1,0:T(8,128)(2,1)S(1)}, f16[2048,1024]{1,0:T(8,128)(2,1)}, u32[]{:S(2)}) copy-start(f16[2048,1024]{1,0:T(8,128)(2,1)} %all-gather.1) | copy-start | bytes 12582916
  83.8 15.0 %copy-start.5 = (s32[256]{0:T(256)S(1)}, s32[256]{0:T(256)}, u32[]{:S(2)}) copy-start(s32[256]{0:T(256)} %param.13) | copy-start | bytes 3076
  83.8 15.0 %copy-start.6 = (s32[128]{0:T(128)S(1)}, s32[128]{0:T(128)}, u32[]{:S(2)}) copy-start(s32[128]{0:T(128)} %param.12) | copy-start | bytes 1540
  83.8 15.0 %copy-start.7 = (s32[128,12]{0,1:T(8,128)S(1)}, s32[128,12]{0,1:T(8,128)}, u32[]{:S(2)}) copy-start(s32[128,12]{0,1:T(8,128)} %param.11) | copy-start | bytes 18436
  85.1 30.8 %all-to-all-start.1 = ((bf16[32,128,128]{2,1,0:T(8,128)(2,1)}), bf16[32,128,128]{2,1,0:T(8,128)(2,1)S(1)}, u32[]{:S(2)}, u32[]{:S(2)}) async-start(bf16[32,128,128]{2,1,0:T(8,128)(2,1)} %gradient.1), calls=%async_computation.1 | async-start | bytes 2097152 | tf_op jit(solution)/shard_map/gradient_exchange/all_to_all | solution.py:203
  98.8 17.2 %copy-start = (bf16[128,3,12,128]{3,0,2,1:T(8,128)(2,1)S(1)}, bf16[128,3,12,128]{3,0,2,1:T(8,128)(2,1)}, u32[]{:S(2)}) copy-start(bf16[128,3,12,128]{3,0,2,1:T(8,128)(2,1)} %param.10) | copy-start | bytes 3538948
  117.0 6.4 %collective-permute-start.1 = (f32[3,128]{1,0:T(4,128)S(1)}, f32[3,128]{1,0:T(4,128)S(1)}, u32[]{:S(2)}, u32[]{:S(2)}) collective-permute-start(f32[3,128]{1,0:T(4,128)S(1)} %slice_select_fusion.1), channel_id=1, source_target_pairs={{0,496},{16,32},{32,16},{48,64},{64,48},{80,96},{96,80},{112,128},... | collective-permute-start | bytes 4616 | tf_op jit(solution)/shard_map/ghosts/ppermute | solution.py:247
  135.6 0.6 copy-start.4

commit v6 on v5

--- a/solution.py
+++ b/solution.py
@@ -7,8 +7,9 @@
 
 DOM = ("z", "yl")
 SP = ("x", "yh", "c")
-PLANE = ("yl", "x", "yh", "c")
-LIFT = 4096.0
+RUN = 4
+PLANE = ("x", "yl", "yh", "c")
+LIFT = 8192.0
 F32, BF16, F16 = jnp.float32, jnp.bfloat16, jnp.float16
 LAST = (((1,), (1,)), ((), ()))
 
@@ -27,17 +28,18 @@
     domains = 2
     blocks = rows_ref.shape[0] // domains
     owned, width = rows_ref.shape[1:]
+    at = [[s // RUN * 2 * RUN + y * RUN + s % RUN for s in range(blocks)] for y in range(domains)]
     shift = side_ref[0] * (width // 2)
     for y in range(domains):
         total = jnp.zeros((owned, width), F32)
         for s in range(blocks):
-            value = rows_ref[y * blocks + s].astype(F32)
+            value = rows_ref[at[y][s]].astype(F32)
             total += value * value
         norm = jnp.sqrt(jnp.sum(total, axis=1, keepdims=True) + 1e-06)
         scale = jnp.broadcast_to(1.0 / norm, (owned, width))
         scale_ref[y * owned : (y + 1) * owned, :] = scale
         for s in range(blocks):
-            value = rows_ref[y * blocks + s].astype(F32) * (scale * (1.0 / LIFT))
+            value = rows_ref[at[y][s]].astype(F32) * (scale * (1.0 / LIFT))
             unit_ref[y * owned : (y + 1) * owned, s * width : (s + 1) * width] = pltpu.roll(
                 value, shift, 1
             ).astype(BF16)
@@ -70,16 +72,16 @@
     blocks = count // domains
     scale = scale_ref[...] * (1.0 / LIFT)
     sends = []
-    for i in range(0, blocks, 4):
-        for p in range(i, i + 4):
+    for i in range(0, blocks, RUN):
+        for p in range(i, i + RUN):
             lanes = slice(p * width, (p + 1) * width)
             part = (
                 gradient_ref[:, lanes] * scale - unit_ref[:, lanes].astype(F32) * inner_ref[...]
             ).astype(BF16)
             for y in range(domains):
-                share[y * blocks + p] = part[y * owned : (y + 1) * owned]
+                share[i * domains + y * RUN + p - i] = part[y * owned : (y + 1) * owned]
         for y in range(domains):
-            at = pl.ds(y * blocks + i, 4)
+            at = pl.ds(i * domains + y * RUN, RUN)
             sends.append(pltpu.make_async_copy(share.at[at], share_hbm.at[at], sems.at[len(sends)]))
             sends[-1].start()
     for send in sends:
@@ -90,9 +92,9 @@
     count, atoms, width = parts_ref.shape
     sides = []
     for y in range(2):
-        total = parts_ref[y * (count // 2)].astype(F32)
+        total = parts_ref[y * RUN].astype(F32)
         for i in range(1, count // 2):
-            total += parts_ref[y * (count // 2) + i].astype(F32)
+            total += parts_ref[i // RUN * 2 * RUN + y * RUN + i % RUN].astype(F32)
         sides.append(total)
     total = sides[0] + pltpu.roll(sides[1], width // 2, 1)
     pairs = deriv_ref.shape[1]
@@ -247,7 +249,8 @@
         keep = keep + lax.ppermute(across, DOM, pairs)
         both = jnp.stack([jnp.where(first, keep, beside), jnp.where(first, beside, keep)])
         both = jnp.concatenate([both, energy_part[:, :1]], axis=1)
-        both = jnp.broadcast_to(both[:, None], (2, n_sp, 4, owned)).reshape(n_plane, 4, owned)
+        both = jnp.broadcast_to(both[None, :, None], (n_sp // RUN, 2, RUN, 4, owned))
+        both = both.reshape(n_plane, 4, owned)
         received = jnp.sum(lax.all_to_all(both, PLANE, 0, 0), axis=0)
     return (received[:3], received[3])
 

time: 137 us -> 137 us (level)
  no operation moved by 1% of the time
where the time goes in v6:
time: 137 us; the launch traced here: 136 us
  blocking collectives  74 us (54%)
  starting transfers between devices  28 us (20%)
  waiting for transfers between devices  19.8 us (14%)
  matrix products  6.1 us (4%)
  Pallas kernels  4.67 us (3%)
  local copies, waits for them, and re-layouts  1.39 us (1%)
    all_gather x1, blocking collectives, body(): lifted = lax.all_gather(block, 'z', axis=0, tiled=True)  61.5 us
    all_to_all x1, waiting for transfers between devices, body(): parts = lax.all_to_all(outgoing, PLANE, 0, 0)  15.3 us
    all_to_all x1, starting transfers between devices, body(): parts = lax.all_to_all(outgoing, PLANE, 0, 0)  13.7 us
    all_to_all x1, blocking collectives, body(): received = jnp.sum(lax.all_to_all(both, PLANE, 0, 0), axis=0)  12.5 us
    all_to_all x1, starting transfers between devices, body(): rows = lax.all_to_all(spread, PLANE, 0, 0)  8.36 us
    ppermute x1, waiting for transfers between devices, body(): keep = keep + lax.ppermute(across, DOM, pairs)  4.5 us
    ppermute x1, starting transfers between devices, body(): got = lax.ppermute(sent.astype(F16), 'yl', swap)  4.03 us
    dot_general x1, matrix products, body(): kernel = jnp.dot(unit_rows, lifted.astype(BF16), preferred_element_type=F32)  3.62 us
  transfers between devices with their start and end apart: 4, of which 2 were waited for; matrix products, arithmetic and copies ran while one was open for 1% of the time, Pallas kernels for 1%

profile of v6, /device:TPU:1, one launch (start us, length us, event | category | flops | bytes accessed | tf_op | source)
XLA Modules:
  0.0 136.0 jit_solution(12162233673127380725)
XLA Ops:
  0.6 0.0 copy-start.3
  0.6 1.0 fusion.8
  1.7 4.0 %collective-permute-start = (f16[64,1024]{1,0:T(8,128)(2,1)S(1)}, f16[64,1024]{1,0:T(8,128)(2,1)S(1)}, u32[]{:S(2)}, u32[]{:S(2)}) collective-permute-start(f16[64,1024]{1,0:T(8,128)(2,1)S(1)} %get-tuple-element.25), channel_id=1, source_target_pairs={{0,16},{16,0},{1,17},{17,1},{2,18},{18,2},{3,19},{19,3},{4,20},{20... | collective-permute-start | bytes 393224 | tf_op jit(solution)/shard_map/points_swap/ppermute | solution.py:145
  5.7 0.0 copy-start.1
  5.7 0.7 copy-done.1
  6.5 1.3 descriptors_gather.2
  7.8 8.4 %all-to-all-start = ((bf16[32,128,128]{2,1,0:T(8,128)(2,1)}), bf16[32,128,128]{2,1,0:T(8,128)(2,1)S(1)}, u32[]{:S(2)}, u32[]{:S(2)}) async-start(bf16[32,128,128]{2,1,0:T(8,128)(2,1)} %descriptors_gather.2), calls=%async_computation | async-start | bytes 2097152 | tf_op jit(solution)/shard_map/descriptors_gather/all_to_all | solution.py:159
  16.1 0.0 copy-done.3
  16.2 0.0 collective-permute-done
  16.2 0.1 pad_maximum_fusion
  16.2 61.5 %all-gather.1 = f16[2048,1024]{1,0:T(8,128)(2,1)} all-gather(f16[128,1024]{1,0:T(8,128)(2,1)S(1)} %pad_maximum_fusion), channel_id=1, replica_groups=mesh['z'=16,'yl'=2,'x'=4,'yh'=2,'c'=2] {'z'}, dimensions={0}, use_global_device_ids=true | all-gather | bytes 4456448 | tf_op jit(solution)/shard_map/points_gather/all_gather | solution.py:148
  77.7 0.0 all-to-all-done.rows_ref
  77.7 0.7 descriptors_gather.3
  78.4 0.0 copy-start.2
  78.4 3.6 %fusion.2.kernel_ref = f32[256,1024]{1,0:T(8,128)S(1)} fusion(bf16[256,2048]{1,0:T(8,128)(2,1)S(1)} %get-tuple-element.13.unit_ref, f16[2048,1024]{1,0:T(8,128)(2,1)} %all-gather.1), kind=kOutput, calls=%fused_computation.2 | convolution fusion | flops 1075838976 | bytes 6291456 | tf_op jit(solution)/shard_map/kernel/dot_general | solution.py:175
  82.1 0.4 kernel.1
  82.5 0.0 copy-done.2
  82.5 1.3 fusion.gradient_ref
  83.8 0.0 copy-start.5
  83.8 0.0 copy-start.6
  83.8 0.0 copy-start.7
  83.8 1.3 gradient.1
  85.1 13.7 %all-to-all-start.1 = ((bf16[32,128,128]{2,1,0:T(8,128)(2,1)}), bf16[32,128,128]{2,1,0:T(8,128)(2,1)S(1)}, u32[]{:S(2)}, u32[]{:S(2)}) async-start(bf16[32,128,128]{2,1,0:T(8,128)(2,1)} %gradient.1), calls=%async_computation.1 | async-start | bytes 2097152 | tf_op jit(solution)/shard_map/gradient_exchange/all_to_all | solution.py:205
  98.8 0.0 copy-start
  98.8 0.0 copy-done.5
  98.9 0.0 copy-done.6
  98.9 0.0 copy-done.7
  98.9 1.2 fusion.5.table_ref
  100.1 15.3 %all-to-all-done.1.parts_ref = bf16[32,128,128]{2,1,0:T(8,128)(2,1)S(1)} async-done(((bf16[32,128,128]{2,1,0:T(8,128)(2,1)}), bf16[32,128,128]{2,1,0:T(8,128)(2,1)S(1)}, u32[]{:S(2)}, u32[]{:S(2)}) %all-to-all-start.1) | async-done | bytes 1048608 | tf_op jit(solution)/shard_map/gradient_exchange/all_to_all | solution.py:205
  115.4 0.0 copy-done
  115.4 1.0 tail.1
  116.4 1.9 %collective-permute-start.1 = (f32[3,128]{1,0:T(4,128)S(1)}, f32[3,128]{1,0:T(4,128)S(1)}, u32[]{:S(2)}, u32[]{:S(2)}) collective-permute-start(f32[3,128]{1,0:T(4,128)S(1)} %slice_select_fusion.1), channel_id=1, source_target_pairs={{0,496},{16,32},{32,16},{48,64},{64,48},{80,96},{96,80},{112,128},... | collective-permute-start | bytes 4616 | tf_op jit(solution)/shard_map/ghosts/ppermute | solution.py:249
  118.4 4.5 %collective-permute-done.1 = f32[3,128]{1,0:T(4,128)S(1)} collective-permute-done((f32[3,128]{1,0:T(4,128)S(1)}, f32[3,128]{1,0:T(4,128)S(1)}, u32[]{:S(2)}, u32[]{:S(2)}) %collective-permute-start.1) | collective-permute-done | bytes 1568 | tf_op jit(solution)/shard_map/ghosts/ppermute | solution.py:249
  122.9 12.5 %all_to_all.15 = f32[32,4,128]{2,1,0:T(4,128)S(1)} all-to-all(f32[32,4,128]{2,1,0:T(4,128)S(1)} %bitcast.24), channel_id=1, replica_groups=mesh['z'=16,'yl'=2,'x'=4,'yh'=2,'c'=2] {'x','yl','yh','c'}, dimensions={0} | all-to-all | bytes 131072 | tf_op jit(solution)/shard_map/ghosts/all_to_all | solution.py:254
  135.4 0.0 copy-start.4
  135.4 0.5 slice_bitcast_fusion
  136.0 0.1 copy-done.4
  (12 shorter events, 0.1 us)
Async XLA Ops:
  0.6 15.5 %copy-start.3 = (f32[2048]{0:T(1024)S(1)}, f32[2048]{0:T(1024)}, u32[]{:S(2)}) copy-start(f32[2048]{0:T(1024)} %param.9) | copy-start | bytes 24580
  1.7 14.5 %collective-permute-start = (f16[64,1024]{1,0:T(8,128)(2,1)S(1)}, f16[64,1024]{1,0:T(8,128)(2,1)S(1)}, u32[]{:S(2)}, u32[]{:S(2)}) collective-permute-start(f16[64,1024]{1,0:T(8,128)(2,1)S(1)} %get-tuple-element.25), channel_id=1, source_target_pairs={{0,16},{16,0},{1,17},{17,1},{2,18},{18,2},{3,19},{19,3},{4,20},{20... | collective-permute-start | bytes 393224 | tf_op jit(solution)/shard_map/points_swap/ppermute | solution.py:145
  5.7 0.8 copy-start.1
  7.8 70.0 %all-to-all-start = ((bf16[32,128,128]{2,1,0:T(8,128)(2,1)}), bf16[32,128,128]{2,1,0:T(8,128)(2,1)S(1)}, u32[]{:S(2)}, u32[]{:S(2)}) async-start(bf16[32,128,128]{2,1,0:T(8,128)(2,1)} %descriptors_gather.2), calls=%async_computation | async-start | bytes 2097152 | tf_op jit(solution)/shard_map/descriptors_gather/all_to_all | solution.py:159
  78.4 4.1 %copy-start.2 = (f16[2048,1024]{1,0:T(8,128)(2,1)S(1)}, f16[2048,1024]{1,0:T(8,128)(2,1)}, u32[]{:S(2)}) copy-start(f16[2048,1024]{1,0:T(8,128)(2,1)} %all-gather.1) | copy-start | bytes 12582916
  83.8 15.0 %copy-start.5 = (s32[256]{0:T(256)S(1)}, s32[256]{0:T(256)}, u32[]{:S(2)}) copy-start(s32[256]{0:T(256)} %param.13) | copy-start | bytes 3076
  83.8 15.0 %copy-start.6 = (s32[128]{0:T(128)S(1)}, s32[128]{0:T(128)}, u32[]{:S(2)}) copy-start(s32[128]{0:T(128)} %param.12) | copy-start | bytes 1540
  83.8 15.1 %copy-start.7 = (s32[128,12]{0,1:T(8,128)S(1)}, s32[128,12]{0,1:T(8,128)}, u32[]{:S(2)}) copy-start(s32[128,12]{0,1:T(8,128)} %param.11) | copy-start | bytes 18436
  85.1 30.3 %all-to-all-start.1 = ((bf16[32,128,128]{2,1,0:T(8,128)(2,1)}), bf16[32,128,128]{2,1,0:T(8,128)(2,1)S(1)}, u32[]{:S(2)}, u32[]{:S(2)}) async-start(bf16[32,128,128]{2,1,0:T(8,128)(2,1)} %gradient.1), calls=%async_computation.1 | async-start | bytes 2097152 | tf_op jit(solution)/shard_map/gradient_exchange/all_to_all | solution.py:205
  98.8 16.6 %copy-start = (bf16[128,3,12,128]{3,0,2,1:T(8,128)(2,1)S(1)}, bf16[128,3,12,128]{3,0,2,1:T(8,128)(2,1)}, u32[]{:S(2)}) copy-start(bf16[128,3,12,128]{3,0,2,1:T(8,128)(2,1)} %param.10) | copy-start | bytes 3538948
  116.4 6.4 %collective-permute-start.1 = (f32[3,128]{1,0:T(4,128)S(1)}, f32[3,128]{1,0:T(4,128)S(1)}, u32[]{:S(2)}, u32[]{:S(2)}) collective-permute-start(f32[3,128]{1,0:T(4,128)S(1)} %slice_select_fusion.1), channel_id=1, source_target_pairs={{0,496},{16,32},{32,16},{48,64},{64,48},{80,96},{96,80},{112,128},... | collective-permute-start | bytes 4616 | tf_op jit(solution)/shard_map/ghosts/ppermute | solution.py:249
  135.4 0.6 copy-start.4

commit v7 on v6

--- a/solution.py
+++ b/solution.py
@@ -7,6 +7,8 @@
 
 DOM = ("z", "yl")
 SP = ("x", "yh", "c")
+CHIPS = ("x", "yl", "yh")
+HALF = 2
 RUN = 4
 PLANE = ("x", "yl", "yh", "c")
 LIFT = 8192.0
@@ -66,35 +68,26 @@
         energy_ref[y] = wide[y * owned : (y + 1) * owned, :].T[0:8, :]
 
 
-def project_kernel(gradient_ref, unit_ref, scale_ref, inner_ref, share_hbm, share, sems):
-    count, owned, width = share.shape
+def project_kernel(core_ref, gradient_ref, unit_ref, scale_ref, inner_ref, own_ref, other_ref):
+    count, owned, width = own_ref.shape
     domains = unit_ref.shape[0] // owned
-    blocks = count // domains
     scale = scale_ref[...] * (1.0 / LIFT)
-    sends = []
-    for i in range(0, blocks, RUN):
-        for p in range(i, i + RUN):
-            lanes = slice(p * width, (p + 1) * width)
-            part = (
-                gradient_ref[:, lanes] * scale - unit_ref[:, lanes].astype(F32) * inner_ref[...]
-            ).astype(BF16)
+    for j in range(count // domains):
+        for ref, core in ((own_ref, core_ref[0]), (other_ref, 1 - core_ref[0])):
+            lanes = pl.ds(pl.multiple_of((2 * j + core) * width, width), width)
+            part = gradient_ref[:, lanes] * scale - unit_ref[:, lanes].astype(F32) * inner_ref[...]
             for y in range(domains):
-                share[i * domains + y * RUN + p - i] = part[y * owned : (y + 1) * owned]
-        for y in range(domains):
-            at = pl.ds(i * domains + y * RUN, RUN)
-            sends.append(pltpu.make_async_copy(share.at[at], share_hbm.at[at], sems.at[len(sends)]))
-            sends[-1].start()
-    for send in sends:
-        send.wait()
+                at = j // HALF * 2 * HALF + y * HALF + j % HALF
+                ref[at] = part[y * owned : (y + 1) * owned].astype(ref.dtype)
 
 
 def tail_kernel(parts_ref, deriv_ref, table_ref, out_ref):
     count, atoms, width = parts_ref.shape
     sides = []
     for y in range(2):
-        total = parts_ref[y * RUN].astype(F32)
+        total = parts_ref[y * HALF].astype(F32)
         for i in range(1, count // 2):
-            total += parts_ref[i // RUN * 2 * RUN + y * RUN + i % RUN].astype(F32)
+            total += parts_ref[i // HALF * 2 * HALF + y * HALF + i % HALF].astype(F32)
         sides.append(total)
     total = sides[0] + pltpu.roll(sides[1], width // 2, 1)
     pairs = deriv_ref.shape[1]
@@ -137,6 +130,7 @@
     anywhere = pl.BlockSpec(memory_space=pl.ANY)
 
     side = yl.reshape(1).astype(jnp.int32)
+    core = lax.axis_index("c").reshape(1).astype(jnp.int32)
 
     with jax.named_scope("points_swap"):
         turned = sparse_points.T
@@ -190,19 +184,21 @@
         gradient = lax.dot_general(
             slopes, again.astype(BF16), LAST, preferred_element_type=F32
         )
-        outgoing = pl.pallas_call(
+        own, other = pl.pallas_call(
             project_kernel,
-            out_shape=jax.ShapeDtypeStruct((n_plane, owned, width), BF16),
-            in_specs=[vmem] * 4,
-            out_specs=anywhere,
-            scratch_shapes=[
-                pltpu.VMEM((n_plane, owned, width), BF16),
-                pltpu.SemaphoreType.DMA((8,)),
-            ],
-            compiler_params=pltpu.CompilerParams(vmem_limit_bytes=8 << 20),
-        )(gradient, unit_rows, scale, inner)
+            out_shape=(
+                jax.ShapeDtypeStruct((n_plane // 2, owned, width), F32),
+                jax.ShapeDtypeStruct((n_plane // 2, owned, width), BF16),
+            ),
+            in_specs=[smem] + [vmem] * 4,
+            out_specs=(vmem, vmem),
+            compiler_params=pltpu.CompilerParams(vmem_limit_bytes=12 << 20),
+        )(core, gradient, unit_rows, scale, inner)
+    with jax.named_scope("core_pair"):
+        theirs = lax.ppermute(other, "c", swap)
+        outgoing = (own + theirs.astype(F32)).astype(BF16)
     with jax.named_scope("gradient_exchange"):
-        parts = lax.all_to_all(outgoing, PLANE, 0, 0)
+        parts = lax.all_to_all(outgoing, CHIPS, 0, 0)
 
     with jax.named_scope("scatter_table"):
         neighbours, counts, ghost_index, energy_part = lax.optimization_barrier(

time: 137 us -> 135 us (0.985)
  waiting for transfers between devices: 19.8 us -> 15.5 us
  starting transfers between devices: 28 us -> 29.5 us
    ppermute x0 -> x1, starting transfers between devices: none -> 8.58 us  [body(): theirs = lax.ppermute(other, 'c', swap)]
    all_to_all x1, starting transfers between devices: 13.7 us -> 6.61 us  [body(): parts = lax.all_to_all(outgoing, CHIPS, 0, 0)]
    all_to_all x1, waiting for transfers between devices: 15.3 us -> 9.51 us  [body(): parts = lax.all_to_all(outgoing, CHIPS, 0, 0)]
    ppermute x0 -> x1, waiting for transfers between devices: none -> 1.48 us  [body(): theirs = lax.ppermute(other, 'c', swap)]
  transfers between devices with their start and end apart: 4 -> 5, of which waited for: 2 -> 3; matrix products, arithmetic and copies ran while one was open for 1% -> 1% of each run, Pallas kernels for 1% -> 1%
where the time goes in v7:
time: 135 us; the launch traced here: 134 us
  blocking collectives  74.5 us (55%)
  starting transfers between devices  29.5 us (22%)
  waiting for transfers between devices  15.5 us (11%)
  matrix products  6.1 us (5%)
  Pallas kernels  4.03 us (3%)
  other arithmetic  2.14 us (2%)
  local copies, waits for them, and re-layouts  1.39 us (1%)
    all_gather x1, blocking collectives, body(): lifted = lax.all_gather(block, 'z', axis=0, tiled=True)  61.5 us
    all_to_all x1, blocking collectives, body(): received = jnp.sum(lax.all_to_all(both, PLANE, 0, 0), axis=0)  13 us
    all_to_all x1, waiting for transfers between devices, body(): parts = lax.all_to_all(outgoing, CHIPS, 0, 0)  9.51 us
    ppermute x1, starting transfers between devices, body(): theirs = lax.ppermute(other, 'c', swap)  8.58 us
    all_to_all x1, starting transfers between devices, body(): rows = lax.all_to_all(spread, PLANE, 0, 0)  8.36 us
    all_to_all x1, starting transfers between devices, body(): parts = lax.all_to_all(outgoing, CHIPS, 0, 0)  6.61 us
    ppermute x1, waiting for transfers between devices, body(): keep = keep + lax.ppermute(across, DOM, pairs)  4.5 us
    ppermute x1, starting transfers between devices, body(): got = lax.ppermute(sent.astype(F16), 'yl', swap)  4.03 us
  transfers between devices with their start and end apart: 5, of which 3 were waited for; matrix products, arithmetic and copies ran while one was open for 1% of the time, Pallas kernels for 1%

profile of v7, /device:TPU:1, one launch (start us, length us, event | category | flops | bytes accessed | tf_op | source)
XLA Modules:
  0.0 134.1 jit_solution(7320947854386727993)
XLA Ops:
  0.6 0.0 copy-start.3
  0.6 1.0 fusion.8
  1.7 4.0 %collective-permute-start = (f16[64,1024]{1,0:T(8,128)(2,1)S(1)}, f16[64,1024]{1,0:T(8,128)(2,1)S(1)}, u32[]{:S(2)}, u32[]{:S(2)}) collective-permute-start(f16[64,1024]{1,0:T(8,128)(2,1)S(1)} %get-tuple-element.29), channel_id=1, source_target_pairs={{0,16},{16,0},{1,17},{17,1},{2,18},{18,2},{3,19},{19,3},{4,20},{20... | collective-permute-start | bytes 393224 | tf_op jit(solution)/shard_map/points_swap/ppermute | solution.py:139
  5.7 0.0 copy-start.1
  5.7 0.7 copy-done.1
  6.5 1.3 descriptors_gather.2
  7.8 8.4 %all-to-all-start = ((bf16[32,128,128]{2,1,0:T(8,128)(2,1)}), bf16[32,128,128]{2,1,0:T(8,128)(2,1)S(1)}, u32[]{:S(2)}, u32[]{:S(2)}) async-start(bf16[32,128,128]{2,1,0:T(8,128)(2,1)} %descriptors_gather.2), calls=%async_computation | async-start | bytes 2097152 | tf_op jit(solution)/shard_map/descriptors_gather/all_to_all | solution.py:153
  16.1 0.0 copy-done.3
  16.1 0.0 collective-permute-done
  16.2 0.1 pad_maximum_fusion
  16.2 61.5 %all-gather.1 = f16[2048,1024]{1,0:T(8,128)(2,1)} all-gather(f16[128,1024]{1,0:T(8,128)(2,1)S(1)} %pad_maximum_fusion), channel_id=1, replica_groups=mesh['z'=16,'yl'=2,'x'=4,'yh'=2,'c'=2] {'z'}, dimensions={0}, use_global_device_ids=true | all-gather | bytes 4456448 | tf_op jit(solution)/shard_map/points_gather/all_gather | solution.py:142
  77.7 0.0 all-to-all-done.rows_ref
  77.7 0.7 descriptors_gather.3
  78.4 0.0 copy-start.2
  78.4 3.6 %fusion.2.kernel_ref = f32[256,1024]{1,0:T(8,128)S(1)} fusion(bf16[256,2048]{1,0:T(8,128)(2,1)S(1)} %get-tuple-element.15.unit_ref, f16[2048,1024]{1,0:T(8,128)(2,1)} %all-gather.1), kind=kOutput, calls=%fused_computation.2 | convolution fusion | flops 1075838976 | bytes 6291456 | tf_op jit(solution)/shard_map/kernel/dot_general | solution.py:169
  82.0 0.4 kernel.1
  82.5 0.0 copy-done.2
  82.5 1.3 fusion.gradient_ref
  83.8 0.0 copy-start.5
  83.8 0.7 gradient.1
  84.5 0.0 copy-start.6
  84.5 0.0 copy-start.7
  84.5 8.6 %collective-permute-start.1 = (bf16[16,128,128]{2,1,0:T(8,128)(2,1)S(1)}, bf16[16,128,128]{2,1,0:T(8,128)(2,1)S(1)}, u32[]{:S(2)}, u32[]{:S(2)}) collective-permute-start(bf16[16,128,128]{2,1,0:T(8,128)(2,1)S(1)} %get-tuple-element.22), channel_id=1, source_target_pairs={{0,1},{1,0},{2,3},{3,2},{4,5},{5,4},{6,7},{7,6},{8,9},{9,8},{10,11... | collective-permute-start | bytes 1572872 | tf_op jit(solution)/shard_map/core_pair/ppermute | solution.py:198
  93.1 0.0 copy-done.5
  93.1 1.5 %collective-permute-done.1 = bf16[16,128,128]{2,1,0:T(8,128)(2,1)S(1)} collective-permute-done((bf16[16,128,128]{2,1,0:T(8,128)(2,1)S(1)}, bf16[16,128,128]{2,1,0:T(8,128)(2,1)S(1)}, u32[]{:S(2)}, u32[]{:S(2)}) %collective-permute-start.1) | collective-permute-done | bytes 524320 | tf_op jit(solution)/shard_map/core_pair/ppermute | solution.py:198
  94.6 0.9 add_convert_fusion
  95.5 6.6 %all-to-all-start.1 = ((bf16[16,128,128]{2,1,0:T(8,128)(2,1)}), bf16[16,128,128]{2,1,0:T(8,128)(2,1)S(1)}, u32[]{:S(2)}, u32[]{:S(2)}) async-start(bf16[16,128,128]{2,1,0:T(8,128)(2,1)} %add_convert_fusion), calls=%async_computation.1 | async-start | bytes 1048576 | tf_op jit(solution)/shard_map/gradient_exchange/all_to_all | solution.py:201
  102.2 0.0 copy-start
  102.2 0.0 copy-done.6
  102.2 0.0 copy-done.7
  102.2 1.2 fusion.5.table_ref
  103.4 9.5 %all-to-all-done.1.parts_ref = bf16[16,128,128]{2,1,0:T(8,128)(2,1)S(1)} async-done(((bf16[16,128,128]{2,1,0:T(8,128)(2,1)}), bf16[16,128,128]{2,1,0:T(8,128)(2,1)S(1)}, u32[]{:S(2)}, u32[]{:S(2)}) %all-to-all-start.1) | async-done | bytes 524320 | tf_op jit(solution)/shard_map/gradient_exchange/all_to_all | solution.py:201
  112.9 0.0 copy-done
  112.9 1.0 tail.1
  114.0 1.9 %collective-permute-start.2 = (f32[3,128]{1,0:T(4,128)S(1)}, f32[3,128]{1,0:T(4,128)S(1)}, u32[]{:S(2)}, u32[]{:S(2)}) collective-permute-start(f32[3,128]{1,0:T(4,128)S(1)} %slice_select_fusion.1), channel_id=1, source_target_pairs={{0,496},{16,32},{32,16},{48,64},{64,48},{80,96},{96,80},{112,128},... | collective-permute-start | bytes 4616 | tf_op jit(solution)/shard_map/ghosts/ppermute | solution.py:245
  115.9 4.5 %collective-permute-done.2 = f32[3,128]{1,0:T(4,128)S(1)} collective-permute-done((f32[3,128]{1,0:T(4,128)S(1)}, f32[3,128]{1,0:T(4,128)S(1)}, u32[]{:S(2)}, u32[]{:S(2)}) %collective-permute-start.2) | collective-permute-done | bytes 1568 | tf_op jit(solution)/shard_map/ghosts/ppermute | solution.py:245
  120.4 13.0 %all_to_all.15 = f32[32,4,128]{2,1,0:T(4,128)S(1)} all-to-all(f32[32,4,128]{2,1,0:T(4,128)S(1)} %bitcast.25), channel_id=1, replica_groups=mesh['z'=16,'yl'=2,'x'=4,'yh'=2,'c'=2] {'x','yl','yh','c'}, dimensions={0} | all-to-all | bytes 131072 | tf_op jit(solution)/shard_map/ghosts/all_to_all | solution.py:250
  133.5 0.0 copy-start.4
  133.5 0.5 slice_bitcast_fusion
  134.0 0.1 copy-done.4
  (12 shorter events, 0.1 us)
Async XLA Ops:
  0.6 15.5 %copy-start.3 = (f32[2048]{0:T(1024)S(1)}, f32[2048]{0:T(1024)}, u32[]{:S(2)}) copy-start(f32[2048]{0:T(1024)} %param.9) | copy-start | bytes 24580
  1.7 14.5 %collective-permute-start = (f16[64,1024]{1,0:T(8,128)(2,1)S(1)}, f16[64,1024]{1,0:T(8,128)(2,1)S(1)}, u32[]{:S(2)}, u32[]{:S(2)}) collective-permute-start(f16[64,1024]{1,0:T(8,128)(2,1)S(1)} %get-tuple-element.29), channel_id=1, source_target_pairs={{0,16},{16,0},{1,17},{17,1},{2,18},{18,2},{3,19},{19,3},{4,20},{20... | collective-permute-start | bytes 393224 | tf_op jit(solution)/shard_map/points_swap/ppermute | solution.py:139
  5.7 0.8 copy-start.1
  7.8 70.0 %all-to-all-start = ((bf16[32,128,128]{2,1,0:T(8,128)(2,1)}), bf16[32,128,128]{2,1,0:T(8,128)(2,1)S(1)}, u32[]{:S(2)}, u32[]{:S(2)}) async-start(bf16[32,128,128]{2,1,0:T(8,128)(2,1)} %descriptors_gather.2), calls=%async_computation | async-start | bytes 2097152 | tf_op jit(solution)/shard_map/descriptors_gather/all_to_all | solution.py:153
  78.4 4.1 %copy-start.2 = (f16[2048,1024]{1,0:T(8,128)(2,1)S(1)}, f16[2048,1024]{1,0:T(8,128)(2,1)}, u32[]{:S(2)}) copy-start(f16[2048,1024]{1,0:T(8,128)(2,1)} %all-gather.1) | copy-start | bytes 12582916
  83.8 9.3 %copy-start.5 = (s32[256]{0:T(256)S(1)}, s32[256]{0:T(256)}, u32[]{:S(2)}) copy-start(s32[256]{0:T(256)} %param.13) | copy-start | bytes 3076
  84.5 17.7 %copy-start.6 = (s32[128]{0:T(128)S(1)}, s32[128]{0:T(128)}, u32[]{:S(2)}) copy-start(s32[128]{0:T(128)} %param.12) | copy-start | bytes 1540
  84.5 17.7 %copy-start.7 = (s32[128,12]{0,1:T(8,128)S(1)}, s32[128,12]{0,1:T(8,128)}, u32[]{:S(2)}) copy-start(s32[128,12]{0,1:T(8,128)} %param.11) | copy-start | bytes 18436
  84.5 10.1 %collective-permute-start.1 = (bf16[16,128,128]{2,1,0:T(8,128)(2,1)S(1)}, bf16[16,128,128]{2,1,0:T(8,128)(2,1)S(1)}, u32[]{:S(2)}, u32[]{:S(2)}) collective-permute-start(bf16[16,128,128]{2,1,0:T(8,128)(2,1)S(1)} %get-tuple-element.22), channel_id=1, source_target_pairs={{0,1},{1,0},{2,3},{3,2},{4,5},{5,4},{6,7},{7,6},{8,9},{9,8},{10,11... | collective-permute-start | bytes 1572872 | tf_op jit(solution)/shard_map/core_pair/ppermute | solution.py:198
  95.5 17.4 %all-to-all-start.1 = ((bf16[16,128,128]{2,1,0:T(8,128)(2,1)}), bf16[16,128,128]{2,1,0:T(8,128)(2,1)S(1)}, u32[]{:S(2)}, u32[]{:S(2)}) async-start(bf16[16,128,128]{2,1,0:T(8,128)(2,1)} %add_convert_fusion), calls=%async_computation.1 | async-start | bytes 1048576 | tf_op jit(solution)/shard_map/gradient_exchange/all_to_all | solution.py:201
  102.2 10.8 %copy-start = (bf16[128,3,12,128]{3,0,2,1:T(8,128)(2,1)S(1)}, bf16[128,3,12,128]{3,0,2,1:T(8,128)(2,1)}, u32[]{:S(2)}) copy-start(bf16[128,3,12,128]{3,0,2,1:T(8,128)(2,1)} %param.10) | copy-start | bytes 3538948
  114.0 6.4 %collective-permute-start.2 = (f32[3,128]{1,0:T(4,128)S(1)}, f32[3,128]{1,0:T(4,128)S(1)}, u32[]{:S(2)}, u32[]{:S(2)}) collective-permute-start(f32[3,128]{1,0:T(4,128)S(1)} %slice_select_fusion.1), channel_id=1, source_target_pairs={{0,496},{16,32},{32,16},{48,64},{64,48},{80,96},{96,80},{112,128},... | collective-permute-start | bytes 4616 | tf_op jit(solution)/shard_map/ghosts/ppermute | solution.py:245
  133.5 0.6 copy-start.4

commit v8 on v7

--- a/solution.py
+++ b/solution.py
@@ -16,9 +16,13 @@
 LAST = (((1,), (1,)), ((), ()))
 
 
-def spread_kernel(rows_ref, out_hbm, sems):
+def spread_kernel(rows_ref, out_hbm, few, sems):
+    count = few.shape[0]
+    for i in range(count):
+        few[i] = rows_ref[...]
     copies = [
-        pltpu.make_async_copy(rows_ref, out_hbm.at[i], sems.at[i]) for i in range(out_hbm.shape[0])
+        pltpu.make_async_copy(few, out_hbm.at[pl.ds(i * count, count)], sems.at[i])
+        for i in range(out_hbm.shape[0] // count)
     ]
     for copy in copies:
         copy.start()
@@ -145,9 +149,12 @@
         spread = pl.pallas_call(
             spread_kernel,
             out_shape=jax.ShapeDtypeStruct((n_plane, owned, width), BF16),
-            in_specs=[anywhere],
+            in_specs=[vmem],
             out_specs=anywhere,
-            scratch_shapes=[pltpu.SemaphoreType.DMA((n_plane,))],
+            scratch_shapes=[
+                pltpu.VMEM((4, owned, width), BF16),
+                pltpu.SemaphoreType.DMA((n_plane // 4,)),
+            ],
             compiler_params=pltpu.CompilerParams(vmem_limit_bytes=4 << 20),
         )(descriptors)
         rows = lax.all_to_all(spread, PLANE, 0, 0)

time: 135 us -> 134 us (level)
  no operation moved by 1% of the time
where the time goes in v8:
time: 134 us
  blocking collectives  74.5 us (56%)
  starting transfers between devices  29.5 us (22%)
  waiting for transfers between devices  15.5 us (12%)
  matrix products  6.09 us (5%)
  Pallas kernels  3.83 us (3%)
  other arithmetic  2.14 us (2%)
  local copies, waits for them, and re-layouts  1.39 us (1%)
    all_gather x1, blocking collectives, body(): lifted = lax.all_gather(block, 'z', axis=0, tiled=True)  61.5 us
    all_to_all x1, blocking collectives, body(): received = jnp.sum(lax.all_to_all(both, PLANE, 0, 0), axis=0)  13 us
    all_to_all x1, waiting for transfers between devices, body(): parts = lax.all_to_all(outgoing, CHIPS, 0, 0)  9.51 us
    ppermute x1, starting transfers between devices, body(): theirs = lax.ppermute(other, 'c', swap)  8.57 us
    all_to_all x1, starting transfers between devices, body(): rows = lax.all_to_all(spread, PLANE, 0, 0)  8.36 us
    all_to_all x1, starting transfers between devices, body(): parts = lax.all_to_all(outgoing, CHIPS, 0, 0)  6.64 us
    ppermute x1, waiting for transfers between devices, body(): keep = keep + lax.ppermute(across, DOM, pairs)  4.5 us
    ppermute x1, starting transfers between devices, body(): got = lax.ppermute(sent.astype(F16), 'yl', swap)  4.03 us
  transfers between devices with their start and end apart: 5, of which 3 were waited for; matrix products, arithmetic and copies ran while one was open for 1% of the time, Pallas kernels for 1%

profile of v8, /device:TPU:1, one launch (start us, length us, event | category | flops | bytes accessed | tf_op | source)
XLA Modules:
  0.0 133.9 jit_solution(9811571798029515706)
XLA Ops:
  0.6 0.0 copy-start.3
  0.6 1.0 fusion.8
  1.7 4.0 %collective-permute-start = (f16[64,1024]{1,0:T(8,128)(2,1)S(1)}, f16[64,1024]{1,0:T(8,128)(2,1)S(1)}, u32[]{:S(2)}, u32[]{:S(2)}) collective-permute-start(f16[64,1024]{1,0:T(8,128)(2,1)S(1)} %get-tuple-element.29), channel_id=1, source_target_pairs={{0,16},{16,0},{1,17},{17,1},{2,18},{18,2},{3,19},{19,3},{4,20},{20... | collective-permute-start | bytes 393224 | tf_op jit(solution)/shard_map/points_swap/ppermute | solution.py:143
  5.7 0.0 copy-start.1
  5.7 0.7 copy-done.1
  6.5 1.1 descriptors_gather.2
  7.6 8.4 %all-to-all-start = ((bf16[32,128,128]{2,1,0:T(8,128)(2,1)}), bf16[32,128,128]{2,1,0:T(8,128)(2,1)S(1)}, u32[]{:S(2)}, u32[]{:S(2)}) async-start(bf16[32,128,128]{2,1,0:T(8,128)(2,1)} %descriptors_gather.2), calls=%async_computation | async-start | bytes 2097152 | tf_op jit(solution)/shard_map/descriptors_gather/all_to_all | solution.py:160
  15.9 0.0 copy-done.3
  15.9 0.0 collective-permute-done
  16.0 0.1 pad_maximum_fusion
  16.0 61.5 %all-gather.1 = f16[2048,1024]{1,0:T(8,128)(2,1)} all-gather(f16[128,1024]{1,0:T(8,128)(2,1)S(1)} %pad_maximum_fusion), channel_id=1, replica_groups=mesh['z'=16,'yl'=2,'x'=4,'yh'=2,'c'=2] {'z'}, dimensions={0}, use_global_device_ids=true | all-gather | bytes 4456448 | tf_op jit(solution)/shard_map/points_gather/all_gather | solution.py:146
  77.5 0.0 all-to-all-done.rows_ref
  77.5 0.7 descriptors_gather.3
  78.2 0.0 copy-start.2
  78.2 3.6 %fusion.2.kernel_ref = f32[256,1024]{1,0:T(8,128)S(1)} fusion(bf16[256,2048]{1,0:T(8,128)(2,1)S(1)} %get-tuple-element.15.unit_ref, f16[2048,1024]{1,0:T(8,128)(2,1)} %all-gather.1), kind=kOutput, calls=%fused_computation.2 | convolution fusion | flops 1075838976 | bytes 6291456 | tf_op jit(solution)/shard_map/kernel/dot_general | solution.py:176
  81.8 0.4 kernel.1
  82.3 0.0 copy-done.2
  82.3 1.3 fusion.gradient_ref
  83.6 0.0 copy-start.5
  83.6 0.7 gradient.1
  84.3 0.0 copy-start.6
  84.3 0.0 copy-start.7
  84.3 8.6 %collective-permute-start.1 = (bf16[16,128,128]{2,1,0:T(8,128)(2,1)S(1)}, bf16[16,128,128]{2,1,0:T(8,128)(2,1)S(1)}, u32[]{:S(2)}, u32[]{:S(2)}) collective-permute-start(bf16[16,128,128]{2,1,0:T(8,128)(2,1)S(1)} %get-tuple-element.22), channel_id=1, source_target_pairs={{0,1},{1,0},{2,3},{3,2},{4,5},{5,4},{6,7},{7,6},{8,9},{9,8},{10,11... | collective-permute-start | bytes 1572872 | tf_op jit(solution)/shard_map/core_pair/ppermute | solution.py:205
  92.9 0.0 copy-done.5
  92.9 1.5 %collective-permute-done.1 = bf16[16,128,128]{2,1,0:T(8,128)(2,1)S(1)} collective-permute-done((bf16[16,128,128]{2,1,0:T(8,128)(2,1)S(1)}, bf16[16,128,128]{2,1,0:T(8,128)(2,1)S(1)}, u32[]{:S(2)}, u32[]{:S(2)}) %collective-permute-start.1) | collective-permute-done | bytes 524320 | tf_op jit(solution)/shard_map/core_pair/ppermute | solution.py:205
  94.4 0.9 add_convert_fusion
  95.3 6.6 %all-to-all-start.1 = ((bf16[16,128,128]{2,1,0:T(8,128)(2,1)}), bf16[16,128,128]{2,1,0:T(8,128)(2,1)S(1)}, u32[]{:S(2)}, u32[]{:S(2)}) async-start(bf16[16,128,128]{2,1,0:T(8,128)(2,1)} %add_convert_fusion), calls=%async_computation.1 | async-start | bytes 1048576 | tf_op jit(solution)/shard_map/gradient_exchange/all_to_all | solution.py:208
  102.0 0.0 copy-start
  102.0 0.0 copy-done.6
  102.0 0.0 copy-done.7
  102.1 1.2 fusion.5.table_ref
  103.2 9.5 %all-to-all-done.1.parts_ref = bf16[16,128,128]{2,1,0:T(8,128)(2,1)S(1)} async-done(((bf16[16,128,128]{2,1,0:T(8,128)(2,1)}), bf16[16,128,128]{2,1,0:T(8,128)(2,1)S(1)}, u32[]{:S(2)}, u32[]{:S(2)}) %all-to-all-start.1) | async-done | bytes 524320 | tf_op jit(solution)/shard_map/gradient_exchange/all_to_all | solution.py:208
  112.8 0.0 copy-done
  112.8 1.0 tail.1
  113.8 1.9 %collective-permute-start.2 = (f32[3,128]{1,0:T(4,128)S(1)}, f32[3,128]{1,0:T(4,128)S(1)}, u32[]{:S(2)}, u32[]{:S(2)}) collective-permute-start(f32[3,128]{1,0:T(4,128)S(1)} %slice_select_fusion.1), channel_id=1, source_target_pairs={{0,496},{16,32},{32,16},{48,64},{64,48},{80,96},{96,80},{112,128},... | collective-permute-start | bytes 4616 | tf_op jit(solution)/shard_map/ghosts/ppermute | solution.py:252
  115.7 4.5 %collective-permute-done.2 = f32[3,128]{1,0:T(4,128)S(1)} collective-permute-done((f32[3,128]{1,0:T(4,128)S(1)}, f32[3,128]{1,0:T(4,128)S(1)}, u32[]{:S(2)}, u32[]{:S(2)}) %collective-permute-start.2) | collective-permute-done | bytes 1568 | tf_op jit(solution)/shard_map/ghosts/ppermute | solution.py:252
  120.3 13.0 %all_to_all.15 = f32[32,4,128]{2,1,0:T(4,128)S(1)} all-to-all(f32[32,4,128]{2,1,0:T(4,128)S(1)} %bitcast.25), channel_id=1, replica_groups=mesh['z'=16,'yl'=2,'x'=4,'yh'=2,'c'=2] {'x','yl','yh','c'}, dimensions={0} | all-to-all | bytes 131072 | tf_op jit(solution)/shard_map/ghosts/all_to_all | solution.py:257
  133.3 0.0 copy-start.4
  133.3 0.5 slice_bitcast_fusion
  133.8 0.1 copy-done.4
  (12 shorter events, 0.1 us)
Async XLA Ops:
  0.6 15.3 %copy-start.3 = (f32[2048]{0:T(1024)S(1)}, f32[2048]{0:T(1024)}, u32[]{:S(2)}) copy-start(f32[2048]{0:T(1024)} %param.9) | copy-start | bytes 24580
  1.7 14.3 %collective-permute-start = (f16[64,1024]{1,0:T(8,128)(2,1)S(1)}, f16[64,1024]{1,0:T(8,128)(2,1)S(1)}, u32[]{:S(2)}, u32[]{:S(2)}) collective-permute-start(f16[64,1024]{1,0:T(8,128)(2,1)S(1)} %get-tuple-element.29), channel_id=1, source_target_pairs={{0,16},{16,0},{1,17},{17,1},{2,18},{18,2},{3,19},{19,3},{4,20},{20... | collective-permute-start | bytes 393224 | tf_op jit(solution)/shard_map/points_swap/ppermute | solution.py:143
  5.7 0.8 copy-start.1
  7.6 70.0 %all-to-all-start = ((bf16[32,128,128]{2,1,0:T(8,128)(2,1)}), bf16[32,128,128]{2,1,0:T(8,128)(2,1)S(1)}, u32[]{:S(2)}, u32[]{:S(2)}) async-start(bf16[32,128,128]{2,1,0:T(8,128)(2,1)} %descriptors_gather.2), calls=%async_computation | async-start | bytes 2097152 | tf_op jit(solution)/shard_map/descriptors_gather/all_to_all | solution.py:160
  78.2 4.0 %copy-start.2 = (f16[2048,1024]{1,0:T(8,128)(2,1)S(1)}, f16[2048,1024]{1,0:T(8,128)(2,1)}, u32[]{:S(2)}) copy-start(f16[2048,1024]{1,0:T(8,128)(2,1)} %all-gather.1) | copy-start | bytes 12582916
  83.6 9.3 %copy-start.5 = (s32[256]{0:T(256)S(1)}, s32[256]{0:T(256)}, u32[]{:S(2)}) copy-start(s32[256]{0:T(256)} %param.13) | copy-start | bytes 3076
  84.3 17.8 %copy-start.6 = (s32[128]{0:T(128)S(1)}, s32[128]{0:T(128)}, u32[]{:S(2)}) copy-start(s32[128]{0:T(128)} %param.12) | copy-start | bytes 1540
  84.3 17.8 %copy-start.7 = (s32[128,12]{0,1:T(8,128)S(1)}, s32[128,12]{0,1:T(8,128)}, u32[]{:S(2)}) copy-start(s32[128,12]{0,1:T(8,128)} %param.11) | copy-start | bytes 18436
  84.3 10.1 %collective-permute-start.1 = (bf16[16,128,128]{2,1,0:T(8,128)(2,1)S(1)}, bf16[16,128,128]{2,1,0:T(8,128)(2,1)S(1)}, u32[]{:S(2)}, u32[]{:S(2)}) collective-permute-start(bf16[16,128,128]{2,1,0:T(8,128)(2,1)S(1)} %get-tuple-element.22), channel_id=1, source_target_pairs={{0,1},{1,0},{2,3},{3,2},{4,5},{5,4},{6,7},{7,6},{8,9},{9,8},{10,11... | collective-permute-start | bytes 1572872 | tf_op jit(solution)/shard_map/core_pair/ppermute | solution.py:205
  95.3 17.4 %all-to-all-start.1 = ((bf16[16,128,128]{2,1,0:T(8,128)(2,1)}), bf16[16,128,128]{2,1,0:T(8,128)(2,1)S(1)}, u32[]{:S(2)}, u32[]{:S(2)}) async-start(bf16[16,128,128]{2,1,0:T(8,128)(2,1)} %add_convert_fusion), calls=%async_computation.1 | async-start | bytes 1048576 | tf_op jit(solution)/shard_map/gradient_exchange/all_to_all | solution.py:208
  102.0 10.8 %copy-start = (bf16[128,3,12,128]{3,0,2,1:T(8,128)(2,1)S(1)}, bf16[128,3,12,128]{3,0,2,1:T(8,128)(2,1)}, u32[]{:S(2)}) copy-start(bf16[128,3,12,128]{3,0,2,1:T(8,128)(2,1)} %param.10) | copy-start | bytes 3538948
  113.8 6.4 %collective-permute-start.2 = (f32[3,128]{1,0:T(4,128)S(1)}, f32[3,128]{1,0:T(4,128)S(1)}, u32[]{:S(2)}, u32[]{:S(2)}) collective-permute-start(f32[3,128]{1,0:T(4,128)S(1)} %slice_select_fusion.1), channel_id=1, source_target_pairs={{0,496},{16,32},{32,16},{48,64},{64,48},{80,96},{96,80},{112,128},... | collective-permute-start | bytes 4616 | tf_op jit(solution)/shard_map/ghosts/ppermute | solution.py:252
  133.3 0.6 copy-start.4

commit v9 on v8

--- a/solution.py
+++ b/solution.py
@@ -173,7 +173,10 @@
         )(side, rows)
 
     with jax.named_scope("kernel"):
-        kernel = jnp.dot(unit_rows, lifted.astype(BF16), preferred_element_type=F32)
+        middle = columns // 2
+        kernel = jnp.dot(
+            unit_rows[:, :middle], lifted[:middle].astype(BF16), preferred_element_type=F32
+        ) + jnp.dot(unit_rows[:, middle:], lifted[middle:].astype(BF16), preferred_element_type=F32)
         slopes, inner, energy_part = pl.pallas_call(
             slope_kernel,
             out_shape=(

time: 134 us -> 134 us (level)
    dot_general x1 -> x2, matrix products: 3.6 us -> 3.18 us  [the longest x1 2.45 us: body(): jnp.dot(unit_rows[:, middle:], lifted[middle:].astype(BF16), preferred_el...]
where the time goes in v9:
time: 134 us
  blocking collectives  74.5 us (56%)
  starting transfers between devices  29.5 us (22%)
  waiting for transfers between devices  15.5 us (12%)
  matrix products  5.67 us (4%)
  Pallas kernels  3.83 us (3%)
  other arithmetic  2.14 us (2%)
  local copies, waits for them, and re-layouts  1.74 us (1%)
    all_gather x1, blocking collectives, body(): lifted = lax.all_gather(block, 'z', axis=0, tiled=True)  61.5 us
    all_to_all x1, blocking collectives, body(): received = jnp.sum(lax.all_to_all(both, PLANE, 0, 0), axis=0)  13 us
    all_to_all x1, waiting for transfers between devices, body(): parts = lax.all_to_all(outgoing, CHIPS, 0, 0)  9.51 us
    ppermute x1, starting transfers between devices, body(): theirs = lax.ppermute(other, 'c', swap)  8.58 us
    all_to_all x1, starting transfers between devices, body(): rows = lax.all_to_all(spread, PLANE, 0, 0)  8.36 us
    all_to_all x1, starting transfers between devices, body(): parts = lax.all_to_all(outgoing, CHIPS, 0, 0)  6.62 us
    ppermute x1, waiting for transfers between devices, body(): keep = keep + lax.ppermute(across, DOM, pairs)  4.5 us
    ppermute x1, starting transfers between devices, body(): got = lax.ppermute(sent.astype(F16), 'yl', swap)  4.03 us
  transfers between devices with their start and end apart: 5, of which 3 were waited for; matrix products, arithmetic and copies ran while one was open for 1% of the time, Pallas kernels for 1%

profile of v9, /device:TPU:1, one launch (start us, length us, event | category | flops | bytes accessed | tf_op | source)
XLA Modules:
  0.0 133.8 jit_solution(13288012132782693706)
XLA Ops:
  0.6 0.0 copy-start.3
  0.6 1.0 fusion.11
  1.7 4.0 %collective-permute-start = (f16[64,1024]{1,0:T(8,128)(2,1)S(1)}, f16[64,1024]{1,0:T(8,128)(2,1)S(1)}, u32[]{:S(2)}, u32[]{:S(2)}) collective-permute-start(f16[64,1024]{1,0:T(8,128)(2,1)S(1)} %get-tuple-element.29), channel_id=1, source_target_pairs={{0,16},{16,0},{1,17},{17,1},{2,18},{18,2},{3,19},{19,3},{4,20},{20... | collective-permute-start | bytes 393224 | tf_op jit(solution)/shard_map/points_swap/ppermute | solution.py:143
  5.7 0.0 copy-start.1
  5.7 0.7 copy-done.1
  6.5 1.1 descriptors_gather.2
  7.6 8.4 %all-to-all-start = ((bf16[32,128,128]{2,1,0:T(8,128)(2,1)}), bf16[32,128,128]{2,1,0:T(8,128)(2,1)S(1)}, u32[]{:S(2)}, u32[]{:S(2)}) async-start(bf16[32,128,128]{2,1,0:T(8,128)(2,1)} %descriptors_gather.2), calls=%async_computation | async-start | bytes 2097152 | tf_op jit(solution)/shard_map/descriptors_gather/all_to_all | solution.py:160
  15.9 0.0 copy-done.3
  15.9 0.0 collective-permute-done
  16.0 0.1 pad_maximum_fusion
  16.0 61.5 %all-gather.1 = f16[2048,1024]{1,0:T(8,128)(2,1)} all-gather(f16[128,1024]{1,0:T(8,128)(2,1)S(1)} %pad_maximum_fusion), channel_id=1, replica_groups=mesh['z'=16,'yl'=2,'x'=4,'yh'=2,'c'=2] {'z'}, dimensions={0}, use_global_device_ids=true | all-gather | bytes 4456448 | tf_op jit(solution)/shard_map/points_gather/all_gather | solution.py:146
  77.5 0.0 all-to-all-done.rows_ref
  77.5 0.7 descriptors_gather.3
  78.2 0.0 copy-start.2
  78.2 2.5 %fusion.4 = f32[256,1024]{1,0:T(8,128)S(1)} fusion(f16[2048,1024]{1,0:T(8,128)(2,1)} %all-gather.1, bf16[256,2048]{1,0:T(8,128)(2,1)S(1)} %get-tuple-element.15.unit_ref), kind=kOutput, calls=%fused_computation.8 | convolution fusion | flops 537919488 | bytes 3670016 | tf_op jit(solution)/shard_map/kernel/dot_general | solution.py:179
  80.7 0.3 copy-done.2
  81.0 0.7 fusion.6.kernel_ref
  81.8 0.4 kernel.1
  82.2 1.3 fusion.gradient_ref
  83.5 0.0 copy-start.5
  83.5 0.7 gradient.1
  84.2 0.0 copy-start.6
  84.2 0.0 copy-start.7
  84.2 8.6 %collective-permute-start.1 = (bf16[16,128,128]{2,1,0:T(8,128)(2,1)S(1)}, bf16[16,128,128]{2,1,0:T(8,128)(2,1)S(1)}, u32[]{:S(2)}, u32[]{:S(2)}) collective-permute-start(bf16[16,128,128]{2,1,0:T(8,128)(2,1)S(1)} %get-tuple-element.22), channel_id=1, source_target_pairs={{0,1},{1,0},{2,3},{3,2},{4,5},{5,4},{6,7},{7,6},{8,9},{9,8},{10,11... | collective-permute-start | bytes 1572872 | tf_op jit(solution)/shard_map/core_pair/ppermute | solution.py:208
  92.8 0.0 copy-done.5
  92.8 1.5 %collective-permute-done.1 = bf16[16,128,128]{2,1,0:T(8,128)(2,1)S(1)} collective-permute-done((bf16[16,128,128]{2,1,0:T(8,128)(2,1)S(1)}, bf16[16,128,128]{2,1,0:T(8,128)(2,1)S(1)}, u32[]{:S(2)}, u32[]{:S(2)}) %collective-permute-start.1) | collective-permute-done | bytes 524320 | tf_op jit(solution)/shard_map/core_pair/ppermute | solution.py:208
  94.3 0.9 add_convert_fusion
  95.3 6.6 %all-to-all-start.1 = ((bf16[16,128,128]{2,1,0:T(8,128)(2,1)}), bf16[16,128,128]{2,1,0:T(8,128)(2,1)S(1)}, u32[]{:S(2)}, u32[]{:S(2)}) async-start(bf16[16,128,128]{2,1,0:T(8,128)(2,1)} %add_convert_fusion), calls=%async_computation.1 | async-start | bytes 1048576 | tf_op jit(solution)/shard_map/gradient_exchange/all_to_all | solution.py:211
  101.9 0.0 copy-start
  101.9 0.0 copy-done.6
  101.9 0.0 copy-done.7
  102.0 1.2 fusion.3.table_ref
  103.1 9.5 %all-to-all-done.1.parts_ref = bf16[16,128,128]{2,1,0:T(8,128)(2,1)S(1)} async-done(((bf16[16,128,128]{2,1,0:T(8,128)(2,1)}), bf16[16,128,128]{2,1,0:T(8,128)(2,1)S(1)}, u32[]{:S(2)}, u32[]{:S(2)}) %all-to-all-start.1) | async-done | bytes 524320 | tf_op jit(solution)/shard_map/gradient_exchange/all_to_all | solution.py:211
  112.7 0.0 copy-done
  112.7 1.0 tail.1
  113.7 1.9 %collective-permute-start.2 = (f32[3,128]{1,0:T(4,128)S(1)}, f32[3,128]{1,0:T(4,128)S(1)}, u32[]{:S(2)}, u32[]{:S(2)}) collective-permute-start(f32[3,128]{1,0:T(4,128)S(1)} %slice_select_fusion.1), channel_id=1, source_target_pairs={{0,496},{16,32},{32,16},{48,64},{64,48},{80,96},{96,80},{112,128},... | collective-permute-start | bytes 4616 | tf_op jit(solution)/shard_map/ghosts/ppermute | solution.py:255
  115.6 4.5 %collective-permute-done.2 = f32[3,128]{1,0:T(4,128)S(1)} collective-permute-done((f32[3,128]{1,0:T(4,128)S(1)}, f32[3,128]{1,0:T(4,128)S(1)}, u32[]{:S(2)}, u32[]{:S(2)}) %collective-permute-start.2) | collective-permute-done | bytes 1568 | tf_op jit(solution)/shard_map/ghosts/ppermute | solution.py:255
  120.2 13.0 %all_to_all.15 = f32[32,4,128]{2,1,0:T(4,128)S(1)} all-to-all(f32[32,4,128]{2,1,0:T(4,128)S(1)} %bitcast.24), channel_id=1, replica_groups=mesh['z'=16,'yl'=2,'x'=4,'yh'=2,'c'=2] {'x','yl','yh','c'}, dimensions={0} | all-to-all | bytes 131072 | tf_op jit(solution)/shard_map/ghosts/all_to_all | solution.py:260
  133.2 0.0 copy-start.4
  133.2 0.5 slice_bitcast_fusion
  133.8 0.1 copy-done.4
  (12 shorter events, 0.1 us)
Async XLA Ops:
  0.6 15.3 %copy-start.3 = (f32[2048]{0:T(1024)S(1)}, f32[2048]{0:T(1024)}, u32[]{:S(2)}) copy-start(f32[2048]{0:T(1024)} %param.9) | copy-start | bytes 24580
  1.7 14.3 %collective-permute-start = (f16[64,1024]{1,0:T(8,128)(2,1)S(1)}, f16[64,1024]{1,0:T(8,128)(2,1)S(1)}, u32[]{:S(2)}, u32[]{:S(2)}) collective-permute-start(f16[64,1024]{1,0:T(8,128)(2,1)S(1)} %get-tuple-element.29), channel_id=1, source_target_pairs={{0,16},{16,0},{1,17},{17,1},{2,18},{18,2},{3,19},{19,3},{4,20},{20... | collective-permute-start | bytes 393224 | tf_op jit(solution)/shard_map/points_swap/ppermute | solution.py:143
  5.7 0.8 copy-start.1
  7.6 70.0 %all-to-all-start = ((bf16[32,128,128]{2,1,0:T(8,128)(2,1)}), bf16[32,128,128]{2,1,0:T(8,128)(2,1)S(1)}, u32[]{:S(2)}, u32[]{:S(2)}) async-start(bf16[32,128,128]{2,1,0:T(8,128)(2,1)} %descriptors_gather.2), calls=%async_computation | async-start | bytes 2097152 | tf_op jit(solution)/shard_map/descriptors_gather/all_to_all | solution.py:160
  78.2 2.8 %copy-start.2 = (f16[2048,1024]{1,0:T(8,128)(2,1)S(1)}, f16[2048,1024]{1,0:T(8,128)(2,1)}, u32[]{:S(2)}) copy-start(f16[2048,1024]{1,0:T(8,128)(2,1)} %all-gather.1) | copy-start | bytes 12582916
  83.5 9.3 %copy-start.5 = (s32[256]{0:T(256)S(1)}, s32[256]{0:T(256)}, u32[]{:S(2)}) copy-start(s32[256]{0:T(256)} %param.13) | copy-start | bytes 3076
  84.2 17.7 %copy-start.6 = (s32[128]{0:T(128)S(1)}, s32[128]{0:T(128)}, u32[]{:S(2)}) copy-start(s32[128]{0:T(128)} %param.12) | copy-start | bytes 1540
  84.2 17.7 %copy-start.7 = (s32[128,12]{0,1:T(8,128)S(1)}, s32[128,12]{0,1:T(8,128)}, u32[]{:S(2)}) copy-start(s32[128,12]{0,1:T(8,128)} %param.11) | copy-start | bytes 18436
  84.2 10.1 %collective-permute-start.1 = (bf16[16,128,128]{2,1,0:T(8,128)(2,1)S(1)}, bf16[16,128,128]{2,1,0:T(8,128)(2,1)S(1)}, u32[]{:S(2)}, u32[]{:S(2)}) collective-permute-start(bf16[16,128,128]{2,1,0:T(8,128)(2,1)S(1)} %get-tuple-element.22), channel_id=1, source_target_pairs={{0,1},{1,0},{2,3},{3,2},{4,5},{5,4},{6,7},{7,6},{8,9},{9,8},{10,11... | collective-permute-start | bytes 1572872 | tf_op jit(solution)/shard_map/core_pair/ppermute | solution.py:208
  95.3 17.4 %all-to-all-start.1 = ((bf16[16,128,128]{2,1,0:T(8,128)(2,1)}), bf16[16,128,128]{2,1,0:T(8,128)(2,1)S(1)}, u32[]{:S(2)}, u32[]{:S(2)}) async-start(bf16[16,128,128]{2,1,0:T(8,128)(2,1)} %add_convert_fusion), calls=%async_computation.1 | async-start | bytes 1048576 | tf_op jit(solution)/shard_map/gradient_exchange/all_to_all | solution.py:211
  101.9 10.8 %copy-start = (bf16[128,3,12,128]{3,0,2,1:T(8,128)(2,1)S(1)}, bf16[128,3,12,128]{3,0,2,1:T(8,128)(2,1)}, u32[]{:S(2)}) copy-start(bf16[128,3,12,128]{3,0,2,1:T(8,128)(2,1)} %param.10) | copy-start | bytes 3538948
  113.7 6.4 %collective-permute-start.2 = (f32[3,128]{1,0:T(4,128)S(1)}, f32[3,128]{1,0:T(4,128)S(1)}, u32[]{:S(2)}, u32[]{:S(2)}) collective-permute-start(f32[3,128]{1,0:T(4,128)S(1)} %slice_select_fusion.1), channel_id=1, source_target_pairs={{0,496},{16,32},{32,16},{48,64},{64,48},{80,96},{96,80},{112,128},... | collective-permute-start | bytes 4616 | tf_op jit(solution)/shard_map/ghosts/ppermute | solution.py:255
  133.2 0.6 copy-start.4
